TPU v7x, 512 devices: a whole 4x8x8 slice. The times are simulated.
512 devices in a mesh: role: 4 (over x), seq: 32 (over z_lo, y), mp: 4 (over z_hi, core).
Axes of the slice: x: 4, y: 8, z: 8 (z_hi: 2, z_lo: 4; z = z_hi * 4 + z_lo), core: 2. Of those that a mesh axis runs over, the one named last changes fastest.
Arguments:
- gen_hidden: bfloat16 [4096, 5120], P('seq', 'mp'), may hold values from -0.59765625 to 0.59765625
- out_weight: bfloat16 [5120, 64], P('mp'), may hold values from -0.078125 to 0.078125
- noise: bfloat16 [4096, 64], P('seq'), may hold values from -12 to 12
- step_index: int32 [1], replicated, may hold values from 200 to 799
- token_order: int32 [4096], P('seq'), may hold values from 0 to 4095, each once
- time_weight: float32 [4, 256, 2, 5120], P('role', None, None, ('seq', 'mp')), may hold values from -0.375 to 0.375
- embed_weight: bfloat16 [4, 64, 5120], P('role'), may hold values from -0.75 to 0.75
- qkv_weight: bfloat16 [4, 32, 5120, 384], P('role', 'seq'), may hold values from -0.078125 to 0.078125
- readout_weight: bfloat16 [4, 32, 128, 64], P('role', 'seq'), may hold values from -0.09375 to 0.09375
Outputs:
- hidden_grad: bfloat16 [4096, 5120], P('seq', 'mp')
- weight_grad: float32 [5120, 64], P('mp')
Inputs may be any that keep to these rules, and one draw needn't show every extreme that they name: `token_order`: each row's position in the clip, every position once.
All inputs are finite; a program needn't handle non-finite values. Where the computation divides by a largest or mean magnitude, that divisor is 1e-20 or more.
Results may differ from a plain program's by a relative error of at most 0.035.
Values may be sent and summed in bfloat16 or wider, within the bound.
No kernel may reach another device: no remote copies, remote signals or barrier semaphores. Data moves between devices by JAX's collectives and lax.ppermute only.
A program may use at most 64 MiB of HBM per device.

v0:
```python
import math

import jax
import jax.numpy as jnp
from jax import lax
from jax.sharding import PartitionSpec as P

D = 5120
FREQ = 256
T_STEPS = 1000


EPS_NORM = 1e-06
EPS_MEAN = 1e-05
GUIDANCE = 5.0
ROPE_BASE = 10000.0
SHARPNESS = 4.0


def normalize_rope(vectors, cosines, sines):
    rescaled = vectors * lax.rsqrt(jnp.mean(vectors * vectors, axis=1, keepdims=True) + EPS_NORM)
    width = vectors.shape[1] // 2
    front = rescaled[:, :width]
    back = rescaled[:, width:]
    return jnp.concatenate(
        [front * cosines - back * sines, front * sines + back * cosines], axis=1
    ).astype(jnp.bfloat16)


def attend(queries, keys, values, running):
    count = keys.shape[0]
    head_dim = queries.shape[1]
    width = 512
    key_blocks = keys.reshape(count // width, width, head_dim)
    value_blocks = values.reshape(count // width, width, head_dim)

    def advance(progress, blocks):
        numer, denom = progress
        scores = lax.dot_general(
            queries, blocks[0], (((1,), (1,)), ((), ())), preferred_element_type=jnp.float32
        ) * (SHARPNESS / math.sqrt(head_dim))
        exponent = jnp.exp(scores)
        numer = numer + jnp.dot(
            exponent.astype(jnp.bfloat16), blocks[1], preferred_element_type=jnp.float32
        )
        denom = denom + jnp.sum(exponent, axis=1)
        return ((numer, denom), None)

    result, unused = lax.scan(advance, running, (key_blocks, value_blocks))
    return result


def body(
    gen_hidden,
    out_weight,
    noise,
    step_index,
    token_order,
    time_weight,
    embed_weight,
    qkv_weight,
    readout_weight,
):
    seq_count = lax.axis_size("seq")
    mp_count = lax.axis_size("mp")
    mp_index = lax.axis_index("mp")
    role_index = lax.axis_index("role")
    local_rows = gen_hidden.shape[0]
    quarter = local_rows // mp_count
    head_dim = qkv_weight.shape[3] // 3
    lat_dim = out_weight.shape[1]
    hidden_wide = gen_hidden.astype(jnp.float32)
    projected, squares = lax.psum(
        (
            jnp.dot(gen_hidden, out_weight, preferred_element_type=jnp.float32),
            jnp.sum(hidden_wide * hidden_wide, axis=1),
        ),
        "mp",
    )
    root_mean = jnp.sqrt(squares / D + EPS_NORM)
    latent = projected / root_mean[:, None]
    timestep = step_index[0].astype(jnp.float32)
    noise_level = timestep / T_STEPS
    noisy = ((1.0 - noise_level) * latent + noise_level * noise.astype(jnp.float32)).astype(
        jnp.bfloat16
    )
    clip_rows, clip_order = (
        lax.all_gather(noisy, "seq", axis=0, tiled=True),
        lax.all_gather(token_order, "seq", axis=0, tiled=True),
    )
    query_count = seq_count * quarter
    mine_rows = lax.dynamic_slice_in_dim(
        clip_rows.reshape(seq_count, local_rows, lat_dim), mp_index * quarter, quarter, 1
    ).reshape(query_count, lat_dim)
    mine_order = lax.dynamic_slice_in_dim(
        clip_order.reshape(seq_count, local_rows), mp_index * quarter, quarter, 1
    ).reshape(query_count)
    half_freq = FREQ // 2
    frequencies = jnp.exp(
        -math.log(ROPE_BASE) * jnp.arange(half_freq, dtype=jnp.float32) / half_freq
    )
    phases = timestep * frequencies
    activated = jax.nn.silu(jnp.concatenate([jnp.cos(phases), jnp.sin(phases)]))
    modulation_part = jnp.einsum(
        "f,fcd->cd", activated, time_weight[0], precision=lax.Precision.HIGHEST
    )
    modulation = lax.all_gather(modulation_part, ("seq", "mp"), axis=1, tiled=True)
    inverse = jnp.exp(
        -math.log(ROPE_BASE) * jnp.arange(head_dim // 2, dtype=jnp.float32) * 2.0 / head_dim
    )
    angles = mine_order.astype(jnp.float32)[:, None] * inverse[None, :]
    block_rows = min(query_count, 512)
    block_count = query_count // block_rows

    def project(inputs):
        row_block, angle_block = inputs
        embedded = jnp.dot(row_block, embed_weight[0], preferred_element_type=jnp.float32)
        normed = embedded * lax.rsqrt(
            jnp.mean(embedded * embedded, axis=1, keepdims=True) + EPS_NORM
        )
        modulated = (normed * (1.0 + modulation[1]) + modulation[0]).astype(jnp.bfloat16)
        combined = jnp.dot(modulated, qkv_weight[0, 0], preferred_element_type=jnp.float32)
        cosines = jnp.cos(angle_block)
        sines = jnp.sin(angle_block)
        return (
            normalize_rope(combined[:, :head_dim], cosines, sines),
            normalize_rope(combined[:, head_dim : 2 * head_dim], cosines, sines),
            combined[:, 2 * head_dim :].astype(jnp.bfloat16),
        )

    query_blocks, key_blocks, value_blocks = lax.map(
        project,
        (
            mine_rows.reshape(block_count, block_rows, lat_dim),
            angles.reshape(block_count, block_rows, head_dim // 2),
        ),
    )
    queries = query_blocks.reshape(query_count, head_dim)
    keys = key_blocks.reshape(query_count, head_dim)
    values = value_blocks.reshape(query_count, head_dim)
    empty = (
        jnp.zeros((query_count, head_dim), jnp.float32),
        jnp.zeros((query_count,), jnp.float32),
    )
    numerator, denominator = attend(
        queries,
        lax.all_gather(keys, "mp", axis=0, tiled=True),
        lax.all_gather(values, "mp", axis=0, tiled=True),
        empty,
    )
    attended = (numerator / denominator[:, None]).astype(jnp.bfloat16)
    score = lax.psum_scatter(
        jnp.dot(attended, readout_weight[0, 0], preferred_element_type=jnp.float32).astype(
            jnp.bfloat16
        ),
        "seq",
        scatter_dimension=0,
        tiled=True,
    ).astype(jnp.float32)
    diff_weight = jnp.where(
        role_index == 3,
        1.0,
        jnp.where(role_index == 1, -GUIDANCE, jnp.where(role_index == 2, GUIDANCE - 1.0, 0.0)),
    )
    real_weight = jnp.where(
        role_index == 1, GUIDANCE, jnp.where(role_index == 2, 1.0 - GUIDANCE, 0.0)
    )
    difference, realistic = lax.psum((diff_weight * score, real_weight * score), "role")
    cell_count = local_rows * seq_count * lat_dim
    own_latent = lax.dynamic_slice_in_dim(latent, mp_index * quarter, quarter, 0)
    own_noisy = lax.dynamic_slice_in_dim(noisy, mp_index * quarter, quarter, 0).astype(jnp.float32)
    magnitude = jnp.sum(jnp.abs(own_latent - (own_noisy - noise_level * realistic)))
    totals = lax.psum(magnitude, ("seq", "mp"))
    own_grad = -noise_level * difference / (totals / cell_count + EPS_MEAN)
    latent_grad = lax.all_gather(own_grad, "mp", axis=0, tiled=True)
    backward = lax.dot_general(
        latent_grad,
        out_weight.astype(jnp.float32),
        (((1,), (1,)), ((), ())),
        precision=lax.Precision.HIGHEST,
    )
    row_terms = jnp.sum(latent_grad * projected, axis=1)
    cubed = root_mean * root_mean * root_mean
    hidden_grad = (
        backward / root_mean[:, None] - hidden_wide * (row_terms / (D * cubed))[:, None]
    ).astype(jnp.bfloat16)
    weight_part = lax.dot_general(
        hidden_wide / root_mean[:, None],
        latent_grad,
        (((0,), (0,)), ((), ())),
        precision=lax.Precision.HIGHEST,
    )
    weight_grad = lax.psum(weight_part.astype(jnp.bfloat16), "seq").astype(jnp.float32) / math.sqrt(
        local_rows * seq_count
    )
    return (hidden_grad, weight_grad)


def solution(mesh):
    placed = (
        P("seq", "mp"),
        P("mp", None),
        P("seq", None),
        P(),
        P("seq"),
        P("role", None, None, ("seq", "mp")),
        P("role", None, None),
        P("role", "seq", None, None),
        P("role", "seq", None, None),
    )
    return jax.shard_map(
        body, mesh=mesh, in_specs=placed, out_specs=(P("seq", "mp"), P("mp", None)), check_vma=False
    )
```

profile of v0, /device:TPU:2, one launch (start us, length us, event | category | flops | bytes accessed | tf_op | source)
XLA Modules:
  0.0 1281.3 jit_solution(4687699539010121972)
XLA Ops:
  9.6 28.2 %all-reduce = (f32[128,64]{1,0:T(8,128)S(1)}, f32[128]{0:T(128)S(1)}) all-reduce(f32[128,64]{1,0:T(8,128)S(1)} %fusion.46, f32[128]{0:T(128)S(1)} %fusion.37), channel_id=1, replica_groups=mesh['role'=4,'seq'=32,'mp'=4] {'mp'}, use_global_device_ids=true, to_apply=%region_0.0 | all-reduce | flops 8320 | bytes 66560 | tf_op jit(solution)/shard_map/psum | solution.py:73
  39.5 84.4 %all_gather.18 = bf16[4096,64]{1,0:T(8,128)(2,1)S(1)} all-gather(bf16[128,64]{1,0:T(8,128)(2,1)S(1)} %get-tuple-element.146), channel_id=1, replica_groups=mesh['role'=4,'seq'=32,'mp'=4] {'seq'}, dimensions={0}, use_global_device_ids=true | all-gather | bytes 540672 | tf_op jit(solution)/shard_map/all_gather | solution.py:88
  123.9 72.6 %all-gather.1 = s32[32,1,128]{2,1,0:T(1,128)S(1)} all-gather(s32[1,1,128]{2,1,0:T(1,128)} %bitcast.152), channel_id=1, replica_groups=mesh['role'=4,'seq'=32,'mp'=4] {'seq'}, dimensions={0}, use_global_device_ids=true | all-gather | bytes 16896 | tf_op jit(solution)/shard_map/all_gather | solution.py:89
  197.8 169.7 %all-gather = f32[128,40,2]{1,2,0:T(2,128)S(1)} all-gather(f32[1,40,2]{1,2,0:T(2,128)S(1)} %bitcast.150), channel_id=1, replica_groups=mesh['role'=4,'seq'=32,'mp'=4] {'seq','mp'}, dimensions={0}, use_global_device_ids=true | all-gather | bytes 41280 | tf_op jit(solution)/shard_map/all_gather | solution.py:107
  367.8 13.5 %while.27 = (s32[]{:T(128)}, bf16[2,512,128]{2,1,0:T(8,128)(2,1)S(1)}, bf16[2,512,128]{2,1,0:T(8,128)(2,1)S(1)}, bf16[2,512,128]{2,1,0:T(8,128)(2,1)S(1)}, bf16[...) while((s32[]{:T(128)}, ...), condition=%wide.region_7.8_spmd, body=%wide.region_3.7_spmd.sunk | while | flops 2365987328 | bytes 47202448 | solution.py:131
  367.9 2.8 multiply_reduce_fusion.6
  370.8 2.6 fusion.63
  374.6 2.8 multiply_reduce_fusion.6
  377.5 2.6 fusion.63
  382.9 39.3 %all-gather.5.cloned.1.call-done = bf16[4096,128]{1,0:T(8,128)(2,1)} async-done(((bf16[1024,128]{1,0:T(8,128)(2,1)}), bf16[4096,128]{1,0:T(8,128)(2,1)}) %all-gather.5.cloned.1.call-update) | async-done | bytes 1048592 | tf_op jit(solution)/shard_map/all_gather | solution.py:147
  422.3 33.8 %all-gather.7.cloned.1.call-done = bf16[4096,128]{1,0:T(8,128)(2,1)} async-done(((bf16[1024,128]{1,0:T(8,128)(2,1)}), bf16[4096,128]{1,0:T(8,128)(2,1)}) %all-gather.7.cloned.1.call-update) | async-done | bytes 1048592 | tf_op jit(solution)/shard_map/all_gather | solution.py:148
  456.0 23.6 %while.28 = (s32[]{:T(128)}, f32[1024,128]{1,0:T(8,128)S(1)}, f32[1024]{0:T(1024)S(1)}, bf16[8,512,128]{2,1,0:T(8,128)(2,1)}, bf16[1024,128]{1,0:T(8,128)(2,1)S(...) while((s32[]{:T(128)}, f32[1024,128]{1,0:T(8,128)S(1)}, f32[1024]{0:T(1024)S(1)}, ...), condition=%wide.region_10.11_spmd.clone, body=%wide.region_8.10_spmd.clone.sunk | while | flops 270795776 | bytes 5784672 | solution.py:49
  460.4 1.5 convolution_add_fusion.2
  466.3 1.5 convolution_add_fusion.2
  469.2 1.5 convolution_add_fusion.2
  475.1 1.5 convolution_add_fusion.2
  478.1 1.5 convolution_add_fusion.2
  479.6 1.8 convolution_convert_fusion.1
  481.5 156.6 %reduce-scatter.4.cloned.1.call-done = bf16[32,64]{1,0:T(8,128)(2,1)} async-done(((bf16[1024,64]{1,0:T(8,128)(2,1)}), bf16[32,64]{1,0:T(8,128)(2,1)}) %reduce-scatter.4.cloned.1.call-update) | async-done | bytes 4112 | tf_op jit(solution)/shard_map/reduce_scatter | solution.py:152
  638.8 14.1 %all-reduce.1 = (f32[32,64]{1,0:T(8,128)S(1)}, f32[32,64]{1,0:T(8,128)S(1)}) all-reduce(f32[32,64]{1,0:T(8,128)S(1)} %get-tuple-element.165, f32[32,64]{1,0:T(8,128)S(1)} %get-tuple-element.164), channel_id=1, replica_groups=mesh['role'=4,'seq'=32,'mp'=4] {'role'}, use_global_device_ids=true, to_apply=%region_12.13 | all-reduce | flops 4096 | bytes 32768 | tf_op jit(solution)/shard_map/psum | solution.py:168
  653.5 286.5 %psum.46 = f32[]{:T(128)} all-reduce(f32[]{:T(128)} %abs_reduce_fusion), channel_id=1, replica_groups=mesh['role'=4,'seq'=32,'mp'=4] {'seq','mp'}, use_global_device_ids=true, to_apply=%region_15.16 | all-reduce | flops 1 | bytes 8 | tf_op jit(solution)/shard_map/psum | solution.py:173
  940.7 11.5 all_gather.23
  954.8 318.3 %all-reduce.4.cloned.1.call-done = bf16[1280,64]{0,1:T(8,128)(2,1)} async-done(((bf16[1280,64]{0,1:T(8,128)(2,1)}), bf16[1280,64]{0,1:T(8,128)(2,1)}) %all-reduce.4.cloned.1.call-update) | async-done | bytes 163856 | tf_op jit(solution)/shard_map/psum | solution.py:193
  1273.1 1.7 convert_multiply_fusion.2
  (96 shorter events, 28.3 us)
Async XLA Ops:
  7.2 1.2 copy-start
  7.2 415.1 %all-gather.5.cloned.1.call-start = ((), (), s32[]{:S(2)}) async-start(), calls=%async_computation.1 | async-start | bytes 1310720 | tf_op jit(solution)/shard_map/all_gather | solution.py:147
  367.9 2.9 copy-start.4
  374.6 2.9 copy-start.4
  381.4 0.7 copy-start.2
  381.4 0.8 copy-start.3
  382.1 73.9 %all-gather.7.cloned.1.call-start = ((), (), s32[]{:S(2)}) async-start(), calls=%async_computation.2 | async-start | bytes 1310720 | tf_op jit(solution)/shard_map/all_gather | solution.py:148
  382.9 255.2 %reduce-scatter.4.cloned.1.call-start = ((), (), s32[]{:S(2)}) async-start(), calls=%async_computation.4 | async-start | bytes 270336 | tf_op jit(solution)/shard_map/reduce_scatter | solution.py:152
  456.0 496.2 %copy-start.1 = (bf16[128,1280]{1,0:T(8,128)(2,1)S(1)}, bf16[128,1280]{1,0:T(8,128)(2,1)}, u32[]{:S(2)}) copy-start(bf16[128,1280]{1,0:T(8,128)(2,1)} %param.13) | copy-start | bytes 983044
  481.4 791.7 %all-reduce.4.cloned.1.call-start = ((), (), s32[]{:S(2)}) async-start(), calls=%async_computation.3 | async-start | bytes 327680 | tf_op jit(solution)/shard_map/psum | solution.py:193
Sparse Core Ops, SparseCore 0:
  382.2 39.9 all-gather.4
  425.0 31.0 all-gather.6
  481.5 156.4 reduce-scatter.3
  953.8 319.2 all-reduce.3
where the time goes:
time: 1280 us
  blocking collectives  667 us (52%)
  waiting for transfers between devices  549 us (43%)
  matrix products  40.6 us (3%)
  between operations  15.3 us (1%)
    psum x1, waiting for transfers between devices, body(): lax.psum(weight_part.astype(jnp.bfloat16), 'seq').astype(jnp.float32)  318 us
    psum x1, blocking collectives, body(): totals = lax.psum(magnitude, ('seq', 'mp'))  287 us
    all_gather x1, blocking collectives, body(): lax.all_gather(modulation_part, ('seq', 'mp'), axis=1, tiled=True)  170 us
    reduce_scatter x1, waiting for transfers between devices, body(): lax.psum_scatter(jnp.dot(attended, readout_weight[0, 0], preferred_elemen...  157 us
    all_gather x1, blocking collectives, body(): lax.all_gather(noisy, 'seq', axis=0, tiled=True)  84.4 us
    all_gather x1, blocking collectives, body(): lax.all_gather(token_order, 'seq', axis=0, tiled=True)  72.6 us
    all_gather x1, waiting for transfers between devices, body(): lax.all_gather(keys, 'mp', axis=0, tiled=True)  39.3 us
    all_gather x1, waiting for transfers between devices, body(): lax.all_gather(values, 'mp', axis=0, tiled=True)  33.8 us
  transfers between devices with their start and end apart: 4, of which 4 were waited for; matrix products, arithmetic and copies ran while one was open for 0% of the time, Pallas kernels for 0%

commit v1 on v0

v1 whole, which is shorter than its diff:
```python
import functools
import math

import jax
import jax.numpy as jnp
from jax import lax
from jax.experimental import pallas as pl
from jax.experimental.pallas import tpu as pltpu
from jax.sharding import PartitionSpec as P

D = 5120
FREQ = 256
T_STEPS = 1000


EPS_NORM = 1e-06
EPS_MEAN = 1e-05
GUIDANCE = 5.0
ROPE_BASE = 10000.0
SHARPNESS = 4.0


def pack(block):
    count = block.shape[0] // 2
    return jnp.concatenate([block[:count], block[count:]], axis=1)


def unpack(block):
    width = block.shape[1] // 2
    return jnp.concatenate([block[:, :width], block[:, width:]], axis=0)


def split(values):
    high = values.astype(jnp.bfloat16)
    return high, (values - high.astype(jnp.float32)).astype(jnp.bfloat16)


def exchange(chunks, axes):
    return lax.all_to_all(chunks, axes, 0, 0, tiled=True)


def to_all(chunk, axes, count):
    return exchange(jnp.broadcast_to(chunk[None], (count, *chunk.shape)), axes)


def dot32(left, right):
    return jnp.dot(left, right, preferred_element_type=jnp.float32)


def normalize_rope(vectors, cosines, sines):
    rescaled = vectors * lax.rsqrt(jnp.mean(vectors * vectors, axis=1, keepdims=True) + EPS_NORM)
    width = vectors.shape[1] // 2
    front = rescaled[:, :width]
    back = rescaled[:, width:]
    return jnp.concatenate(
        [front * cosines - back * sines, front * sines + back * cosines], axis=1
    ).astype(jnp.bfloat16)


def attend_kernel(query_ref, key_ref, value_ref, readout_ref, score_ref, wide, attended):
    query_rows, head_dim = query_ref.shape
    key_rows = key_ref.shape[0]
    rows, width = 256, 512
    wide[:, :head_dim] = value_ref[...]
    wide[:, head_dim:] = jnp.ones((key_rows, head_dim), jnp.bfloat16)
    factor = SHARPNESS / math.sqrt(head_dim) * math.log2(math.e)

    def step(index, carry):
        at = pl.multiple_of(index * rows, rows)
        queries = query_ref[pl.ds(at, rows), :]
        total = jnp.zeros((rows, 2 * head_dim), jnp.float32)
        for begin in range(0, key_rows, width):
            scores = lax.dot_general(
                queries,
                key_ref[begin : begin + width, :],
                (((1,), (1,)), ((), ())),
                preferred_element_type=jnp.float32,
            )
            weights = jnp.exp2(scores * factor).astype(jnp.bfloat16)
            total = total + dot32(weights, wide[begin : begin + width, :])
        attended[pl.ds(at, rows), :] = (total[:, :head_dim] / total[:, head_dim:]).astype(
            jnp.bfloat16
        )
        return carry

    lax.fori_loop(0, query_rows // rows, step, 0)
    half = query_rows // 2
    score_ref[...] = jnp.concatenate(
        [dot32(attended[:half, :], readout_ref[...]), dot32(attended[half:, :], readout_ref[...])],
        axis=1,
    ).astype(jnp.bfloat16)


def attend(queries, keys, values, readout):
    query_rows, head_dim = queries.shape
    key_rows = keys.shape[0]
    return pl.pallas_call(
        attend_kernel,
        out_shape=jax.ShapeDtypeStruct((query_rows // 2, 2 * readout.shape[1]), jnp.bfloat16),
        in_specs=[pl.BlockSpec(memory_space=pltpu.VMEM)] * 4,
        out_specs=pl.BlockSpec(memory_space=pltpu.VMEM),
        scratch_shapes=[
            pltpu.VMEM((key_rows, 2 * head_dim), jnp.bfloat16),
            pltpu.VMEM((query_rows, head_dim), jnp.bfloat16),
        ],
        compiler_params=pltpu.CompilerParams(vmem_limit_bytes=32 * 1024 * 1024),
    )(queries, keys, values, readout)


def body(
    gen_hidden,
    out_weight,
    noise,
    step_index,
    token_order,
    time_weight,
    embed_weight,
    qkv_weight,
    readout_weight,
):
    seq_count = lax.axis_size("seq")
    mp_count = lax.axis_size("mp")
    role_count = lax.axis_size("role")
    mp_index = lax.axis_index("mp")
    local_rows = gen_hidden.shape[0]
    packed_rows = local_rows // 2
    quarter = packed_rows // mp_count
    head_dim = qkv_weight.shape[3] // 3
    lat_dim = out_weight.shape[1]
    lanes = 2 * lat_dim
    mod_width = time_weight.shape[3]
    f32 = jnp.float32
    timestep = step_index[0].astype(f32)
    noise_level = timestep / T_STEPS

    half_freq = FREQ // 2
    frequencies = jnp.exp(-math.log(ROPE_BASE) * jnp.arange(half_freq, dtype=f32) / half_freq)
    phases = timestep * frequencies
    activated = jax.nn.silu(jnp.concatenate([jnp.cos(phases), jnp.sin(phases)]))
    modulation_part = jnp.sum(activated[:, None, None] * time_weight[0], axis=0)

    hidden_wide = gen_hidden.astype(f32)
    mod_row = jnp.pad(modulation_part.reshape(1, 2 * mod_width), ((0, 0), (0, lanes - 2 * mod_width)))
    first = jnp.concatenate(
        [
            pack(dot32(gen_hidden, out_weight)),
            jnp.sum(hidden_wide * hidden_wide, axis=1)[None],
            mod_row,
            jnp.zeros((6, lanes), f32),
        ]
    )
    first = to_all(first, "mp", mp_count)
    projected = jnp.sum(first[:, :packed_rows], axis=0)
    squares = jnp.sum(first[:, packed_rows], axis=0)
    root_mean = jnp.sqrt(squares / D + EPS_NORM)
    root_packed = pack(jnp.broadcast_to(root_mean[:, None], (local_rows, lat_dim)))
    latent = projected / root_packed
    noisy = ((1.0 - noise_level) * latent + noise_level * pack(noise).astype(f32)).astype(
        jnp.bfloat16
    )

    mod_rows = -(-2 * mp_count * mod_width // lanes)
    mod_mine = (
        first[:, packed_rows + 1, : 2 * mod_width]
        .reshape(mp_count, 2, mod_width)
        .transpose(1, 0, 2)
        .reshape(2 * mp_count * mod_width)
    )
    mod_mine = jnp.pad(mod_mine, (0, mod_rows * lanes - mod_mine.shape[0])).reshape(mod_rows, lanes)
    order = jnp.stack([token_order // 64, token_order % 64]).astype(jnp.bfloat16)
    used = packed_rows + 2 + 2 * mod_rows
    second = jnp.concatenate(
        [noisy, order, *split(mod_mine), jnp.zeros((-used % 16, lanes), jnp.bfloat16)]
    )
    second = to_all(second, "seq", seq_count)
    rows = second[:, :packed_rows]
    order_wide = second[:, packed_rows : packed_rows + 2].astype(f32)
    positions = order_wide[:, 0] * 64.0 + order_wide[:, 1]
    mod_at = packed_rows + 2
    modulation = (
        second[:, mod_at : mod_at + mod_rows].astype(f32)
        + second[:, mod_at + mod_rows : mod_at + 2 * mod_rows].astype(f32)
    ).reshape(seq_count, mod_rows * lanes)[:, : 2 * mp_count * mod_width]
    modulation = modulation.reshape(seq_count, 2, mp_count * mod_width).transpose(1, 0, 2).reshape(2, D)

    embed = embed_weight[0]
    weights = qkv_weight[0, 0]
    scaled = split(embed.astype(f32) * (1.0 + modulation[1])[None])
    shifted = split(modulation[0][None])
    folded = dot32(jnp.concatenate([*scaled, *shifted], axis=0), weights)
    matrix = folded[:lat_dim] + folded[lat_dim : 2 * lat_dim]
    offset = folded[2 * lat_dim] + folded[2 * lat_dim + 1]
    gram = lax.dot_general(embed, embed, (((1,), (1,)), ((), ())), preferred_element_type=f32)
    matrix_parts = split(jnp.concatenate([matrix, gram], axis=1))

    def project(block):
        product = dot32(block, matrix_parts[0]) + dot32(block, matrix_parts[1])
        mean = jnp.sum(block.astype(f32) * product[:, 3 * head_dim :], axis=1, keepdims=True) / D
        return product[:, : 3 * head_dim] * lax.rsqrt(mean + EPS_NORM) + offset[None]

    inverse = jnp.exp(-math.log(ROPE_BASE) * jnp.arange(head_dim // 2, dtype=f32) * 2.0 / head_dim)

    def turn(places):
        angles = places.reshape(-1)[:, None] * inverse[None, :]
        return jnp.cos(angles), jnp.sin(angles)

    mine = lax.dynamic_slice_in_dim(rows, mp_index * quarter, quarter, 1)
    all_rows = jnp.concatenate(
        [rows[:, :, :lat_dim].reshape(-1, lat_dim), rows[:, :, lat_dim:].reshape(-1, lat_dim)]
    )
    combined = project(all_rows)
    cosines, sines = turn(
        jnp.concatenate([positions[:, :packed_rows].reshape(-1), positions[:, packed_rows:].reshape(-1)])
    )
    keys = normalize_rope(combined[:, head_dim : 2 * head_dim], cosines, sines)
    values = combined[:, 2 * head_dim :].astype(jnp.bfloat16)

    def own(array):
        grid = array.reshape(2, seq_count, packed_rows, array.shape[1])
        return lax.dynamic_slice_in_dim(grid, mp_index * quarter, quarter, 2).reshape(-1, array.shape[1])

    queries = normalize_rope(own(combined[:, :head_dim]), own(cosines), own(sines))
    scores = attend(queries, keys, values, readout_weight[0, 0])

    scores = exchange(scores.reshape(seq_count, quarter, lanes), "seq")
    score = jnp.sum(scores.astype(f32), axis=0)

    score = to_all(score, ("role", "mp"), role_count * mp_count).reshape(
        role_count, packed_rows, lanes
    )
    realistic = GUIDANCE * score[1] + (1.0 - GUIDANCE) * score[2]
    difference = score[3] - realistic
    magnitude = jnp.sum(jnp.abs(latent - (noisy.astype(f32) - noise_level * realistic)))

    direction = split(unpack(difference / root_packed))
    both = jnp.concatenate(direction, axis=1)
    weight_part = lax.dot_general(
        gen_hidden, both, (((0,), (0,)), ((), ())), preferred_element_type=f32
    )
    weight_part = pack(weight_part[:, :lat_dim] + weight_part[:, lat_dim:])
    share = weight_part.shape[0] // seq_count
    pieces = []
    rest = magnitude
    for unused in range(3):
        piece = rest.astype(jnp.bfloat16)
        rest = rest - piece.astype(f32)
        pieces.append(piece)
    extra = jnp.pad(jnp.stack(pieces)[None], ((0, 0), (0, lanes - 3)))
    padding = -(share + 1) % 16
    third = jnp.concatenate(
        [
            weight_part.astype(jnp.bfloat16).reshape(seq_count, share, lanes),
            jnp.broadcast_to(extra[None], (seq_count, 1, lanes)),
            jnp.zeros((seq_count, padding, lanes), jnp.bfloat16),
        ],
        axis=1,
    )
    third = jnp.sum(exchange(third, "seq").astype(f32), axis=0)
    cell_count = local_rows * seq_count * lat_dim
    spread = jnp.sum(third[share]) / cell_count + EPS_MEAN
    factor = -noise_level / spread
    fourth = (third[: share + 1 + padding] * (factor / math.sqrt(local_rows * seq_count))).astype(
        jnp.bfloat16
    )
    fourth = to_all(fourth, "seq", seq_count)
    weight_grad = unpack(fourth[:, :share].reshape(seq_count * share, lanes).astype(f32))

    backward = lax.dot_general(
        both,
        jnp.concatenate([out_weight, out_weight], axis=1),
        (((1,), (1,)), ((), ())),
        preferred_element_type=f32,
    )
    row_terms = jnp.sum(unpack(difference * projected), axis=1)
    cubed = root_mean * root_mean * root_mean
    hidden_grad = (
        factor * (backward - hidden_wide * (row_terms / (D * cubed))[:, None])
    ).astype(jnp.bfloat16)
    return (hidden_grad, weight_grad)


def solution(mesh):
    placed = (
        P("seq", "mp"),
        P("mp", None),
        P("seq", None),
        P(),
        P("seq"),
        P("role", None, None, ("seq", "mp")),
        P("role", None, None),
        P("role", "seq", None, None),
        P("role", "seq", None, None),
    )
    return jax.shard_map(
        body, mesh=mesh, in_specs=placed, out_specs=(P("seq", "mp"), P("mp", None)), check_vma=False
    )
```

time: 1280 us -> 178 us (0.14)
  the two profiles are of different devices: /device:TPU:2 before, /device:TPU:8 now
where the time goes in v1:
time: 178 us; the launch traced here: 177 us
  waiting for transfers between devices  62.9 us (35%)
  starting transfers between devices  33.4 us (19%)
  other arithmetic  23.8 us (13%)
  local copies, waits for them, and re-layouts  23.4 us (13%)
  blocking collectives  14.7 us (8%)
  matrix products  8.39 us (5%)
  Pallas kernels  6.8 us (4%)
  between operations  3.93 us (2%)
    all_to_all x5, waiting for transfers between devices, exchange(): return lax.all_to_all(chunks, axes, 0, 0, tiled=True)  62.9 us
    all_to_all x5, starting transfers between devices, exchange(): return lax.all_to_all(chunks, axes, 0, 0, tiled=True)  33.4 us
    all_to_all x1, blocking collectives, exchange(): return lax.all_to_all(chunks, axes, 0, 0, tiled=True)  14.7 us
    unnamed x24, local copies, waits for them, and re-layouts  10.4 us
    another operation x3, other arithmetic  9.19 us
    pallas_call x1, Pallas kernels, attend(): pl.pallas_call(attend_kernel, out_shape=jax.ShapeDtypeStruct((query_rows...  6.8 us
    dot_general x4, matrix products, dot32(): return jnp.dot(left, right, preferred_element_type=jnp.float32)  6.69 us
  transfers between devices with their start and end apart: 5, of which 5 were waited for; matrix products, arithmetic and copies ran while one was open for 2% of the time, Pallas kernels for 0%

profile of v1, /device:TPU:8, one launch (start us, length us, event | category | flops | bytes accessed | tf_op | source)
XLA Modules:
  0.0 177.4 jit_solution(14705416927292496657)
XLA Ops:
  1.3 1.1 fusion.21
  2.5 1.3 fusion.71
  6.1 10.3 %all-to-all-start = ((f32[4,72,128]{2,1,0:T(8,128)}), f32[4,72,128]{2,1,0:T(8,128)S(1)}, u32[]{:S(2)}, u32[]{:S(2)}) async-start(f32[4,72,128]{2,1,0:T(8,128)} %broadcast_in_dim.36), calls=%async_computation | async-start | bytes 294912 | tf_op jit(solution)/shard_map/all_to_all | solution.py:39
  17.4 9.2 %all-to-all-done = f32[4,72,128]{2,1,0:T(8,128)S(1)} async-done(((f32[4,72,128]{2,1,0:T(8,128)}), f32[4,72,128]{2,1,0:T(8,128)S(1)}, u32[]{:S(2)}, u32[]{:S(2)}) %all-to-all-start) | async-done | bytes 147488 | tf_op jit(solution)/shard_map/all_to_all | solution.py:39
  28.2 9.4 %all-to-all-start.1 = ((bf16[32,80,128]{2,1,0:T(8,128)(2,1)}), bf16[32,80,128]{2,1,0:T(8,128)(2,1)S(1)}, u32[]{:S(2)}, u32[]{:S(2)}) async-start(bf16[32,80,128]{2,1,0:T(8,128)(2,1)} %broadcast_in_dim.78), calls=%async_computation.1 | async-start | bytes 1310720 | tf_op jit(solution)/shard_map/all_to_all | solution.py:39
  38.2 19.9 %all-to-all-done.1 = bf16[32,80,128]{2,1,0:T(8,128)(2,1)S(1)} async-done(((bf16[32,80,128]{2,1,0:T(8,128)(2,1)}), bf16[32,80,128]{2,1,0:T(8,128)(2,1)S(1)}, u32[]{:S(2)}, u32[]{:S(2)}) %all-to-all-start.1) | async-done | bytes 655392 | tf_op jit(solution)/shard_map/all_to_all | solution.py:39
  58.9 3.1 %fusion = f32[130,384]{1,0:T(8,128)S(1)} fusion(bf16[1,1,5120,384]{3,2,1,0:T(8,128)(2,1)} %param.16, bf16[1,5120]{1,0:T(2,128)(2,1)S(1)} %get-tuple-element.41, bf16[1,5120]{1,0:T(2,128)(2,1)S(1)} %get-tuple-element.40, bf16[64,5120]{1,0:T(8,128)(2,1)S(1)} %get-tuple-element.23, bf16[64,5120]{1,0:T(8,128)(2,1)S(1)} %get-tuple-element.22), kind=kOutput, calls=%fused_computation.2 | convolution fusion | flops 516505600 | bytes 5463040 | tf_op jit(solution)/shard_map/dot_general | solution.py:47
  62.7 1.1 fusion.32
  63.8 1.1 convolution_add_fusion
  65.2 3.1 %slice.230 = f32[4096,384]{0,1:T(8,128)} slice(f32[4096,448]{0,1:T(8,128)S(1)} %convolution_add_fusion), slice={[0:4096], [0:384]} | slice | bytes 12582912 | tf_op jit(solution)/shard_map/slice | solution.py:199
  68.2 6.5 %copy.73 = f32[4096,384]{1,0:T(8,128)} copy(f32[4096,384]{0,1:T(8,128)} %slice.230) | data formatting | bytes 12582912
  74.8 3.2 %multiply_add_fusion = f32[4096,384]{1,0:T(8,128)S(1)} fusion(f32[4096,384]{1,0:T(8,128)} %copy.73, f32[384]{0:T(512)S(1)} %fusion.47, f32[4096]{0:T(1024)S(1)} %add_rsqrt_fusion.2), kind=kLoop, calls=%fused_computation | loop fusion | flops 3145728 | bytes 12600832 | tf_op jit(solution)/shard_map/add | solution.py:199
  78.6 2.0 %copy-done = f32[4096,384]{1,0:T(8,128)} copy-done((f32[4096,384]{1,0:T(8,128)}, f32[4096,384]{1,0:T(8,128)S(1)}, u32[]{:S(2)}) %copy-start) | copy-done | bytes 6291480
  81.0 2.6 %slice_multiply_fusion = (f32[4096,128]{1,0:T(8,128)S(1)}, f32[4096,128]{1,0:T(8,128)S(1)}) fusion(f32[4096,384]{1,0:T(8,128)} %copy-done, f32[4096]{0:T(1024)S(1)} %add_rsqrt_fusion.1), kind=kLoop, calls=%fused_computation.20 | loop fusion | flops 524288 | bytes 8404992 | tf_op jit(solution)/shard_map/mul | solution.py:51
  84.3 2.7 %dynamic-slice_cosine_fusion = (f32[2,32,16,64]{3,2,1,0:T(8,128)}, f32[2,32,16,64]{3,2,1,0:T(8,128)}) fusion(f32[2,32,64,64]{3,2,1,0:T(8,128)S(1)} %broadcast_multiply_fusion, s32[]{:T(128)S(6)} %select_n.19), kind=kLoop, calls=%fused_computation.54 | loop fusion | bytes 786436 | tf_op jit(solution)/shard_map/cos | solution.py:205
  87.9 8.9 %fusion.9 = (bf16[4096,64]{1,0:T(8,128)(2,1)S(1)}, bf16[4096,64]{1,0:T(8,128)(2,1)S(1)}) fusion(f32[4096,128]{1,0:T(8,128)S(1)} %get-tuple-element.14, f32[4096]{0:T(1024)S(1)} %pad_maximum_fusion.11, f32[64]{0:T(128)S(1)} %multiply_exponential_fusion), kind=kLoop, calls=%fused_computation.15 | loop fusion | flops 2359296 | bytes 3162368 | tf_op jit(solution)/shard_map/convert.8
  98.6 6.8 %shard_map.104 = bf16[512,128]{1,0:T(8,128)(2,1)S(1)} custom-call(bf16[1024,128]{1,0:T(8,128)(2,1)S(1)} %pad_maximum_fusion.3.query_ref, bf16[4096,128]{1,0:T(8,128)(2,1)S(1)} %pad_maximum_fusion.key_ref, bf16[4096,128]{1,0:T(8,128)(2,1)S(1)} %slice.318.value_ref, bf16[128,64]{1,0:T(8,128)(2,1)S(1)} %bitcast.83), custom_call_target="tpu_custom_call" | custom-call | tf_op jit(solution)/shard_map/pallas_call | solution.py:97
  105.4 14.7 %all_to_all.30 = bf16[32,16,128]{2,1,0:T(8,128)(2,1)S(1)} all-to-all(bf16[32,16,128]{2,1,0:T(8,128)(2,1)S(1)} %bitcast.82), channel_id=1, replica_groups=mesh['role'=4,'seq'=32,'mp'=4] {'seq'}, dimensions={0} | all-to-all | bytes 262144 | tf_op jit(solution)/shard_map/all_to_all | solution.py:39
  120.8 4.4 %all-to-all-start.3 = ((f32[16,16,128]{2,1,0:T(8,128)}), f32[16,16,128]{2,1,0:T(8,128)S(1)}, u32[]{:S(2)}, u32[]{:S(2)}) async-start(f32[16,16,128]{2,1,0:T(8,128)} %broadcast_in_dim.79), calls=%async_computation.3 | async-start | bytes 262144 | tf_op jit(solution)/shard_map/all_to_all | solution.py:39
  125.5 10.4 %all-to-all-done.3 = f32[16,16,128]{2,1,0:T(8,128)S(1)} async-done(((f32[16,16,128]{2,1,0:T(8,128)}), f32[16,16,128]{2,1,0:T(8,128)S(1)}, u32[]{:S(2)}, u32[]{:S(2)}) %all-to-all-start.3) | async-done | bytes 131104 | tf_op jit(solution)/shard_map/all_to_all | solution.py:39
  140.1 5.0 %all-to-all-start.4 = ((bf16[32,32,128]{2,1,0:T(8,128)(2,1)}), bf16[32,32,128]{2,1,0:T(8,128)(2,1)S(1)}, u32[]{:S(2)}, u32[]{:S(2)}) async-start(bf16[32,32,128]{2,1,0:T(8,128)(2,1)} %maximum_maximum_fusion), calls=%async_computation.4 | async-start | bytes 524288 | tf_op jit(solution)/shard_map/all_to_all | solution.py:39
  145.2 12.5 %all-to-all-done.4 = bf16[32,32,128]{2,1,0:T(8,128)(2,1)S(1)} async-done(((bf16[32,32,128]{2,1,0:T(8,128)(2,1)}), bf16[32,32,128]{2,1,0:T(8,128)(2,1)S(1)}, u32[]{:S(2)}, u32[]{:S(2)}) %all-to-all-start.4) | async-done | bytes 262176 | tf_op jit(solution)/shard_map/all_to_all | solution.py:39
  159.8 4.2 %all-to-all-start.5 = ((bf16[32,32,128]{2,1,0:T(8,128)(2,1)}), bf16[32,32,128]{2,1,0:T(8,128)(2,1)S(1)}, u32[]{:S(2)}, u32[]{:S(2)}) async-start(bf16[32,32,128]{2,1,0:T(8,128)(2,1)} %broadcast_in_dim.88), calls=%async_computation.5 | async-start | bytes 524288 | tf_op jit(solution)/shard_map/all_to_all | solution.py:39
  165.3 10.9 %all-to-all-done.5 = bf16[32,32,128]{2,1,0:T(8,128)(2,1)S(1)} async-done(((bf16[32,32,128]{2,1,0:T(8,128)(2,1)}), bf16[32,32,128]{2,1,0:T(8,128)(2,1)S(1)}, u32[]{:S(2)}, u32[]{:S(2)}) %all-to-all-start.5) | async-done | bytes 262176 | tf_op jit(solution)/shard_map/all_to_all | solution.py:39
  (121 shorter events, 18.8 us)
Async XLA Ops:
  0.6 16.8 %copy-start.8 = (s32[128]{0:T(128)S(1)}, s32[128]{0:T(128)}, u32[]{:S(2)}) copy-start(s32[128]{0:T(128)} %param.13) | copy-start | bytes 1540
  2.5 35.2 %copy-start.7 = (bf16[1,1,128,64]{2,3,1,0:T(8,128)(2,1)S(1)}, bf16[1,1,128,64]{2,3,1,0:T(8,128)(2,1)}, u32[]{:S(2)}) copy-start(bf16[1,1,128,64]{2,3,1,0:T(8,128)(2,1)} %param.17) | copy-start | bytes 49156
  2.5 35.3 %copy-start.5 = (bf16[1,64,5120]{2,1,0:T(8,128)(2,1)S(1)}, bf16[1,64,5120]{2,1,0:T(8,128)(2,1)}, u32[]{:S(2)}) copy-start(bf16[1,64,5120]{2,1,0:T(8,128)(2,1)} %param.15) | copy-start | bytes 1966084
  6.1 20.6 %all-to-all-start = ((f32[4,72,128]{2,1,0:T(8,128)}), f32[4,72,128]{2,1,0:T(8,128)S(1)}, u32[]{:S(2)}, u32[]{:S(2)}) async-start(f32[4,72,128]{2,1,0:T(8,128)} %broadcast_in_dim.36), calls=%async_computation | async-start | bytes 294912 | tf_op jit(solution)/shard_map/all_to_all | solution.py:39
  28.2 29.9 %all-to-all-start.1 = ((bf16[32,80,128]{2,1,0:T(8,128)(2,1)}), bf16[32,80,128]{2,1,0:T(8,128)(2,1)S(1)}, u32[]{:S(2)}, u32[]{:S(2)}) async-start(bf16[32,80,128]{2,1,0:T(8,128)(2,1)} %broadcast_in_dim.78), calls=%async_computation.1 | async-start | bytes 1310720 | tf_op jit(solution)/shard_map/all_to_all | solution.py:39
  78.0 2.7 %copy-start = (f32[4096,384]{1,0:T(8,128)}, f32[4096,384]{1,0:T(8,128)S(1)}, u32[]{:S(2)}) copy-start(f32[4096,384]{1,0:T(8,128)S(1)} %multiply_add_fusion) | copy-start | bytes 18874372
  96.9 1.0 copy-start.4
  96.9 1.2 copy-start.2
  96.9 1.3 copy-start.3
  98.6 39.7 %copy-start.1 = (bf16[128,1280]{1,0:T(8,128)(2,1)S(1)}, bf16[128,1280]{1,0:T(8,128)(2,1)}, u32[]{:S(2)}) copy-start(bf16[128,1280]{1,0:T(8,128)(2,1)} %param.9) | copy-start | bytes 983044
  120.8 15.0 %all-to-all-start.3 = ((f32[16,16,128]{2,1,0:T(8,128)}), f32[16,16,128]{2,1,0:T(8,128)S(1)}, u32[]{:S(2)}, u32[]{:S(2)}) async-start(f32[16,16,128]{2,1,0:T(8,128)} %broadcast_in_dim.79), calls=%async_computation.3 | async-start | bytes 262144 | tf_op jit(solution)/shard_map/all_to_all | solution.py:39
  138.7 25.5 %copy-start.6 = (bf16[1280,64]{0,1:T(8,128)(2,1)S(1)}, bf16[1280,64]{0,1:T(8,128)(2,1)}, u32[]{:S(2)}) copy-start(bf16[1280,64]{0,1:T(8,128)(2,1)} %param.10) | copy-start | bytes 491524
  140.1 17.6 %all-to-all-start.4 = ((bf16[32,32,128]{2,1,0:T(8,128)(2,1)}), bf16[32,32,128]{2,1,0:T(8,128)(2,1)S(1)}, u32[]{:S(2)}, u32[]{:S(2)}) async-start(bf16[32,32,128]{2,1,0:T(8,128)(2,1)} %maximum_maximum_fusion), calls=%async_computation.4 | async-start | bytes 524288 | tf_op jit(solution)/shard_map/all_to_all | solution.py:39
  159.8 16.5 %all-to-all-start.5 = ((bf16[32,32,128]{2,1,0:T(8,128)(2,1)}), bf16[32,32,128]{2,1,0:T(8,128)(2,1)S(1)}, u32[]{:S(2)}, u32[]{:S(2)}) async-start(bf16[32,32,128]{2,1,0:T(8,128)(2,1)} %broadcast_in_dim.88), calls=%async_computation.5 | async-start | bytes 524288 | tf_op jit(solution)/shard_map/all_to_all | solution.py:39

commit v2 on v1

v2 whole, which is shorter than its diff:
```python
import math

import jax
import jax.numpy as jnp
import numpy as np
from jax import lax
from jax.experimental import pallas as pl
from jax.experimental.pallas import tpu as pltpu
from jax.sharding import PartitionSpec as P

D = 5120
FREQ = 256
T_STEPS = 1000


EPS_NORM = 1e-06
EPS_MEAN = 1e-05
GUIDANCE = 5.0
ROPE_BASE = 10000.0
SHARPNESS = 4.0


def pack(block):
    count = block.shape[0] // 2
    return jnp.concatenate([block[:count], block[count:]], axis=1)


def unpack(block):
    width = block.shape[1] // 2
    return jnp.concatenate([block[:, :width], block[:, width:]], axis=0)


def split(values):
    high = values.astype(jnp.bfloat16)
    return high, (values - high.astype(jnp.float32)).astype(jnp.bfloat16)


def exchange(chunks, axes):
    return lax.all_to_all(chunks, axes, 0, 0, tiled=True)


def to_all(chunk, axes, count):
    return exchange(jnp.broadcast_to(chunk[None], (count, *chunk.shape)), axes)


def dot32(left, right):
    return jnp.dot(left, right, preferred_element_type=jnp.float32)


def rotation_tables(head_dim):
    turns = ROPE_BASE ** (-2.0 * np.arange(head_dim // 2) / head_dim) / (2.0 * np.pi)
    grain = 2.0 ** (np.floor(np.log2(turns)) - 11)
    high = np.floor(turns / grain) * grain
    return tuple(
        np.ascontiguousarray(np.broadcast_to(part[:, None], (head_dim // 2, 128)), np.float32)
        for part in (high, turns - high)
    )


def rotations(positions, high, low):
    tiles = positions.shape[1] // high.shape[1]
    high = jnp.concatenate([high] * tiles, axis=1)
    low = jnp.concatenate([low] * tiles, axis=1)
    whole = positions * high
    part = (whole - jnp.round(whole)) + positions * low
    angle = (part - jnp.round(part)) * math.pi
    square = angle * angle
    sine = square * (-1.0 / 39916800) + 1.0 / 362880
    sine = sine * square - 1.0 / 5040
    sine = sine * square + 1.0 / 120
    sine = sine * square - 1.0 / 6
    sine = (sine * square + 1.0) * angle
    cosine = square * (1.0 / 479001600) - 1.0 / 3628800
    cosine = cosine * square + 1.0 / 40320
    cosine = cosine * square - 1.0 / 720
    cosine = cosine * square + 1.0 / 24
    cosine = cosine * square - 0.5
    cosine = cosine * square + 1.0
    return 1.0 - 2.0 * sine * sine, 2.0 * sine * cosine


def normalize_rope(vectors, cosines, sines):
    rescaled = vectors * lax.rsqrt(jnp.mean(vectors * vectors, axis=0, keepdims=True) + EPS_NORM)
    width = vectors.shape[0] // 2
    front = rescaled[:width]
    back = rescaled[width:]
    return jnp.concatenate([front * cosines - back * sines, front * sines + back * cosines], axis=0)


def pass_kernel(
    place_ref,
    gathered_ref,
    embed_ref,
    weight_ref,
    readout_ref,
    high_ref,
    low_ref,
    score_ref,
    modulation,
    scaled,
    clip,
    places,
    own,
    own_places,
    query,
    key,
    wide,
    attended,
):
    f32 = jnp.float32
    blocks, used, lanes = gathered_ref.shape
    lat_dim, width = embed_ref.shape
    head_dim = weight_ref.shape[1] // 3
    key_rows = blocks * lanes
    query_rows = query.shape[0]
    quarter = query_rows // blocks
    per_tile = lanes // quarter
    piece = width // blocks
    place = place_ref[0]

    for block in range(blocks):
        at = slice(block * lanes, (block + 1) * lanes)
        clip[:lat_dim, at] = gathered_ref[block, :lat_dim, :]
        clip[lat_dim:, at] = gathered_ref[block, :lat_dim, :]
        extra = gathered_ref[block, lat_dim : lat_dim + 16, :].astype(f32)
        places[0:1, at] = extra[0:1] * 64.0 + extra[1:2]
        pair = extra[2:6] + extra[6:10]
        begin = block * piece
        modulation[0:1, begin : begin + lanes] = pair[0:1]
        modulation[0:1, begin + lanes : begin + piece] = pair[1:2, : piece - lanes]
        modulation[1:2, begin : begin + lanes] = pair[2:3]
        modulation[1:2, begin + lanes : begin + piece] = pair[3:4, : piece - lanes]

    lane = lax.broadcasted_iota(jnp.int32, (lat_dim + 16, lanes), 1)
    for tile in range(blocks // per_tile):
        found = jnp.zeros((lat_dim + 16, lanes), f32)
        for part in range(per_tile):
            block = gathered_ref[tile * per_tile + part, : lat_dim + 16, :].astype(f32)
            shift = lax.rem((part - place + per_tile) * quarter, lanes)
            found = jnp.where(lane // quarter == part, pltpu.roll(block, shift, 1), found)
        at = slice(tile * lanes, (tile + 1) * lanes)
        rows = found[:lat_dim].astype(jnp.bfloat16)
        own[:lat_dim, at] = rows
        own[lat_dim:, at] = rows
        own_places[0:1, at] = found[lat_dim : lat_dim + 1] * 64.0 + found[lat_dim + 1 : lat_dim + 2]

    chunk = width // 5
    for begin in range(0, width, chunk):
        at = slice(begin, begin + chunk)
        high, low = split(embed_ref[:, at].astype(f32) * (1.0 + modulation[1:2, at]))
        scaled[:lat_dim, at] = high
        scaled[lat_dim : 2 * lat_dim, at] = low
        row = lax.broadcasted_iota(jnp.int32, (16, chunk), 0)
        shifted = jnp.broadcast_to(modulation[0:1, at], (16, chunk))
        shifted_high = shifted.astype(jnp.bfloat16).astype(f32)
        shifted = jnp.where(row == 0, shifted_high, shifted - shifted_high)
        scaled[2 * lat_dim :, at] = jnp.where(row < 2, shifted, 0.0).astype(jnp.bfloat16)
    folded = dot32(scaled[...], weight_ref[...])
    gram = lax.dot_general(
        embed_ref[...], embed_ref[...], (((1,), (1,)), ((), ())), preferred_element_type=f32
    )
    matrix = folded[:lat_dim] + folded[lat_dim : 2 * lat_dim]
    offset = folded[2 * lat_dim : 2 * lat_dim + 1] + folded[2 * lat_dim + 1 : 2 * lat_dim + 2]
    turned = jnp.concatenate(
        [matrix, jnp.broadcast_to(offset, (lanes - lat_dim, 3 * head_dim))], axis=0
    ).T
    offsets = jnp.broadcast_to(turned[:, lat_dim : lat_dim + 1], (3 * head_dim, lanes))
    matrix_parts = jnp.concatenate(split(turned[:, :lat_dim]), axis=1)
    gram_parts = jnp.concatenate(split(gram), axis=1)

    def project(parts, offsets, rows):
        product = dot32(jnp.concatenate([parts, gram_parts], axis=0), rows)
        count = parts.shape[0]
        mean = jnp.sum(rows[:lat_dim].astype(f32) * product[count:], axis=0, keepdims=True) / width
        offsets = jnp.concatenate([offsets] * (rows.shape[1] // lanes), axis=1)
        return product[:count] * lax.rsqrt(mean + EPS_NORM) + offsets

    step = 4 * lanes
    wide[:, head_dim:] = jnp.ones((key_rows, head_dim), jnp.bfloat16)
    for begin in range(0, query_rows, step):
        at = slice(begin, begin + step)
        vectors = project(matrix_parts[:head_dim], offsets[:head_dim], own[:, at])
        turns = rotations(own_places[0:1, at], high_ref[...], low_ref[...])
        query[at, :] = normalize_rope(vectors, *turns).T.astype(jnp.bfloat16)

    def keys_and_values(index, carry):
        at = pl.ds(pl.multiple_of(index * step, step), step)
        vectors = project(matrix_parts[head_dim:], offsets[head_dim:], clip[:, at])
        turns = rotations(places[0:1, at], high_ref[...], low_ref[...])
        key[:, at] = normalize_rope(vectors[:head_dim], *turns).astype(jnp.bfloat16)
        wide[at, :head_dim] = vectors[head_dim:].T.astype(jnp.bfloat16)
        return carry

    lax.fori_loop(0, key_rows // step, keys_and_values, 0)

    rows = 256
    factor = SHARPNESS / math.sqrt(head_dim) * math.log2(math.e)

    def attend(index, carry):
        at = pl.ds(pl.multiple_of(index * rows, rows), rows)
        queries = query[at, :]
        total = jnp.zeros((rows, 2 * head_dim), f32)
        for begin in range(0, key_rows, step):
            scores = dot32(queries, key[:, begin : begin + step])
            weights = jnp.exp2(scores * factor).astype(jnp.bfloat16)
            total = total + dot32(weights, wide[begin : begin + step, :])
        result = (total[:, :head_dim] / total[:, head_dim:]).astype(jnp.bfloat16)
        attended[pl.ds(index * (rows // quarter), rows // quarter)] = result.reshape(
            rows // quarter, quarter, head_dim
        )
        return carry

    lax.fori_loop(0, query_rows // rows, attend, 0)
    half = quarter // 2
    halves = [
        dot32(attended[:, begin : begin + half, :].reshape(blocks * half, head_dim), readout_ref[...])
        for begin in (0, half)
    ]
    score_ref[...] = (
        jnp.concatenate(halves, axis=1).astype(jnp.bfloat16).reshape(blocks, half, 2 * lat_dim)
    )


def run_pass(place, gathered, embed, weights, readout):
    blocks, unused, lanes = gathered.shape
    lat_dim, width = embed.shape
    head_dim = weights.shape[1] // 3
    key_rows = blocks * lanes
    query_rows = key_rows // 4
    bf16, f32 = jnp.bfloat16, jnp.float32
    vmem = pl.BlockSpec(memory_space=pltpu.VMEM)
    return pl.pallas_call(
        pass_kernel,
        out_shape=jax.ShapeDtypeStruct((blocks, lanes // 8, lanes), bf16),
        in_specs=[pl.BlockSpec(memory_space=pltpu.SMEM)] + [vmem] * 6,
        out_specs=vmem,
        scratch_shapes=[
            pltpu.VMEM((8, width), f32),
            pltpu.VMEM((2 * lat_dim + 16, width), bf16),
            pltpu.VMEM((2 * lat_dim, key_rows), bf16),
            pltpu.VMEM((8, key_rows), f32),
            pltpu.VMEM((2 * lat_dim, query_rows), bf16),
            pltpu.VMEM((8, query_rows), f32),
            pltpu.VMEM((query_rows, head_dim), bf16),
            pltpu.VMEM((head_dim, key_rows), bf16),
            pltpu.VMEM((key_rows, 2 * head_dim), bf16),
            pltpu.VMEM((blocks, lanes // 4, head_dim), bf16),
        ],
        compiler_params=pltpu.CompilerParams(vmem_limit_bytes=32 * 1024 * 1024),
    )(place, gathered, embed, weights, readout, *rotation_tables(head_dim))


def body(
    gen_hidden,
    out_weight,
    noise,
    step_index,
    token_order,
    time_weight,
    embed_weight,
    qkv_weight,
    readout_weight,
):
    seq_count = lax.axis_size("seq")
    mp_count = lax.axis_size("mp")
    role_count = lax.axis_size("role")
    mp_index = lax.axis_index("mp")
    local_rows = gen_hidden.shape[0]
    packed_rows = local_rows // 2
    lat_dim = out_weight.shape[1]
    lanes = 2 * lat_dim
    mod_width = time_weight.shape[3]
    bf16, f32 = jnp.bfloat16, jnp.float32
    timestep = step_index[0].astype(f32)
    noise_level = timestep / T_STEPS

    half_freq = FREQ // 2
    frequencies = jnp.exp(-math.log(ROPE_BASE) * jnp.arange(half_freq, dtype=f32) / half_freq)
    phases = timestep * frequencies
    activated = jax.nn.silu(jnp.concatenate([jnp.cos(phases), jnp.sin(phases)]))
    modulation_part = jnp.sum(activated[:, None, None] * time_weight[0], axis=0)

    hidden_wide = gen_hidden.astype(f32)
    mod_row = jnp.pad(modulation_part.reshape(1, 2 * mod_width), ((0, 0), (0, lanes - 2 * mod_width)))
    first = jnp.concatenate(
        [
            pack(dot32(gen_hidden, out_weight)),
            jnp.sum(hidden_wide * hidden_wide, axis=1)[None],
            mod_row,
            jnp.zeros((6, lanes), f32),
        ]
    )
    first = to_all(first, "mp", mp_count)
    projected = unpack(jnp.sum(first[:, :packed_rows], axis=0))
    squares = jnp.sum(first[:, packed_rows], axis=0)
    root_mean = jnp.sqrt(squares / D + EPS_NORM)
    latent = projected / root_mean[:, None]
    noisy = ((1.0 - noise_level) * latent + noise_level * noise.astype(f32)).astype(bf16)

    piece = mp_count * mod_width
    mod_mine = first[:, packed_rows + 1, : 2 * mod_width].reshape(mp_count, 2, mod_width)
    mod_mine = mod_mine.transpose(1, 0, 2).reshape(2, piece)
    mod_mine = jnp.pad(mod_mine, ((0, 0), (0, 2 * lanes - piece))).reshape(4, lanes)
    order = jnp.stack([token_order // 64, token_order % 64]).astype(bf16)
    second = jnp.concatenate([noisy.T, order, *split(mod_mine), jnp.zeros((6, lanes), bf16)])
    second = to_all(second, "seq", seq_count)

    scores = run_pass(
        mp_index.astype(jnp.int32)[None], second, embed_weight[0], qkv_weight[0, 0], readout_weight[0, 0]
    )

    score = jnp.sum(exchange(scores, "seq").astype(f32), axis=0)

    score = to_all(score, ("role", "mp"), role_count * mp_count)
    score = score.reshape(role_count, mp_count, local_rows // (2 * mp_count), 2, lat_dim)
    score = score.transpose(0, 1, 3, 2, 4).reshape(role_count, local_rows, lat_dim)
    realistic = GUIDANCE * score[1] + (1.0 - GUIDANCE) * score[2]
    difference = score[3] - realistic
    magnitude = jnp.sum(jnp.abs(latent - (noisy.astype(f32) - noise_level * realistic)))

    both = jnp.concatenate(split(difference / root_mean[:, None]), axis=1)
    weight_part = lax.dot_general(
        gen_hidden, both, (((0,), (0,)), ((), ())), preferred_element_type=f32
    )
    weight_part = pack(weight_part[:, :lat_dim] + weight_part[:, lat_dim:])
    share = weight_part.shape[0] // seq_count
    pieces = []
    rest = magnitude
    for unused in range(3):
        part = rest.astype(bf16)
        rest = rest - part.astype(f32)
        pieces.append(part)
    extra = jnp.pad(jnp.stack(pieces)[None], ((0, 0), (0, lanes - 3)))
    padding = -(share + 1) % 16
    third = jnp.concatenate(
        [
            weight_part.astype(bf16).reshape(seq_count, share, lanes),
            jnp.broadcast_to(extra[None], (seq_count, 1, lanes)),
            jnp.zeros((seq_count, padding, lanes), bf16),
        ],
        axis=1,
    )
    third = jnp.sum(exchange(third, "seq").astype(f32), axis=0)
    cell_count = local_rows * seq_count * lat_dim
    spread = jnp.sum(third[share]) / cell_count + EPS_MEAN
    factor = -noise_level / spread
    fourth = (third * (factor / math.sqrt(local_rows * seq_count))).astype(bf16)
    fourth = to_all(fourth, "seq", seq_count)
    weight_grad = unpack(fourth[:, :share].reshape(seq_count * share, lanes).astype(f32))

    backward = lax.dot_general(
        both,
        jnp.concatenate([out_weight, out_weight], axis=1),
        (((1,), (1,)), ((), ())),
        preferred_element_type=f32,
    )
    row_terms = jnp.sum(difference * projected, axis=1)
    cubed = root_mean * root_mean * root_mean
    hidden_grad = (
        factor * (backward - hidden_wide * (row_terms / (D * cubed))[:, None])
    ).astype(bf16)
    return (hidden_grad, weight_grad)


def solution(mesh):
    placed = (
        P("seq", "mp"),
        P("mp", None),
        P("seq", None),
        P(),
        P("seq"),
        P("role", None, None, ("seq", "mp")),
        P("role", None, None),
        P("role", "seq", None, None),
        P("role", "seq", None, None),
    )
    return jax.shard_map(
        body, mesh=mesh, in_specs=placed, out_specs=(P("seq", "mp"), P("mp", None)), check_vma=False
    )
```

time: 178 us -> 145 us (0.81)
  other arithmetic: 23.8 us -> 5.7 us
  local copies, waits for them, and re-layouts: 23.4 us -> 9.62 us
  matrix products: 8.39 us -> 2.59 us
  Pallas kernels: 6.8 us -> 12.1 us
    another operation x4 -> x2, other arithmetic: 9.2 us -> 0.71 us  [the longest x1 0.68 us: body(): order = jnp.stack([token_order // 64, token_order % 64]).astype(bf16)]
    unnamed x24 -> x17, local copies, waits for them, and re-layouts: 10.4 us -> 4.02 us
    dot_general x4 -> x1, matrix products: 6.69 us -> 1.22 us  [dot32(): return jnp.dot(left, right, preferred_element_type=jnp.float32)]
    pallas_call x1, Pallas kernels: 6.8 us -> 12.1 us  [run_pass(): pl.pallas_call(pass_kernel, out_shape=jax.ShapeDtypeStruct((blocks, lanes...]
    slice x5 -> x0, local copies, waits for them, and re-layouts: 3.59 us -> none  [the longest x1 3.07 us: project(): return product[:, :3 * head_dim] * lax.rsqrt(mean + EPS_NORM) + offset[None]]
    add x6 -> x0, other arithmetic: 3.48 us -> none  [the longest x1 3.21 us: project(): return product[:, :3 * head_dim] * lax.rsqrt(mean + EPS_NORM) + offset[None]]
    mul x3 -> x0, other arithmetic: 3.4 us -> none  [the longest x2 2.79 us: normalize_rope(): vectors * lax.rsqrt(jnp.mean(vectors * vectors, axis=1, keepdims=True) +...]
    cos x1 -> x0, local copies, waits for them, and re-layouts: 2.67 us -> none  [turn(): return (jnp.cos(angles), jnp.sin(angles))]
where the time goes in v2:
time: 145 us
  waiting for transfers between devices  62.9 us (43%)
  starting transfers between devices  33.4 us (23%)
  blocking collectives  14.7 us (10%)
  Pallas kernels  12.1 us (8%)
  local copies, waits for them, and re-layouts  9.62 us (7%)
  other arithmetic  5.7 us (4%)
  between operations  3.67 us (3%)
  matrix products  2.59 us (2%)
    all_to_all x5, waiting for transfers between devices, exchange(): return lax.all_to_all(chunks, axes, 0, 0, tiled=True)  62.9 us
    all_to_all x5, starting transfers between devices, exchange(): return lax.all_to_all(chunks, axes, 0, 0, tiled=True)  33.4 us
    all_to_all x1, blocking collectives, exchange(): return lax.all_to_all(chunks, axes, 0, 0, tiled=True)  14.7 us
    pallas_call x1, Pallas kernels, run_pass(): pl.pallas_call(pass_kernel, out_shape=jax.ShapeDtypeStruct((blocks, lanes...  12.1 us
    unnamed x17, local copies, waits for them, and re-layouts  4.02 us
    broadcast_in_dim x4, local copies, waits for them, and re-layouts, to_all(): return exchange(jnp.broadcast_to(chunk[None], (count, *chunk.shape)), axes)  3.02 us
  transfers between devices with their start and end apart: 5, of which 5 were waited for; matrix products, arithmetic and copies ran while one was open for 2% of the time, Pallas kernels for 0%

profile of v2, /device:TPU:8, one launch (start us, length us, event | category | flops | bytes accessed | tf_op | source)
XLA Modules:
  0.0 144.7 jit_solution(8598371136455221740)
XLA Ops:
  1.5 1.0 fusion.7
  2.6 1.1 fusion.2
  3.7 1.2 fusion.28
  5.4 0.7 broadcast_in_dim.27
  6.1 10.3 %all-to-all-start = ((f32[4,72,128]{2,1,0:T(8,128)}), f32[4,72,128]{2,1,0:T(8,128)S(1)}, u32[]{:S(2)}, u32[]{:S(2)}) async-start(f32[4,72,128]{2,1,0:T(8,128)} %broadcast_in_dim.27), calls=%async_computation | async-start | bytes 294912 | tf_op jit(solution)/shard_map/all_to_all | solution.py:39
  16.4 0.8 copy.69
  18.1 8.5 %all-to-all-done = f32[4,72,128]{2,1,0:T(8,128)S(1)} async-done(((f32[4,72,128]{2,1,0:T(8,128)}), f32[4,72,128]{2,1,0:T(8,128)S(1)}, u32[]{:S(2)}, u32[]{:S(2)}) %all-to-all-start) | async-done | bytes 147488 | tf_op jit(solution)/shard_map/all_to_all | solution.py:39
  27.7 0.9 broadcast_in_dim.29
  28.6 9.4 %all-to-all-start.1 = ((bf16[32,80,128]{2,1,0:T(8,128)(2,1)}), bf16[32,80,128]{2,1,0:T(8,128)(2,1)S(1)}, u32[]{:S(2)}, u32[]{:S(2)}) async-start(bf16[32,80,128]{2,1,0:T(8,128)(2,1)} %broadcast_in_dim.29), calls=%async_computation.1 | async-start | bytes 1310720 | tf_op jit(solution)/shard_map/all_to_all | solution.py:39
  38.2 20.3 %all-to-all-done.1.gathered_ref = bf16[32,80,128]{2,1,0:T(8,128)(2,1)S(1)} async-done(((bf16[32,80,128]{2,1,0:T(8,128)(2,1)}), bf16[32,80,128]{2,1,0:T(8,128)(2,1)S(1)}, u32[]{:S(2)}, u32[]{:S(2)}) %all-to-all-start.1) | async-done | bytes 655392 | tf_op jit(solution)/shard_map/all_to_all | solution.py:39
  58.5 2.1 %copy-done = bf16[1,1,5120,384]{3,2,1,0:T(8,128)(2,1)S(1)} copy-done((bf16[1,1,5120,384]{3,2,1,0:T(8,128)(2,1)S(1)}, bf16[1,1,5120,384]{3,2,1,0:T(8,128)(2,1)}, u32[]{:S(2)}) %copy-start) | copy-done | bytes 3932184
  60.6 12.1 %shard_map.122 = bf16[32,16,128]{2,1,0:T(8,128)(2,1)S(1)} custom-call(s32[1]{0:T(128)} %bitcast.1.place_ref, bf16[32,80,128]{2,1,0:T(8,128)(2,1)S(1)} %all-to-all-done.1.gathered_ref, bf16[64,5120]{1,0:T(8,128)(2,1)S(1)} %bitcast.50, bf16[5120,384]{1,0:T(8,128)(2,1)S(1)} %bitcast.49, bf16[128,64]{1,0:T(8,128)(2,1)S(1)} %bitcast.51, f32[64,128]{1,0:T(8,128)S(1)} %copy-done.2, ...), custom_call_target="tpu_custom_call" | custom-call | tf_op jit(solution)/shard_map/pallas_call | solution.py:232
  72.7 14.7 %all_to_all.30 = bf16[32,16,128]{2,1,0:T(8,128)(2,1)S(1)} all-to-all(bf16[32,16,128]{2,1,0:T(8,128)(2,1)S(1)} %shard_map.122), channel_id=1, replica_groups=mesh['role'=4,'seq'=32,'mp'=4] {'seq'}, dimensions={0} | all-to-all | bytes 262144 | tf_op jit(solution)/shard_map/all_to_all | solution.py:39
  88.0 4.4 %all-to-all-start.3 = ((f32[16,16,128]{2,1,0:T(8,128)}), f32[16,16,128]{2,1,0:T(8,128)S(1)}, u32[]{:S(2)}, u32[]{:S(2)}) async-start(f32[16,16,128]{2,1,0:T(8,128)} %broadcast_in_dim.60), calls=%async_computation.3 | async-start | bytes 262144 | tf_op jit(solution)/shard_map/all_to_all | solution.py:39
  92.6 10.5 %all-to-all-done.3 = f32[16,16,128]{2,1,0:T(8,128)S(1)} async-done(((f32[16,16,128]{2,1,0:T(8,128)}), f32[16,16,128]{2,1,0:T(8,128)S(1)}, u32[]{:S(2)}, u32[]{:S(2)}) %all-to-all-start.3) | async-done | bytes 131104 | tf_op jit(solution)/shard_map/all_to_all | solution.py:39
  103.4 0.7 fusion.15
  106.4 0.9 maximum_maximum_fusion
  107.3 5.0 %all-to-all-start.4 = ((bf16[32,32,128]{2,1,0:T(8,128)(2,1)}), bf16[32,32,128]{2,1,0:T(8,128)(2,1)S(1)}, u32[]{:S(2)}, u32[]{:S(2)}) async-start(bf16[32,32,128]{2,1,0:T(8,128)(2,1)} %maximum_maximum_fusion), calls=%async_computation.4 | async-start | bytes 524288 | tf_op jit(solution)/shard_map/all_to_all | solution.py:39
  112.4 12.5 %all-to-all-done.4 = bf16[32,32,128]{2,1,0:T(8,128)(2,1)S(1)} async-done(((bf16[32,32,128]{2,1,0:T(8,128)(2,1)}), bf16[32,32,128]{2,1,0:T(8,128)(2,1)S(1)}, u32[]{:S(2)}, u32[]{:S(2)}) %all-to-all-start.4) | async-done | bytes 262176 | tf_op jit(solution)/shard_map/all_to_all | solution.py:39
  126.2 0.7 broadcast_in_dim.65
  127.0 4.3 %all-to-all-start.5 = ((bf16[32,32,128]{2,1,0:T(8,128)(2,1)}), bf16[32,32,128]{2,1,0:T(8,128)(2,1)S(1)}, u32[]{:S(2)}, u32[]{:S(2)}) async-start(bf16[32,32,128]{2,1,0:T(8,128)(2,1)} %broadcast_in_dim.65), calls=%async_computation.5 | async-start | bytes 524288 | tf_op jit(solution)/shard_map/all_to_all | solution.py:39
  131.4 1.0 fusion.1
  132.4 11.1 %all-to-all-done.5 = bf16[32,32,128]{2,1,0:T(8,128)(2,1)S(1)} async-done(((bf16[32,32,128]{2,1,0:T(8,128)(2,1)}), bf16[32,32,128]{2,1,0:T(8,128)(2,1)S(1)}, u32[]{:S(2)}, u32[]{:S(2)}) %all-to-all-start.5) | async-done | bytes 262176 | tf_op jit(solution)/shard_map/all_to_all | solution.py:39
  143.7 0.9 copy.82
  (69 shorter events, 5.7 us)
Async XLA Ops:
  0.6 57.8 %copy-start.2 = (f32[64,128]{1,0:T(8,128)S(1)}, f32[64,128]{1,0:T(8,128)}, u32[]{:S(2)}) copy-start(f32[64,128]{1,0:T(8,128)} %constant.75.clone.high_ref) | copy-start | bytes 98308
  0.6 57.8 %copy-start.3 = (f32[64,128]{1,0:T(8,128)S(1)}, f32[64,128]{1,0:T(8,128)}, u32[]{:S(2)}) copy-start(f32[64,128]{1,0:T(8,128)} %constant.76.clone.low_ref) | copy-start | bytes 98308
  0.7 37.4 %copy-start.6 = (bf16[1,1,128,64]{2,3,1,0:T(8,128)(2,1)S(1)}, bf16[1,1,128,64]{2,3,1,0:T(8,128)(2,1)}, u32[]{:S(2)}) copy-start(bf16[1,1,128,64]{2,3,1,0:T(8,128)(2,1)} %param.19) | copy-start | bytes 49156
  0.7 57.8 %copy-start.1 = (bf16[1,64,5120]{2,1,0:T(8,128)(2,1)S(1)}, bf16[1,64,5120]{2,1,0:T(8,128)(2,1)}, u32[]{:S(2)}) copy-start(bf16[1,64,5120]{2,1,0:T(8,128)(2,1)} %param.17) | copy-start | bytes 1966084
  6.1 20.6 %all-to-all-start = ((f32[4,72,128]{2,1,0:T(8,128)}), f32[4,72,128]{2,1,0:T(8,128)S(1)}, u32[]{:S(2)}, u32[]{:S(2)}) async-start(f32[4,72,128]{2,1,0:T(8,128)} %broadcast_in_dim.27), calls=%async_computation | async-start | bytes 294912 | tf_op jit(solution)/shard_map/all_to_all | solution.py:39
  28.6 29.9 %all-to-all-start.1 = ((bf16[32,80,128]{2,1,0:T(8,128)(2,1)}), bf16[32,80,128]{2,1,0:T(8,128)(2,1)S(1)}, u32[]{:S(2)}, u32[]{:S(2)}) async-start(bf16[32,80,128]{2,1,0:T(8,128)(2,1)} %broadcast_in_dim.29), calls=%async_computation.1 | async-start | bytes 1310720 | tf_op jit(solution)/shard_map/all_to_all | solution.py:39
  58.5 2.1 %copy-start = (bf16[1,1,5120,384]{3,2,1,0:T(8,128)(2,1)S(1)}, bf16[1,1,5120,384]{3,2,1,0:T(8,128)(2,1)}, u32[]{:S(2)}) copy-start(bf16[1,1,5120,384]{3,2,1,0:T(8,128)(2,1)} %param.18) | copy-start | bytes 11796484
  60.6 43.6 %copy-start.4 = (bf16[128,1280]{1,0:T(8,128)(2,1)S(1)}, bf16[128,1280]{1,0:T(8,128)(2,1)}, u32[]{:S(2)}) copy-start(bf16[128,1280]{1,0:T(8,128)(2,1)} %param.11) | copy-start | bytes 983044
  87.3 44.0 %copy-start.5 = (bf16[1280,64]{0,1:T(8,128)(2,1)S(1)}, bf16[1280,64]{0,1:T(8,128)(2,1)}, u32[]{:S(2)}) copy-start(bf16[1280,64]{0,1:T(8,128)(2,1)} %param.12) | copy-start | bytes 491524
  88.0 15.1 %all-to-all-start.3 = ((f32[16,16,128]{2,1,0:T(8,128)}), f32[16,16,128]{2,1,0:T(8,128)S(1)}, u32[]{:S(2)}, u32[]{:S(2)}) async-start(f32[16,16,128]{2,1,0:T(8,128)} %broadcast_in_dim.60), calls=%async_computation.3 | async-start | bytes 262144 | tf_op jit(solution)/shard_map/all_to_all | solution.py:39
  107.3 17.6 %all-to-all-start.4 = ((bf16[32,32,128]{2,1,0:T(8,128)(2,1)}), bf16[32,32,128]{2,1,0:T(8,128)(2,1)S(1)}, u32[]{:S(2)}, u32[]{:S(2)}) async-start(bf16[32,32,128]{2,1,0:T(8,128)(2,1)} %maximum_maximum_fusion), calls=%async_computation.4 | async-start | bytes 524288 | tf_op jit(solution)/shard_map/all_to_all | solution.py:39
  127.0 16.5 %all-to-all-start.5 = ((bf16[32,32,128]{2,1,0:T(8,128)(2,1)}), bf16[32,32,128]{2,1,0:T(8,128)(2,1)S(1)}, u32[]{:S(2)}, u32[]{:S(2)}) async-start(bf16[32,32,128]{2,1,0:T(8,128)(2,1)} %broadcast_in_dim.65), calls=%async_computation.5 | async-start | bytes 524288 | tf_op jit(solution)/shard_map/all_to_all | solution.py:39

commit v3 on v2

--- a/solution.py
+++ b/solution.py
@@ -1,3 +1,4 @@
+import functools
 import math
 
 import jax
@@ -20,16 +21,6 @@
 SHARPNESS = 4.0
 
 
-def pack(block):
-    count = block.shape[0] // 2
-    return jnp.concatenate([block[:count], block[count:]], axis=1)
-
-
-def unpack(block):
-    width = block.shape[1] // 2
-    return jnp.concatenate([block[:, :width], block[:, width:]], axis=0)
-
-
 def split(values):
     high = values.astype(jnp.bfloat16)
     return high, (values - high.astype(jnp.float32)).astype(jnp.bfloat16)
@@ -39,12 +30,14 @@
     return lax.all_to_all(chunks, axes, 0, 0, tiled=True)
 
 
-def to_all(chunk, axes, count):
-    return exchange(jnp.broadcast_to(chunk[None], (count, *chunk.shape)), axes)
-
-
 def dot32(left, right):
     return jnp.dot(left, right, preferred_element_type=jnp.float32)
+
+
+def dot_rows(left, right):
+    return lax.dot_general(
+        left, right, (((1,), (1,)), ((), ())), preferred_element_type=jnp.float32
+    )
 
 
 def rotation_tables(head_dim):
@@ -106,8 +99,12 @@
     key,
     wide,
     attended,
+    weights,
+    weights_in,
 ):
     f32 = jnp.float32
+    fetch = pltpu.make_async_copy(weight_ref, weights, weights_in)
+    fetch.start()
     blocks, used, lanes = gathered_ref.shape
     lat_dim, width = embed_ref.shape
     head_dim = weight_ref.shape[1] // 3
@@ -155,10 +152,9 @@
         shifted_high = shifted.astype(jnp.bfloat16).astype(f32)
         shifted = jnp.where(row == 0, shifted_high, shifted - shifted_high)
         scaled[2 * lat_dim :, at] = jnp.where(row < 2, shifted, 0.0).astype(jnp.bfloat16)
-    folded = dot32(scaled[...], weight_ref[...])
-    gram = lax.dot_general(
-        embed_ref[...], embed_ref[...], (((1,), (1,)), ((), ())), preferred_element_type=f32
-    )
+    gram = dot_rows(embed_ref[...], embed_ref[...])
+    fetch.wait()
+    folded = dot32(scaled[...], weights[...])
     matrix = folded[:lat_dim] + folded[lat_dim : 2 * lat_dim]
     offset = folded[2 * lat_dim : 2 * lat_dim + 1] + folded[2 * lat_dim + 1 : 2 * lat_dim + 2]
     turned = jnp.concatenate(
@@ -202,8 +198,8 @@
         total = jnp.zeros((rows, 2 * head_dim), f32)
         for begin in range(0, key_rows, step):
             scores = dot32(queries, key[:, begin : begin + step])
-            weights = jnp.exp2(scores * factor).astype(jnp.bfloat16)
-            total = total + dot32(weights, wide[begin : begin + step, :])
+            exponents = jnp.exp2(scores * factor).astype(jnp.bfloat16)
+            total = total + dot32(exponents, wide[begin : begin + step, :])
         result = (total[:, :head_dim] / total[:, head_dim:]).astype(jnp.bfloat16)
         attended[pl.ds(index * (rows // quarter), rows // quarter)] = result.reshape(
             rows // quarter, quarter, head_dim
@@ -213,7 +209,7 @@
     lax.fori_loop(0, query_rows // rows, attend, 0)
     half = quarter // 2
     halves = [
-        dot32(attended[:, begin : begin + half, :].reshape(blocks * half, head_dim), readout_ref[...])
+        dot_rows(attended[:, begin : begin + half, :].reshape(blocks * half, head_dim), readout_ref[...])
         for begin in (0, half)
     ]
     score_ref[...] = (
@@ -232,7 +228,15 @@
     return pl.pallas_call(
         pass_kernel,
         out_shape=jax.ShapeDtypeStruct((blocks, lanes // 8, lanes), bf16),
-        in_specs=[pl.BlockSpec(memory_space=pltpu.SMEM)] + [vmem] * 6,
+        in_specs=[
+            pl.BlockSpec(memory_space=pltpu.SMEM),
+            vmem,
+            vmem,
+            pl.BlockSpec(memory_space=pl.ANY),
+            vmem,
+            vmem,
+            vmem,
+        ],
         out_specs=vmem,
         scratch_shapes=[
             pltpu.VMEM((8, width), f32),
@@ -245,9 +249,176 @@
             pltpu.VMEM((head_dim, key_rows), bf16),
             pltpu.VMEM((key_rows, 2 * head_dim), bf16),
             pltpu.VMEM((blocks, lanes // 4, head_dim), bf16),
+            pltpu.VMEM(weights.shape, bf16),
+            pltpu.SemaphoreType.DMA,
         ],
         compiler_params=pltpu.CompilerParams(vmem_limit_bytes=32 * 1024 * 1024),
     )(place, gathered, embed, weights, readout, *rotation_tables(head_dim))
+
+
+def call(kernel, outputs, *operands, scalars=0, scratch=()):
+    vmem = pl.BlockSpec(memory_space=pltpu.VMEM)
+    smem = pl.BlockSpec(memory_space=pltpu.SMEM)
+    return pl.pallas_call(
+        kernel,
+        out_shape=[jax.ShapeDtypeStruct(*output) for output in outputs],
+        in_specs=[smem] * scalars + [vmem] * (len(operands) - scalars),
+        out_specs=[vmem] * len(outputs),
+        scratch_shapes=scratch,
+        compiler_params=pltpu.CompilerParams(vmem_limit_bytes=16 * 1024 * 1024),
+    )(*operands)
+
+
+def start_kernel(hidden_ref, out_ref, active_ref, time_ref, first_ref):
+    hidden = hidden_ref[...]
+    lat_dim = out_ref.shape[0]
+    partial = dot_rows(out_ref[...], hidden)
+    wide = hidden.astype(jnp.float32)
+    ones = jnp.ones((8, hidden.shape[1]), jnp.bfloat16)
+    high, low = split(wide * wide)
+    squares = dot_rows(ones, high) + dot_rows(ones, low)
+    modulation = lax.dot_general(
+        jnp.broadcast_to(active_ref[...], (8, active_ref.shape[1])),
+        time_ref[...],
+        (((1,), (1,)), ((), ())),
+        precision=lax.Precision.HIGHEST,
+        preferred_element_type=jnp.float32,
+    )
+    lanes = hidden.shape[0]
+    modulation = jnp.concatenate(
+        [modulation, jnp.zeros((8, lanes - modulation.shape[1]), jnp.float32)], axis=1
+    )
+    row = lax.broadcasted_iota(jnp.int32, (8, lanes), 0)
+    extra = jnp.where(row == 0, squares, modulation)
+    for peer in range(first_ref.shape[0]):
+        first_ref[peer, :lat_dim, :] = partial
+        first_ref[peer, lat_dim:, :] = extra
+
+
+def noise_kernel(level_ref, first_ref, noise_ref, order_ref, second_ref, kept_ref, pair, extra):
+    f32 = jnp.float32
+    level = level_ref[0]
+    peers, used, lanes = first_ref.shape
+    lat_dim = noise_ref.shape[0]
+    mod_width = 40
+    total = first_ref[0]
+    for peer in range(1, peers):
+        total = total + first_ref[peer]
+    projected = total[:lat_dim]
+    root_mean = jnp.sqrt(total[lat_dim : lat_dim + 1] / D + EPS_NORM)
+    latent = projected / root_mean
+    noisy = ((1.0 - level) * latent + level * noise_ref[...].astype(f32)).astype(jnp.bfloat16)
+    kept_ref[:lat_dim, :] = projected
+    kept_ref[lat_dim : 2 * lat_dim, :] = latent - noisy.astype(f32)
+    kept_ref[2 * lat_dim :, :] = jnp.broadcast_to(root_mean, (8, lanes))
+    pair[...] = jnp.zeros_like(pair)
+    for peer in range(peers):
+        at = slice(peer * mod_width, (peer + 1) * mod_width)
+        row = first_ref[peer, lat_dim : lat_dim + 8, :]
+        pair[0:1, at] = row[1:2, :mod_width]
+        pair[1:2, at] = row[1:2, mod_width : 2 * mod_width]
+    order = order_ref[...]
+    extra[...] = jnp.zeros_like(extra)
+    extra[0:1, :] = (order // 64).astype(f32)
+    extra[1:2, :] = (order % 64).astype(f32)
+    for index in range(2):
+        for half in range(2):
+            part = pair[index : index + 1, half * lanes : (half + 1) * lanes]
+            high = part.astype(jnp.bfloat16).astype(f32)
+            at = 2 + 2 * index + half
+            extra[at : at + 1, :] = high
+            extra[at + 4 : at + 5, :] = part - high
+    rows = jnp.concatenate([noisy, extra[...].astype(jnp.bfloat16)], axis=0)
+    for peer in range(second_ref.shape[0]):
+        second_ref[peer] = rows
+
+
+def heads_kernel(scores_ref, score_ref):
+    total = jnp.sum(scores_ref[...].astype(jnp.float32), axis=0)
+    for peer in range(score_ref.shape[0]):
+        score_ref[peer] = total
+
+
+def gradient_kernel(level_ref, score_ref, kept_ref, hidden_ref, third_ref, side_ref):
+    f32 = jnp.float32
+    level = level_ref[0]
+    peers, half, lanes = score_ref.shape
+    parts = peers // 4
+    lat_dim = lanes // 2
+    left = lax.broadcasted_iota(jnp.int32, (half, lanes), 1) < lat_dim
+    pieces = []
+    for part in range(parts):
+        realistic = GUIDANCE * score_ref[parts + part] + (1.0 - GUIDANCE) * score_ref[2 * parts + part]
+        difference = score_ref[3 * parts + part] - realistic
+        pieces.append(jnp.where(left, difference, pltpu.roll(realistic, lat_dim, 1)))
+        pieces.append(jnp.where(left, pltpu.roll(difference, lat_dim, 1), realistic))
+    both = jnp.concatenate(pieces, axis=0).T
+    difference = both[:lat_dim]
+    realistic = both[lat_dim:]
+    projected = kept_ref[:lat_dim, :]
+    root_mean = kept_ref[2 * lat_dim : 2 * lat_dim + 1, :]
+    distance = jnp.abs(kept_ref[lat_dim : 2 * lat_dim, :] + level * realistic)
+    magnitude = jnp.sum(jnp.sum(distance, axis=0, keepdims=True), axis=1, keepdims=True)
+    direction = difference / root_mean
+    high, low = split(direction)
+    hidden = hidden_ref[...]
+    weight_part = dot32(high, hidden) + dot32(low, hidden)
+
+    row = lax.broadcasted_iota(jnp.int32, (8, lat_dim), 0)
+    first = magnitude.astype(jnp.bfloat16).astype(f32)
+    second = (magnitude - first).astype(jnp.bfloat16).astype(f32)
+    third = magnitude - first - second
+    extra = jnp.where(row == 0, first, jnp.where(row == 1, second, jnp.where(row == 2, third, 0.0)))
+    groups = third_ref.shape[0] // (lat_dim // 8)
+    width = weight_part.shape[1] // groups
+    for group in range(groups):
+        columns = weight_part[:, group * width : (group + 1) * width]
+        for block in range(lat_dim // 8):
+            third_ref[block * groups + group] = jnp.concatenate(
+                [columns[8 * block : 8 * (block + 1)], extra], axis=1
+            ).astype(jnp.bfloat16)
+
+    coefficient = jnp.sum(difference * projected, axis=0, keepdims=True) / (
+        D * root_mean * root_mean * root_mean
+    )
+    side_ref[...] = jnp.concatenate(
+        [direction, jnp.broadcast_to(coefficient, (lat_dim, lanes))], axis=0
+    ).T
+
+
+def scale_kernel(cells, rows, level_ref, third_ref, fourth_ref, factor_ref):
+    total = jnp.sum(third_ref[...].astype(jnp.float32), axis=0)
+    width = total.shape[1] - 64
+    sums = total[:, width : width + 1]
+    spread = (sums[0:1] + sums[1:2] + sums[2:3]) / cells + EPS_MEAN
+    factor = -level_ref[0] / spread
+    factor_ref[...] = jnp.broadcast_to(factor, factor_ref.shape)
+    scaled = (total * (factor / math.sqrt(rows))).astype(jnp.bfloat16)
+    for peer in range(fourth_ref.shape[0]):
+        fourth_ref[peer] = scaled
+
+
+def weight_kernel(fourth_ref, weight_ref):
+    lat_dim, columns = weight_ref.shape
+    groups = fourth_ref.shape[0] // (lat_dim // 8)
+    width = columns // groups
+    for block in range(lat_dim // 8):
+        parts = [
+            fourth_ref[block * groups + group].astype(jnp.float32)[:, :width]
+            for group in range(groups)
+        ]
+        weight_ref[8 * block : 8 * (block + 1), :] = jnp.concatenate(parts, axis=1)
+
+
+def hidden_kernel(factor_ref, side_ref, hidden_ref, out_ref, grad_ref):
+    lat_dim = out_ref.shape[0]
+    high, low = split(side_ref[:, :lat_dim])
+    backward = dot32(high, out_ref[...]) + dot32(low, out_ref[...])
+    coefficient = side_ref[:, lat_dim : lat_dim + 1]
+    factor = factor_ref[0:1, 0:1]
+    grad_ref[...] = (
+        factor * (backward - hidden_ref[...].astype(jnp.float32) * coefficient)
+    ).astype(jnp.bfloat16)
 
 
 def body(
@@ -265,101 +436,81 @@
     mp_count = lax.axis_size("mp")
     role_count = lax.axis_size("role")
     mp_index = lax.axis_index("mp")
-    local_rows = gen_hidden.shape[0]
-    packed_rows = local_rows // 2
+    local_rows, columns = gen_hidden.shape
     lat_dim = out_weight.shape[1]
-    lanes = 2 * lat_dim
-    mod_width = time_weight.shape[3]
     bf16, f32 = jnp.bfloat16, jnp.float32
     timestep = step_index[0].astype(f32)
-    noise_level = timestep / T_STEPS
+    level = (timestep / T_STEPS)[None]
+    out_turned = out_weight.T
 
     half_freq = FREQ // 2
     frequencies = jnp.exp(-math.log(ROPE_BASE) * jnp.arange(half_freq, dtype=f32) / half_freq)
     phases = timestep * frequencies
     activated = jax.nn.silu(jnp.concatenate([jnp.cos(phases), jnp.sin(phases)]))
-    modulation_part = jnp.sum(activated[:, None, None] * time_weight[0], axis=0)
-
-    hidden_wide = gen_hidden.astype(f32)
-    mod_row = jnp.pad(modulation_part.reshape(1, 2 * mod_width), ((0, 0), (0, lanes - 2 * mod_width)))
-    first = jnp.concatenate(
-        [
-            pack(dot32(gen_hidden, out_weight)),
-            jnp.sum(hidden_wide * hidden_wide, axis=1)[None],
-            mod_row,
-            jnp.zeros((6, lanes), f32),
-        ]
-    )
-    first = to_all(first, "mp", mp_count)
-    projected = unpack(jnp.sum(first[:, :packed_rows], axis=0))
-    squares = jnp.sum(first[:, packed_rows], axis=0)
-    root_mean = jnp.sqrt(squares / D + EPS_NORM)
-    latent = projected / root_mean[:, None]
-    noisy = ((1.0 - noise_level) * latent + noise_level * noise.astype(f32)).astype(bf16)
-
-    piece = mp_count * mod_width
-    mod_mine = first[:, packed_rows + 1, : 2 * mod_width].reshape(mp_count, 2, mod_width)
-    mod_mine = mod_mine.transpose(1, 0, 2).reshape(2, piece)
-    mod_mine = jnp.pad(mod_mine, ((0, 0), (0, 2 * lanes - piece))).reshape(4, lanes)
-    order = jnp.stack([token_order // 64, token_order % 64]).astype(bf16)
-    second = jnp.concatenate([noisy.T, order, *split(mod_mine), jnp.zeros((6, lanes), bf16)])
-    second = to_all(second, "seq", seq_count)
-
+    time_turned = time_weight[0].transpose(1, 2, 0).reshape(-1, FREQ)
+
+    (first,) = call(
+        start_kernel,
+        [((mp_count, lat_dim + 8, local_rows), f32)],
+        gen_hidden,
+        out_turned,
+        activated[None],
+        time_turned,
+    )
+    first = exchange(first, "mp")
+
+    second, kept = call(
+        noise_kernel,
+        [((seq_count, lat_dim + 16, local_rows), bf16), ((2 * lat_dim + 8, local_rows), f32)],
+        level,
+        first,
+        noise.T,
+        token_order[None],
+        scalars=1,
+        scratch=[pltpu.VMEM((8, 2 * local_rows), f32), pltpu.VMEM((16, local_rows), f32)],
+    )
+    second = exchange(second, "seq")
     scores = run_pass(
-        mp_index.astype(jnp.int32)[None], second, embed_weight[0], qkv_weight[0, 0], readout_weight[0, 0]
-    )
-
-    score = jnp.sum(exchange(scores, "seq").astype(f32), axis=0)
-
-    score = to_all(score, ("role", "mp"), role_count * mp_count)
-    score = score.reshape(role_count, mp_count, local_rows // (2 * mp_count), 2, lat_dim)
-    score = score.transpose(0, 1, 3, 2, 4).reshape(role_count, local_rows, lat_dim)
-    realistic = GUIDANCE * score[1] + (1.0 - GUIDANCE) * score[2]
-    difference = score[3] - realistic
-    magnitude = jnp.sum(jnp.abs(latent - (noisy.astype(f32) - noise_level * realistic)))
-
-    both = jnp.concatenate(split(difference / root_mean[:, None]), axis=1)
-    weight_part = lax.dot_general(
-        gen_hidden, both, (((0,), (0,)), ((), ())), preferred_element_type=f32
-    )
-    weight_part = pack(weight_part[:, :lat_dim] + weight_part[:, lat_dim:])
-    share = weight_part.shape[0] // seq_count
-    pieces = []
-    rest = magnitude
-    for unused in range(3):
-        part = rest.astype(bf16)
-        rest = rest - part.astype(f32)
-        pieces.append(part)
-    extra = jnp.pad(jnp.stack(pieces)[None], ((0, 0), (0, lanes - 3)))
-    padding = -(share + 1) % 16
-    third = jnp.concatenate(
-        [
-            weight_part.astype(bf16).reshape(seq_count, share, lanes),
-            jnp.broadcast_to(extra[None], (seq_count, 1, lanes)),
-            jnp.zeros((seq_count, padding, lanes), bf16),
-        ],
-        axis=1,
-    )
-    third = jnp.sum(exchange(third, "seq").astype(f32), axis=0)
-    cell_count = local_rows * seq_count * lat_dim
-    spread = jnp.sum(third[share]) / cell_count + EPS_MEAN
-    factor = -noise_level / spread
-    fourth = (third * (factor / math.sqrt(local_rows * seq_count))).astype(bf16)
-    fourth = to_all(fourth, "seq", seq_count)
-    weight_grad = unpack(fourth[:, :share].reshape(seq_count * share, lanes).astype(f32))
-
-    backward = lax.dot_general(
-        both,
-        jnp.concatenate([out_weight, out_weight], axis=1),
-        (((1,), (1,)), ((), ())),
-        preferred_element_type=f32,
-    )
-    row_terms = jnp.sum(difference * projected, axis=1)
-    cubed = root_mean * root_mean * root_mean
-    hidden_grad = (
-        factor * (backward - hidden_wide * (row_terms / (D * cubed))[:, None])
-    ).astype(bf16)
-    return (hidden_grad, weight_grad)
+        mp_index.astype(jnp.int32)[None],
+        second,
+        embed_weight[0],
+        qkv_weight[0, 0],
+        readout_weight[0, 0].T,
+    )
+
+    scores = exchange(scores, "seq")
+    quarter = local_rows // mp_count
+    peers = role_count * mp_count
+    (score,) = call(heads_kernel, [((peers, quarter // 2, 2 * lat_dim), f32)], scores)
+
+    score = exchange(score, ("role", "mp"))
+
+    width = columns // 4 + lat_dim
+    third, side = call(
+        gradient_kernel,
+        [((seq_count, 8, width), bf16), ((local_rows, 2 * lat_dim), f32)],
+        level,
+        score,
+        kept,
+        gen_hidden,
+        scalars=1,
+    )
+
+    third = exchange(third, "seq")
+    cells = local_rows * seq_count * lat_dim
+    fourth, factor = call(
+        functools.partial(scale_kernel, cells, local_rows * seq_count),
+        [((seq_count, 8, width), bf16), ((8, 128), f32)],
+        level,
+        third,
+        scalars=1,
+    )
+    fourth = exchange(fourth, "seq")
+    (hidden_grad,) = call(
+        hidden_kernel, [((local_rows, columns), bf16)], factor, side, gen_hidden, out_turned
+    )
+    (weight_grad,) = call(weight_kernel, [((lat_dim, columns), f32)], fourth)
+    return (hidden_grad, weight_grad.T)
 
 
 def solution(mesh):

time: 145 us -> 140 us (0.966)
  blocking collectives: 14.7 us -> 45.7 us
  waiting for transfers between devices: 62.9 us -> 40.4 us
  starting transfers between devices: 33.4 us -> 24 us
  Pallas kernels: 12.1 us -> 18.2 us
  other arithmetic: 5.7 us -> 0.06 us
  matrix products: 2.59 us -> 0 us
  between operations: 3.67 us -> 1.35 us
    all_to_all x1 -> x3, blocking collectives: 14.7 us -> 45.7 us  [exchange(): return lax.all_to_all(chunks, axes, 0, 0, tiled=True)]
    all_to_all x5 -> x3, waiting for transfers between devices: 62.9 us -> 40.4 us  [exchange(): return lax.all_to_all(chunks, axes, 0, 0, tiled=True)]
    all_to_all x5 -> x3, starting transfers between devices: 33.4 us -> 24 us  [exchange(): return lax.all_to_all(chunks, axes, 0, 0, tiled=True)]
    unnamed x17 -> x24, local copies, waits for them, and re-layouts: 4.02 us -> 9.59 us
    pallas_call x0 -> x7, Pallas kernels: none -> 5.34 us  [call(): pl.pallas_call(kernel, out_shape=[jax.ShapeDtypeStruct(*output) for outpu...]
    broadcast_in_dim x10 -> x0, local copies, waits for them, and re-layouts: 3.17 us -> none  [the longest x4 3.02 us: to_all(): return exchange(jnp.broadcast_to(chunk[None], (count, *chunk.shape)), axes)]
    reduce_sum x8 -> x0, other arithmetic: 2.94 us -> none  [the longest x1 1.13 us: body(): jnp.sum(hidden_wide * hidden_wide, axis=1)[None]]
    dot_general x3 -> x0, matrix products: 2.59 us -> none  [the longest x1 1.22 us: dot32(): return jnp.dot(left, right, preferred_element_type=jnp.float32)]
  transfers between devices with their start and end apart: 5 -> 3, of which waited for: 5 -> 3; matrix products, arithmetic and copies ran while one was open for 2% -> 0% of each run, Pallas kernels for 0% -> 1%
where the time goes in v3:
time: 140 us; the launch traced here: 139 us
  blocking collectives  45.7 us (33%)
  waiting for transfers between devices  40.4 us (29%)
  starting transfers between devices  24 us (17%)
  Pallas kernels  18.2 us (13%)
  local copies, waits for them, and re-layouts  9.59 us (7%)
    all_to_all x3, blocking collectives, exchange(): return lax.all_to_all(chunks, axes, 0, 0, tiled=True)  45.7 us
    all_to_all x3, waiting for transfers between devices, exchange(): return lax.all_to_all(chunks, axes, 0, 0, tiled=True)  40.4 us
    all_to_all x3, starting transfers between devices, exchange(): return lax.all_to_all(chunks, axes, 0, 0, tiled=True)  24 us
    pallas_call x1, Pallas kernels, run_pass(): pl.pallas_call(pass_kernel, out_shape=jax.ShapeDtypeStruct((blocks, lanes...  12.9 us
    unnamed x24, local copies, waits for them, and re-layouts  9.59 us
    pallas_call x7, Pallas kernels, call(): pl.pallas_call(kernel, out_shape=[jax.ShapeDtypeStruct(*output) for outpu...  5.34 us
  transfers between devices with their start and end apart: 3, of which 3 were waited for; matrix products, arithmetic and copies ran while one was open for 0% of the time, Pallas kernels for 1%

profile of v3, /device:TPU:8, one launch (start us, length us, event | category | flops | bytes accessed | tf_op | source)
XLA Modules:
  0.0 139.3 jit_solution(11722818934630942165)
XLA Ops:
  1.4 1.0 copy-done.1
  2.3 0.9 copy-done.3
  3.2 0.9 copy-done.6
  4.1 1.1 shard_map.122
  5.3 10.3 %all-to-all-start = ((f32[4,72,128]{2,1,0:T(8,128)}), f32[4,72,128]{2,1,0:T(8,128)S(1)}, u32[]{:S(2)}, u32[]{:S(2)}) async-start(f32[4,72,128]{2,1,0:T(8,128)} %shard_map.122), calls=%async_computation | async-start | bytes 294912 | tf_op jit(solution)/shard_map/all_to_all | solution.py:30
  15.6 10.3 %all-to-all-done.first_ref = f32[4,72,128]{2,1,0:T(8,128)S(1)} async-done(((f32[4,72,128]{2,1,0:T(8,128)}), f32[4,72,128]{2,1,0:T(8,128)S(1)}, u32[]{:S(2)}, u32[]{:S(2)}) %all-to-all-start) | async-done | bytes 147488 | tf_op jit(solution)/shard_map/all_to_all | solution.py:30
  25.9 0.7 copy-done.10
  27.2 1.0 shard_map.123
  28.2 9.6 %all-to-all-start.1 = ((bf16[32,80,128]{2,1,0:T(8,128)(2,1)}), bf16[32,80,128]{2,1,0:T(8,128)(2,1)S(1)}, u32[]{:S(2)}, u32[]{:S(2)}) async-start(bf16[32,80,128]{2,1,0:T(8,128)(2,1)} %get-tuple-element.8), calls=%async_computation.1 | async-start | bytes 1310720 | tf_op jit(solution)/shard_map/all_to_all | solution.py:30
  37.8 20.4 %all-to-all-done.1.gathered_ref = bf16[32,80,128]{2,1,0:T(8,128)(2,1)S(1)} async-done(((bf16[32,80,128]{2,1,0:T(8,128)(2,1)}), bf16[32,80,128]{2,1,0:T(8,128)(2,1)S(1)}, u32[]{:S(2)}, u32[]{:S(2)}) %all-to-all-start.1) | async-done | bytes 655392 | tf_op jit(solution)/shard_map/all_to_all | solution.py:30
  58.2 2.1 %copy-done = bf16[1,1,5120,384]{3,2,1,0:T(8,128)(2,1)S(1)} copy-done((bf16[1,1,5120,384]{3,2,1,0:T(8,128)(2,1)S(1)}, bf16[1,1,5120,384]{3,2,1,0:T(8,128)(2,1)}, u32[]{:S(2)}) %copy-start) | copy-done | bytes 3932184
  60.3 1.1 copy-done.5
  61.4 0.8 copy-done.7
  62.1 0.8 copy-done.8
  62.9 0.7 copy-done.9
  63.6 12.9 %shard_map.124 = bf16[32,16,128]{2,1,0:T(8,128)(2,1)S(1)} custom-call(s32[1]{0:T(128)} %bitcast.2.place_ref, bf16[32,80,128]{2,1,0:T(8,128)(2,1)S(1)} %all-to-all-done.1.gathered_ref, bf16[64,5120]{1,0:T(8,128)(2,1)S(1)} %bitcast.24, bf16[5120,384]{1,0:T(8,128)(2,1)S(1)} %bitcast.21, bf16[64,128]{1,0:T(8,128)(2,1)S(1)} %bitcast.26, f32[64,128]{1,0:T(8,128)S(1)} %copy-done.7, ...), custom_call_target="tpu_custom_call" | custom-call | tf_op jit(solution)/shard_map/pallas_call | solution.py:228
  76.5 14.7 %all_to_all.30.scores_ref = bf16[32,16,128]{2,1,0:T(8,128)(2,1)S(1)} all-to-all(bf16[32,16,128]{2,1,0:T(8,128)(2,1)S(1)} %shard_map.124), channel_id=1, replica_groups=mesh['role'=4,'seq'=32,'mp'=4] {'seq'}, dimensions={0} | all-to-all | bytes 262144 | tf_op jit(solution)/shard_map/all_to_all | solution.py:30
  91.2 14.8 %all_to_all.31.score_ref = f32[16,16,128]{2,1,0:T(8,128)S(1)} all-to-all(f32[16,16,128]{2,1,0:T(8,128)S(1)} %shard_map.125), channel_id=1, replica_groups=mesh['role'=4,'seq'=32,'mp'=4] {'role','mp'}, dimensions={0} | all-to-all | bytes 262144 | tf_op jit(solution)/shard_map/all_to_all | solution.py:30
  106.5 16.2 %all_to_all.32.third_ref = bf16[32,8,384]{2,1,0:T(8,128)(2,1)S(1)} all-to-all(bf16[32,8,384]{2,1,0:T(8,128)(2,1)S(1)} %get-tuple-element.10), channel_id=1, replica_groups=mesh['role'=4,'seq'=32,'mp'=4] {'seq'}, dimensions={0} | all-to-all | bytes 393216 | tf_op jit(solution)/shard_map/all_to_all | solution.py:30
  122.7 0.8 shard_map.127
  123.6 4.2 %all-to-all-start.5 = ((bf16[32,8,384]{2,1,0:T(8,128)(2,1)}), bf16[32,8,384]{2,1,0:T(8,128)(2,1)S(1)}, u32[]{:S(2)}, u32[]{:S(2)}) async-start(bf16[32,8,384]{2,1,0:T(8,128)(2,1)} %get-tuple-element.13), calls=%async_computation.5 | async-start | bytes 393216 | tf_op jit(solution)/shard_map/all_to_all | solution.py:30
  127.7 1.0 shard_map.128
  128.8 9.7 %all-to-all-done.5.fourth_ref = bf16[32,8,384]{2,1,0:T(8,128)(2,1)S(1)} async-done(((bf16[32,8,384]{2,1,0:T(8,128)(2,1)}), bf16[32,8,384]{2,1,0:T(8,128)(2,1)S(1)}, u32[]{:S(2)}, u32[]{:S(2)}) %all-to-all-start.5) | async-done | bytes 196640 | tf_op jit(solution)/shard_map/all_to_all | solution.py:30
  138.5 0.8 shard_map.129
  (19 shorter events, 1.3 us)
Async XLA Ops:
  1.3 1.0 copy-start.1
  2.3 0.9 copy-start.3
  3.2 0.9 copy-start.6
  5.3 20.6 %all-to-all-start = ((f32[4,72,128]{2,1,0:T(8,128)}), f32[4,72,128]{2,1,0:T(8,128)S(1)}, u32[]{:S(2)}, u32[]{:S(2)}) async-start(f32[4,72,128]{2,1,0:T(8,128)} %shard_map.122), calls=%async_computation | async-start | bytes 294912 | tf_op jit(solution)/shard_map/all_to_all | solution.py:30
  15.6 90.5 %copy-start.2 = (bf16[128,1280]{1,0:T(8,128)(2,1)S(1)}, bf16[128,1280]{1,0:T(8,128)(2,1)}, u32[]{:S(2)}) copy-start(bf16[128,1280]{1,0:T(8,128)(2,1)} %hidden_ref.5) | copy-start | bytes 983044
  25.9 0.7 copy-start.10
  26.6 0.7 copy-start.11
  28.2 99.5 %copy-start.4 = (bf16[1280,64]{0,1:T(8,128)(2,1)S(1)}, bf16[1280,64]{0,1:T(8,128)(2,1)}, u32[]{:S(2)}) copy-start(bf16[1280,64]{0,1:T(8,128)(2,1)} %param.12) | copy-start | bytes 491524
  28.2 30.0 %all-to-all-start.1 = ((bf16[32,80,128]{2,1,0:T(8,128)(2,1)}), bf16[32,80,128]{2,1,0:T(8,128)(2,1)S(1)}, u32[]{:S(2)}, u32[]{:S(2)}) async-start(bf16[32,80,128]{2,1,0:T(8,128)(2,1)} %get-tuple-element.8), calls=%async_computation.1 | async-start | bytes 1310720 | tf_op jit(solution)/shard_map/all_to_all | solution.py:30
  58.2 2.1 %copy-start = (bf16[1,1,5120,384]{3,2,1,0:T(8,128)(2,1)S(1)}, bf16[1,1,5120,384]{3,2,1,0:T(8,128)(2,1)}, u32[]{:S(2)}) copy-start(bf16[1,1,5120,384]{3,2,1,0:T(8,128)(2,1)} %param.18) | copy-start | bytes 11796484
  60.3 1.1 copy-start.5
  61.4 0.8 copy-start.7
  62.1 0.8 copy-start.8
  62.9 0.7 copy-start.9
  123.6 14.9 %all-to-all-start.5 = ((bf16[32,8,384]{2,1,0:T(8,128)(2,1)}), bf16[32,8,384]{2,1,0:T(8,128)(2,1)S(1)}, u32[]{:S(2)}, u32[]{:S(2)}) async-start(bf16[32,8,384]{2,1,0:T(8,128)(2,1)} %get-tuple-element.13), calls=%async_computation.5 | async-start | bytes 393216 | tf_op jit(solution)/shard_map/all_to_all | solution.py:30

commit v4 on v3

--- a/solution.py
+++ b/solution.py
@@ -19,6 +19,8 @@
 GUIDANCE = 5.0
 ROPE_BASE = 10000.0
 SHARPNESS = 4.0
+VMEM_LIMIT = 61 * 1024 * 1024
+CHUNK = 1024
 
 
 def split(values):
@@ -38,22 +40,30 @@
     return lax.dot_general(
         left, right, (((1,), (1,)), ((), ())), preferred_element_type=jnp.float32
     )
+
+
+def fetch_all(arrived, *pairs):
+    fetches = [
+        pltpu.make_async_copy(source, target, arrived.at[index])
+        for index, (source, target) in enumerate(pairs)
+    ]
+    for fetch in fetches:
+        fetch.start()
+    return fetches
 
 
 def rotation_tables(head_dim):
     turns = ROPE_BASE ** (-2.0 * np.arange(head_dim // 2) / head_dim) / (2.0 * np.pi)
     grain = 2.0 ** (np.floor(np.log2(turns)) - 11)
     high = np.floor(turns / grain) * grain
-    return tuple(
-        np.ascontiguousarray(np.broadcast_to(part[:, None], (head_dim // 2, 128)), np.float32)
-        for part in (high, turns - high)
-    )
-
-
-def rotations(positions, high, low):
-    tiles = positions.shape[1] // high.shape[1]
-    high = jnp.concatenate([high] * tiles, axis=1)
-    low = jnp.concatenate([low] * tiles, axis=1)
+    both = np.concatenate([high, turns - high])
+    return np.ascontiguousarray(np.broadcast_to(both[:, None], (head_dim, 128)), np.float32)
+
+
+def rotations(positions, table):
+    table = jnp.concatenate([table] * (positions.shape[1] // table.shape[1]), axis=1)
+    high = table[: table.shape[0] // 2]
+    low = table[table.shape[0] // 2 :]
     whole = positions * high
     part = (whole - jnp.round(whole)) + positions * low
     angle = (part - jnp.round(part)) * math.pi
@@ -83,11 +93,10 @@
 def pass_kernel(
     place_ref,
     gathered_ref,
-    embed_ref,
-    weight_ref,
-    readout_ref,
-    high_ref,
-    low_ref,
+    embed_in,
+    weight_in,
+    readout_in,
+    table_in,
     score_ref,
     modulation,
     scaled,
@@ -99,12 +108,23 @@
     key,
     wide,
     attended,
-    weights,
-    weights_in,
+    embed_ref,
+    weight_ref,
+    readout_ref,
+    table_ref,
+    arrived,
 ):
     f32 = jnp.float32
-    fetch = pltpu.make_async_copy(weight_ref, weights, weights_in)
-    fetch.start()
+    fetches = fetch_all(
+        arrived,
+        (embed_in, embed_ref),
+        *(
+            (weight_in.at[pl.ds(begin, CHUNK), :], weight_ref.at[pl.ds(begin, CHUNK), :])
+            for begin in range(0, weight_ref.shape[0], CHUNK)
+        ),
+        (table_in, table_ref),
+        (readout_in, readout_ref),
+    )
     blocks, used, lanes = gathered_ref.shape
     lat_dim, width = embed_ref.shape
     head_dim = weight_ref.shape[1] // 3
@@ -117,22 +137,24 @@
 
     for block in range(blocks):
         at = slice(block * lanes, (block + 1) * lanes)
-        clip[:lat_dim, at] = gathered_ref[block, :lat_dim, :]
-        clip[lat_dim:, at] = gathered_ref[block, :lat_dim, :]
-        extra = gathered_ref[block, lat_dim : lat_dim + 16, :].astype(f32)
+        received = gathered_ref[block]
+        clip[:lat_dim, at] = received[:lat_dim]
+        clip[lat_dim:, at] = received[:lat_dim]
+        extra = received[lat_dim:].astype(f32)
         places[0:1, at] = extra[0:1] * 64.0 + extra[1:2]
-        pair = extra[2:6] + extra[6:10]
+        pair = extra[2:4] + extra[4:6]
+        tail = extra[6:7] + pltpu.roll(extra[6:7], lanes // 2, 1)
         begin = block * piece
-        modulation[0:1, begin : begin + lanes] = pair[0:1]
-        modulation[0:1, begin + lanes : begin + piece] = pair[1:2, : piece - lanes]
-        modulation[1:2, begin : begin + lanes] = pair[2:3]
-        modulation[1:2, begin + lanes : begin + piece] = pair[3:4, : piece - lanes]
-
-    lane = lax.broadcasted_iota(jnp.int32, (lat_dim + 16, lanes), 1)
+        rest = piece - lanes
+        modulation[0:2, begin : begin + lanes] = pair
+        modulation[0:1, begin + lanes : begin + piece] = tail[:, :rest]
+        modulation[1:2, begin + lanes : begin + piece] = tail[:, rest : 2 * rest]
+
+    lane = lax.broadcasted_iota(jnp.int32, (used, lanes), 1)
     for tile in range(blocks // per_tile):
-        found = jnp.zeros((lat_dim + 16, lanes), f32)
+        found = jnp.zeros((used, lanes), f32)
         for part in range(per_tile):
-            block = gathered_ref[tile * per_tile + part, : lat_dim + 16, :].astype(f32)
+            block = gathered_ref[tile * per_tile + part].astype(f32)
             shift = lax.rem((part - place + per_tile) * quarter, lanes)
             found = jnp.where(lane // quarter == part, pltpu.roll(block, shift, 1), found)
         at = slice(tile * lanes, (tile + 1) * lanes)
@@ -141,20 +163,21 @@
         own[lat_dim:, at] = rows
         own_places[0:1, at] = found[lat_dim : lat_dim + 1] * 64.0 + found[lat_dim + 1 : lat_dim + 2]
 
-    chunk = width // 5
-    for begin in range(0, width, chunk):
-        at = slice(begin, begin + chunk)
+    fetches[0].wait()
+    folded = jnp.zeros((2 * lat_dim + 16, 3 * head_dim), f32)
+    for begin in range(0, width, CHUNK):
+        at = slice(begin, begin + CHUNK)
         high, low = split(embed_ref[:, at].astype(f32) * (1.0 + modulation[1:2, at]))
         scaled[:lat_dim, at] = high
         scaled[lat_dim : 2 * lat_dim, at] = low
-        row = lax.broadcasted_iota(jnp.int32, (16, chunk), 0)
-        shifted = jnp.broadcast_to(modulation[0:1, at], (16, chunk))
+        row = lax.broadcasted_iota(jnp.int32, (16, CHUNK), 0)
+        shifted = jnp.broadcast_to(modulation[0:1, at], (16, CHUNK))
         shifted_high = shifted.astype(jnp.bfloat16).astype(f32)
         shifted = jnp.where(row == 0, shifted_high, shifted - shifted_high)
         scaled[2 * lat_dim :, at] = jnp.where(row < 2, shifted, 0.0).astype(jnp.bfloat16)
+        fetches[1 + begin // CHUNK].wait()
+        folded = folded + dot32(scaled[:, at], weight_ref[at, :])
     gram = dot_rows(embed_ref[...], embed_ref[...])
-    fetch.wait()
-    folded = dot32(scaled[...], weights[...])
     matrix = folded[:lat_dim] + folded[lat_dim : 2 * lat_dim]
     offset = folded[2 * lat_dim : 2 * lat_dim + 1] + folded[2 * lat_dim + 1 : 2 * lat_dim + 2]
     turned = jnp.concatenate(
@@ -172,24 +195,26 @@
         return product[:count] * lax.rsqrt(mean + EPS_NORM) + offsets
 
     step = 4 * lanes
+    fetches[-2].wait()
+    table = table_ref[...]
     wide[:, head_dim:] = jnp.ones((key_rows, head_dim), jnp.bfloat16)
     for begin in range(0, query_rows, step):
         at = slice(begin, begin + step)
         vectors = project(matrix_parts[:head_dim], offsets[:head_dim], own[:, at])
-        turns = rotations(own_places[0:1, at], high_ref[...], low_ref[...])
+        turns = rotations(own_places[0:1, at], table)
         query[at, :] = normalize_rope(vectors, *turns).T.astype(jnp.bfloat16)
 
     def keys_and_values(index, carry):
         at = pl.ds(pl.multiple_of(index * step, step), step)
         vectors = project(matrix_parts[head_dim:], offsets[head_dim:], clip[:, at])
-        turns = rotations(places[0:1, at], high_ref[...], low_ref[...])
+        turns = rotations(places[0:1, at], table)
         key[:, at] = normalize_rope(vectors[:head_dim], *turns).astype(jnp.bfloat16)
         wide[at, :head_dim] = vectors[head_dim:].T.astype(jnp.bfloat16)
         return carry
 
-    lax.fori_loop(0, key_rows // step, keys_and_values, 0)
-
-    rows = 256
+    lax.fori_loop(0, key_rows // step, keys_and_values, 0, unroll=True)
+
+    rows = 512
     factor = SHARPNESS / math.sqrt(head_dim) * math.log2(math.e)
 
     def attend(index, carry):
@@ -206,8 +231,9 @@
         )
         return carry
 
-    lax.fori_loop(0, query_rows // rows, attend, 0)
+    lax.fori_loop(0, query_rows // rows, attend, 0, unroll=True)
     half = quarter // 2
+    fetches[-1].wait()
     halves = [
         dot_rows(attended[:, begin : begin + half, :].reshape(blocks * half, head_dim), readout_ref[...])
         for begin in (0, half)
@@ -231,12 +257,8 @@
         in_specs=[
             pl.BlockSpec(memory_space=pltpu.SMEM),
             vmem,
-            vmem,
-            pl.BlockSpec(memory_space=pl.ANY),
-            vmem,
-            vmem,
-            vmem,
-        ],
+        ]
+        + [pl.BlockSpec(memory_space=pl.ANY)] * 4,
         out_specs=vmem,
         scratch_shapes=[
             pltpu.VMEM((8, width), f32),
@@ -249,45 +271,62 @@
             pltpu.VMEM((head_dim, key_rows), bf16),
             pltpu.VMEM((key_rows, 2 * head_dim), bf16),
             pltpu.VMEM((blocks, lanes // 4, head_dim), bf16),
+            pltpu.VMEM(embed.shape, bf16),
             pltpu.VMEM(weights.shape, bf16),
-            pltpu.SemaphoreType.DMA,
+            pltpu.VMEM(readout.shape, bf16),
+            pltpu.VMEM((head_dim, 128), f32),
+            pltpu.SemaphoreType.DMA((3 + width // CHUNK,)),
         ],
-        compiler_params=pltpu.CompilerParams(vmem_limit_bytes=32 * 1024 * 1024),
-    )(place, gathered, embed, weights, readout, *rotation_tables(head_dim))
-
-
-def call(kernel, outputs, *operands, scalars=0, scratch=()):
+        compiler_params=pltpu.CompilerParams(vmem_limit_bytes=VMEM_LIMIT),
+    )(place, gathered, embed, weights, readout, jnp.asarray(rotation_tables(head_dim)))
+
+
+def call(kernel, outputs, *operands, scalars=0, fetched=0, scratch=()):
     vmem = pl.BlockSpec(memory_space=pltpu.VMEM)
     smem = pl.BlockSpec(memory_space=pltpu.SMEM)
+    plain = len(operands) - scalars - fetched
+    scratch = list(scratch)
+    if fetched:
+        scratch += [pltpu.VMEM(a.shape, a.dtype) for a in operands[-fetched:]]
+        scratch.append(pltpu.SemaphoreType.DMA((fetched,)))
     return pl.pallas_call(
         kernel,
         out_shape=[jax.ShapeDtypeStruct(*output) for output in outputs],
-        in_specs=[smem] * scalars + [vmem] * (len(operands) - scalars),
+        in_specs=[smem] * scalars + [vmem] * plain + [pl.BlockSpec(memory_space=pl.ANY)] * fetched,
         out_specs=[vmem] * len(outputs),
         scratch_shapes=scratch,
-        compiler_params=pltpu.CompilerParams(vmem_limit_bytes=16 * 1024 * 1024),
+        compiler_params=pltpu.CompilerParams(
+            vmem_limit_bytes=VMEM_LIMIT if fetched else 16 * 1024 * 1024
+        ),
     )(*operands)
 
 
-def start_kernel(hidden_ref, out_ref, active_ref, time_ref, first_ref):
+def start_kernel(
+    active_ref, hidden_in, out_in, time_in, first_ref, hidden_ref, out_ref, time_ref, arrived
+):
+    fetches = fetch_all(arrived, (hidden_in, hidden_ref), (out_in, out_ref), (time_in, time_ref))
+    lanes = hidden_ref.shape[0]
+    lat_dim = out_ref.shape[0]
+    active = jnp.broadcast_to(active_ref[...], (8, active_ref.shape[1]))
+    fetches[2].wait()
+    modulation = lax.dot_general(
+        active,
+        time_ref[...],
+        (((1,), (1,)), ((), ())),
+        precision=lax.Precision.HIGHEST,
+        preferred_element_type=jnp.float32,
+    )
+    modulation = jnp.concatenate(
+        [modulation, jnp.zeros((8, lanes - modulation.shape[1]), jnp.float32)], axis=1
+    )
+    fetches[0].wait()
     hidden = hidden_ref[...]
-    lat_dim = out_ref.shape[0]
-    partial = dot_rows(out_ref[...], hidden)
     wide = hidden.astype(jnp.float32)
     ones = jnp.ones((8, hidden.shape[1]), jnp.bfloat16)
     high, low = split(wide * wide)
     squares = dot_rows(ones, high) + dot_rows(ones, low)
-    modulation = lax.dot_general(
-        jnp.broadcast_to(active_ref[...], (8, active_ref.shape[1])),
-        time_ref[...],
-        (((1,), (1,)), ((), ())),
-        precision=lax.Precision.HIGHEST,
-        preferred_element_type=jnp.float32,
-    )
-    lanes = hidden.shape[0]
-    modulation = jnp.concatenate(
-        [modulation, jnp.zeros((8, lanes - modulation.shape[1]), jnp.float32)], axis=1
-    )
+    fetches[1].wait()
+    partial = dot_rows(out_ref[...], hidden)
     row = lax.broadcasted_iota(jnp.int32, (8, lanes), 0)
     extra = jnp.where(row == 0, squares, modulation)
     for peer in range(first_ref.shape[0]):
@@ -295,7 +334,20 @@
         first_ref[peer, lat_dim:, :] = extra
 
 
-def noise_kernel(level_ref, first_ref, noise_ref, order_ref, second_ref, kept_ref, pair, extra):
+def noise_kernel(
+    level_ref,
+    first_ref,
+    noise_in,
+    order_in,
+    second_ref,
+    kept_ref,
+    pair,
+    extra,
+    noise_ref,
+    order_ref,
+    arrived,
+):
+    fetches = fetch_all(arrived, (noise_in, noise_ref), (order_in, order_ref))
     f32 = jnp.float32
     level = level_ref[0]
     peers, used, lanes = first_ref.shape
@@ -307,9 +359,7 @@
     projected = total[:lat_dim]
     root_mean = jnp.sqrt(total[lat_dim : lat_dim + 1] / D + EPS_NORM)
     latent = projected / root_mean
-    noisy = ((1.0 - level) * latent + level * noise_ref[...].astype(f32)).astype(jnp.bfloat16)
     kept_ref[:lat_dim, :] = projected
-    kept_ref[lat_dim : 2 * lat_dim, :] = latent - noisy.astype(f32)
     kept_ref[2 * lat_dim :, :] = jnp.broadcast_to(root_mean, (8, lanes))
     pair[...] = jnp.zeros_like(pair)
     for peer in range(peers):
@@ -317,17 +367,22 @@
         row = first_ref[peer, lat_dim : lat_dim + 8, :]
         pair[0:1, at] = row[1:2, :mod_width]
         pair[1:2, at] = row[1:2, mod_width : 2 * mod_width]
+    rest = peers * mod_width - lanes
+    head = pair[0:2, :lanes]
+    head_high = head.astype(jnp.bfloat16).astype(f32)
+    tail = jnp.concatenate([pair[0:1, lanes : lanes + rest], pair[1:2, lanes : lanes + rest]], axis=1)
+    tail_high = tail.astype(jnp.bfloat16).astype(f32)
+    extra[2:4, :] = head_high
+    extra[4:6, :] = head - head_high
+    extra[6:7, :] = jnp.concatenate([tail_high, tail - tail_high], axis=1)
+    extra[7:8, :] = jnp.zeros((1, lanes), f32)
+    fetches[1].wait()
     order = order_ref[...]
-    extra[...] = jnp.zeros_like(extra)
     extra[0:1, :] = (order // 64).astype(f32)
     extra[1:2, :] = (order % 64).astype(f32)
-    for index in range(2):
-        for half in range(2):
-            part = pair[index : index + 1, half * lanes : (half + 1) * lanes]
-            high = part.astype(jnp.bfloat16).astype(f32)
-            at = 2 + 2 * index + half
-            extra[at : at + 1, :] = high
-            extra[at + 4 : at + 5, :] = part - high
+    fetches[0].wait()
+    noisy = ((1.0 - level) * latent + level * noise_ref[...].astype(f32)).astype(jnp.bfloat16)
+    kept_ref[lat_dim : 2 * lat_dim, :] = latent - noisy.astype(f32)
     rows = jnp.concatenate([noisy, extra[...].astype(jnp.bfloat16)], axis=0)
     for peer in range(second_ref.shape[0]):
         second_ref[peer] = rows
@@ -452,22 +507,24 @@
     (first,) = call(
         start_kernel,
         [((mp_count, lat_dim + 8, local_rows), f32)],
+        activated[None],
         gen_hidden,
         out_turned,
-        activated[None],
         time_turned,
+        fetched=3,
     )
     first = exchange(first, "mp")
 
     second, kept = call(
         noise_kernel,
-        [((seq_count, lat_dim + 16, local_rows), bf16), ((2 * lat_dim + 8, local_rows), f32)],
+        [((seq_count, lat_dim + 8, local_rows), bf16), ((2 * lat_dim + 8, local_rows), f32)],
         level,
         first,
         noise.T,
         token_order[None],
         scalars=1,
-        scratch=[pltpu.VMEM((8, 2 * local_rows), f32), pltpu.VMEM((16, local_rows), f32)],
+        fetched=2,
+        scratch=[pltpu.VMEM((8, 2 * local_rows), f32), pltpu.VMEM((8, local_rows), f32)],
     )
     second = exchange(second, "seq")
     scores = run_pass(

time: 140 us -> 135 us (0.964)
  local copies, waits for them, and re-layouts: 9.59 us -> 1.5 us
  Pallas kernels: 18.2 us -> 22.1 us
    unnamed x24 -> x10, local copies, waits for them, and re-layouts: 9.59 us -> 1.5 us
    pallas_call x7, Pallas kernels: 5.34 us -> 9.2 us  [call(): pl.pallas_call(kernel, out_shape=[jax.ShapeDtypeStruct(*output) for outpu...]
where the time goes in v4:
time: 135 us
  blocking collectives  45.8 us (34%)
  waiting for transfers between devices  39.1 us (29%)
  starting transfers between devices  24.1 us (18%)
  Pallas kernels  22.1 us (16%)
  local copies, waits for them, and re-layouts  1.5 us (1%)
  between operations  1.37 us (1%)
    all_to_all x3, blocking collectives, exchange(): return lax.all_to_all(chunks, axes, 0, 0, tiled=True)  45.8 us
    all_to_all x3, waiting for transfers between devices, exchange(): return lax.all_to_all(chunks, axes, 0, 0, tiled=True)  39.1 us
    all_to_all x3, starting transfers between devices, exchange(): return lax.all_to_all(chunks, axes, 0, 0, tiled=True)  24.1 us
    pallas_call x1, Pallas kernels, run_pass(): pl.pallas_call(pass_kernel, out_shape=jax.ShapeDtypeStruct((blocks, lanes...  12.9 us
    pallas_call x7, Pallas kernels, call(): pl.pallas_call(kernel, out_shape=[jax.ShapeDtypeStruct(*output) for outpu...  9.2 us
  transfers between devices with their start and end apart: 3, of which 3 were waited for; matrix products, arithmetic and copies ran while one was open for 0% of the time, Pallas kernels for 1%

profile of v4, /device:TPU:8, one launch (start us, length us, event | category | flops | bytes accessed | tf_op | source)
XLA Modules:
  0.0 134.6 jit_solution(699317040026625152)
XLA Ops:
  1.3 0.6 divide_multiply_fusion.active_ref
  1.9 3.4 %shard_map.113 = f32[4,72,128]{2,1,0:T(8,128)} custom-call(f32[1,256]{1,0:T(1,128)} %divide_multiply_fusion.active_ref, bf16[128,1280]{1,0:T(8,128)(2,1)} %hidden_ref.3, bf16[64,1280]{1,0:T(8,128)(2,1)} %bitcast.21, f32[80,256]{1,0:T(8,128)} %bitcast.26), custom_call_target="tpu_custom_call" | custom-call | tf_op jit(solution)/shard_map/pallas_call | solution.py:292
  5.4 0.0 copy-start
  5.4 10.4 %all-to-all-start = ((f32[4,72,128]{2,1,0:T(8,128)}), f32[4,72,128]{2,1,0:T(8,128)S(1)}, u32[]{:S(2)}, u32[]{:S(2)}) async-start(f32[4,72,128]{2,1,0:T(8,128)} %shard_map.113), calls=%async_computation | async-start | bytes 294912 | tf_op jit(solution)/shard_map/all_to_all | solution.py:32
  15.8 10.3 %all-to-all-done.first_ref = f32[4,72,128]{2,1,0:T(8,128)S(1)} async-done(((f32[4,72,128]{2,1,0:T(8,128)}), f32[4,72,128]{2,1,0:T(8,128)S(1)}, u32[]{:S(2)}, u32[]{:S(2)}) %all-to-all-start) | async-done | bytes 147488 | tf_op jit(solution)/shard_map/all_to_all | solution.py:32
  26.1 0.7 copy-done.4
  26.7 2.5 %shard_map.114 = (bf16[32,72,128]{2,1,0:T(8,128)(2,1)}, f32[136,128]{1,0:T(8,128)}) custom-call(f32[1]{0:T(128)} %bitcast.1.level_ref, f32[4,72,128]{2,1,0:T(8,128)} %copy-done.4, bf16[64,128]{1,0:T(8,128)(2,1)} %bitcast.28, s32[1,128]{1,0:T(1,128)} %bitcast.29), custom_call_target="tpu_custom_call" | custom-call | tf_op jit(solution)/shard_map/pallas_call | solution.py:292
  29.3 0.0 copy-start.2
  29.3 9.6 %all-to-all-start.1 = ((bf16[32,72,128]{2,1,0:T(8,128)(2,1)}), bf16[32,72,128]{2,1,0:T(8,128)(2,1)S(1)}, u32[]{:S(2)}, u32[]{:S(2)}) async-start(bf16[32,72,128]{2,1,0:T(8,128)(2,1)} %get-tuple-element.8), calls=%async_computation.1 | async-start | bytes 1179648 | tf_op jit(solution)/shard_map/all_to_all | solution.py:32
  38.9 0.0 copy-start.1
  38.9 19.1 %all-to-all-done.1.gathered_ref = bf16[32,72,128]{2,1,0:T(8,128)(2,1)S(1)} async-done(((bf16[32,72,128]{2,1,0:T(8,128)(2,1)}), bf16[32,72,128]{2,1,0:T(8,128)(2,1)S(1)}, u32[]{:S(2)}, u32[]{:S(2)}) %all-to-all-start.1) | async-done | bytes 589856 | tf_op jit(solution)/shard_map/all_to_all | solution.py:32
  58.0 0.8 copy-done.3
  58.9 12.9 %shard_map.115 = bf16[32,16,128]{2,1,0:T(8,128)(2,1)} custom-call(s32[1]{0:T(128)} %bitcast.2.place_ref, bf16[32,72,128]{2,1,0:T(8,128)(2,1)} %copy-done.3, bf16[64,5120]{1,0:T(8,128)(2,1)} %bitcast.24, bf16[5120,384]{1,0:T(8,128)(2,1)} %bitcast.23, bf16[64,128]{1,0:T(8,128)(2,1)} %bitcast.27, f32[128,128]{1,0:T(8,128)} %constant.17.clone.table_in), custom_call_target="tpu_custom_call" | custom-call | tf_op jit(solution)/shard_map/pallas_call | solution.py:254
  71.7 14.7 %all_to_all.30.scores_ref = bf16[32,16,128]{2,1,0:T(8,128)(2,1)S(1)} all-to-all(bf16[32,16,128]{2,1,0:T(8,128)(2,1)} %shard_map.115), channel_id=1, replica_groups=mesh['role'=4,'seq'=32,'mp'=4] {'seq'}, dimensions={0} | all-to-all | bytes 262144 | tf_op jit(solution)/shard_map/all_to_all | solution.py:32
  86.5 14.8 %all_to_all.31.score_ref = f32[16,16,128]{2,1,0:T(8,128)S(1)} all-to-all(f32[16,16,128]{2,1,0:T(8,128)S(1)} %shard_map.116), channel_id=1, replica_groups=mesh['role'=4,'seq'=32,'mp'=4] {'role','mp'}, dimensions={0} | all-to-all | bytes 262144 | tf_op jit(solution)/shard_map/all_to_all | solution.py:32
  101.3 0.0 copy-done
  101.3 0.0 copy-done.2
  101.3 0.5 shard_map.117
  101.8 16.2 %all_to_all.32.third_ref = bf16[32,8,384]{2,1,0:T(8,128)(2,1)S(1)} all-to-all(bf16[32,8,384]{2,1,0:T(8,128)(2,1)S(1)} %get-tuple-element.10), channel_id=1, replica_groups=mesh['role'=4,'seq'=32,'mp'=4] {'seq'}, dimensions={0} | all-to-all | bytes 393216 | tf_op jit(solution)/shard_map/all_to_all | solution.py:32
  118.0 0.8 shard_map.118
  118.9 4.1 %all-to-all-start.5 = ((bf16[32,8,384]{2,1,0:T(8,128)(2,1)}), bf16[32,8,384]{2,1,0:T(8,128)(2,1)S(1)}, u32[]{:S(2)}, u32[]{:S(2)}) async-start(bf16[32,8,384]{2,1,0:T(8,128)(2,1)} %get-tuple-element.13), calls=%async_computation.5 | async-start | bytes 393216 | tf_op jit(solution)/shard_map/all_to_all | solution.py:32
  123.0 1.0 shard_map.119
  124.1 9.7 %all-to-all-done.5.fourth_ref = bf16[32,8,384]{2,1,0:T(8,128)(2,1)S(1)} async-done(((bf16[32,8,384]{2,1,0:T(8,128)(2,1)}), bf16[32,8,384]{2,1,0:T(8,128)(2,1)S(1)}, u32[]{:S(2)}, u32[]{:S(2)}) %all-to-all-start.5) | async-done | bytes 196640 | tf_op jit(solution)/shard_map/all_to_all | solution.py:32
  133.8 0.8 shard_map.120
  (5 shorter events, 0.1 us)
Async XLA Ops:
  5.4 96.0 %copy-start = (bf16[128,1280]{1,0:T(8,128)(2,1)S(1)}, bf16[128,1280]{1,0:T(8,128)(2,1)}, u32[]{:S(2)}) copy-start(bf16[128,1280]{1,0:T(8,128)(2,1)} %hidden_ref.3) | copy-start | bytes 983044
  5.4 20.7 %all-to-all-start = ((f32[4,72,128]{2,1,0:T(8,128)}), f32[4,72,128]{2,1,0:T(8,128)S(1)}, u32[]{:S(2)}, u32[]{:S(2)}) async-start(f32[4,72,128]{2,1,0:T(8,128)} %shard_map.113), calls=%async_computation | async-start | bytes 294912 | tf_op jit(solution)/shard_map/all_to_all | solution.py:32
  26.1 0.7 copy-start.4
  29.3 72.1 %copy-start.2 = (f32[136,128]{1,0:T(8,128)S(1)}, f32[136,128]{1,0:T(8,128)}, u32[]{:S(2)}) copy-start(f32[136,128]{1,0:T(8,128)} %get-tuple-element.9.kept_ref) | copy-start | bytes 208900
  29.3 28.7 %all-to-all-start.1 = ((bf16[32,72,128]{2,1,0:T(8,128)(2,1)}), bf16[32,72,128]{2,1,0:T(8,128)(2,1)S(1)}, u32[]{:S(2)}, u32[]{:S(2)}) async-start(bf16[32,72,128]{2,1,0:T(8,128)(2,1)} %get-tuple-element.8), calls=%async_computation.1 | async-start | bytes 1179648 | tf_op jit(solution)/shard_map/all_to_all | solution.py:32
  38.9 84.1 %copy-start.1 = (bf16[1280,64]{0,1:T(8,128)(2,1)S(1)}, bf16[1280,64]{0,1:T(8,128)(2,1)}, u32[]{:S(2)}) copy-start(bf16[1280,64]{0,1:T(8,128)(2,1)} %param.11) | copy-start | bytes 491524
  58.0 0.8 copy-start.3
  118.9 14.9 %all-to-all-start.5 = ((bf16[32,8,384]{2,1,0:T(8,128)(2,1)}), bf16[32,8,384]{2,1,0:T(8,128)(2,1)S(1)}, u32[]{:S(2)}, u32[]{:S(2)}) async-start(bf16[32,8,384]{2,1,0:T(8,128)(2,1)} %get-tuple-element.13), calls=%async_computation.5 | async-start | bytes 393216 | tf_op jit(solution)/shard_map/all_to_all | solution.py:32

commit v5 on v4

--- a/solution.py
+++ b/solution.py
@@ -52,12 +52,16 @@
     return fetches
 
 
+def in_parts(turns):
+    grain = 2.0 ** (np.floor(np.log2(turns)) - 11)
+    high = np.floor(turns / grain) * grain
+    return np.stack([high, turns - high]).astype(np.float32)
+
+
 def rotation_tables(head_dim):
     turns = ROPE_BASE ** (-2.0 * np.arange(head_dim // 2) / head_dim) / (2.0 * np.pi)
-    grain = 2.0 ** (np.floor(np.log2(turns)) - 11)
-    high = np.floor(turns / grain) * grain
-    both = np.concatenate([high, turns - high])
-    return np.ascontiguousarray(np.broadcast_to(both[:, None], (head_dim, 128)), np.float32)
+    both = in_parts(turns).reshape(head_dim)
+    return np.ascontiguousarray(np.broadcast_to(both[:, None], (head_dim, 128)))
 
 
 def rotations(positions, table):
@@ -92,7 +96,7 @@
 
 def pass_kernel(
     place_ref,
-    gathered_ref,
+    gathered_in,
     embed_in,
     weight_in,
     readout_in,
@@ -108,6 +112,7 @@
     key,
     wide,
     attended,
+    gathered_ref,
     embed_ref,
     weight_ref,
     readout_ref,
@@ -117,6 +122,7 @@
     f32 = jnp.float32
     fetches = fetch_all(
         arrived,
+        (gathered_in, gathered_ref),
         (embed_in, embed_ref),
         *(
             (weight_in.at[pl.ds(begin, CHUNK), :], weight_ref.at[pl.ds(begin, CHUNK), :])
@@ -135,6 +141,7 @@
     piece = width // blocks
     place = place_ref[0]
 
+    fetches[0].wait()
     for block in range(blocks):
         at = slice(block * lanes, (block + 1) * lanes)
         received = gathered_ref[block]
@@ -163,7 +170,7 @@
         own[lat_dim:, at] = rows
         own_places[0:1, at] = found[lat_dim : lat_dim + 1] * 64.0 + found[lat_dim + 1 : lat_dim + 2]
 
-    fetches[0].wait()
+    fetches[1].wait()
     folded = jnp.zeros((2 * lat_dim + 16, 3 * head_dim), f32)
     for begin in range(0, width, CHUNK):
         at = slice(begin, begin + CHUNK)
@@ -175,7 +182,7 @@
         shifted_high = shifted.astype(jnp.bfloat16).astype(f32)
         shifted = jnp.where(row == 0, shifted_high, shifted - shifted_high)
         scaled[2 * lat_dim :, at] = jnp.where(row < 2, shifted, 0.0).astype(jnp.bfloat16)
-        fetches[1 + begin // CHUNK].wait()
+        fetches[2 + begin // CHUNK].wait()
         folded = folded + dot32(scaled[:, at], weight_ref[at, :])
     gram = dot_rows(embed_ref[...], embed_ref[...])
     matrix = folded[:lat_dim] + folded[lat_dim : 2 * lat_dim]
@@ -254,11 +261,7 @@
     return pl.pallas_call(
         pass_kernel,
         out_shape=jax.ShapeDtypeStruct((blocks, lanes // 8, lanes), bf16),
-        in_specs=[
-            pl.BlockSpec(memory_space=pltpu.SMEM),
-            vmem,
-        ]
-        + [pl.BlockSpec(memory_space=pl.ANY)] * 4,
+        in_specs=[pl.BlockSpec(memory_space=pltpu.SMEM)] + [pl.BlockSpec(memory_space=pl.ANY)] * 5,
         out_specs=vmem,
         scratch_shapes=[
             pltpu.VMEM((8, width), f32),
@@ -271,11 +274,12 @@
             pltpu.VMEM((head_dim, key_rows), bf16),
             pltpu.VMEM((key_rows, 2 * head_dim), bf16),
             pltpu.VMEM((blocks, lanes // 4, head_dim), bf16),
+            pltpu.VMEM(gathered.shape, bf16),
             pltpu.VMEM(embed.shape, bf16),
             pltpu.VMEM(weights.shape, bf16),
             pltpu.VMEM(readout.shape, bf16),
             pltpu.VMEM((head_dim, 128), f32),
-            pltpu.SemaphoreType.DMA((3 + width // CHUNK,)),
+            pltpu.SemaphoreType.DMA((4 + width // CHUNK,)),
         ],
         compiler_params=pltpu.CompilerParams(vmem_limit_bytes=VMEM_LIMIT),
     )(place, gathered, embed, weights, readout, jnp.asarray(rotation_tables(head_dim)))
@@ -302,16 +306,34 @@
 
 
 def start_kernel(
-    active_ref, hidden_in, out_in, time_in, first_ref, hidden_ref, out_ref, time_ref, arrived
+    time_ref,
+    hidden_in,
+    out_in,
+    weight_in,
+    table_in,
+    first_ref,
+    hidden_ref,
+    out_ref,
+    weight_ref,
+    table_ref,
+    arrived,
 ):
-    fetches = fetch_all(arrived, (hidden_in, hidden_ref), (out_in, out_ref), (time_in, time_ref))
+    fetches = fetch_all(
+        arrived,
+        (table_in, table_ref),
+        (weight_in, weight_ref),
+        (hidden_in, hidden_ref),
+        (out_in, out_ref),
+    )
     lanes = hidden_ref.shape[0]
     lat_dim = out_ref.shape[0]
-    active = jnp.broadcast_to(active_ref[...], (8, active_ref.shape[1]))
-    fetches[2].wait()
+    fetches[0].wait()
+    waves = rotations(jnp.broadcast_to(time_ref[0], (1, lanes)), table_ref[...])
+    active = jnp.concatenate([wave / (1.0 + jnp.exp(-wave)) for wave in waves], axis=1)
+    fetches[1].wait()
     modulation = lax.dot_general(
         active,
-        time_ref[...],
+        weight_ref[...],
         (((1,), (1,)), ((), ())),
         precision=lax.Precision.HIGHEST,
         preferred_element_type=jnp.float32,
@@ -319,13 +341,13 @@
     modulation = jnp.concatenate(
         [modulation, jnp.zeros((8, lanes - modulation.shape[1]), jnp.float32)], axis=1
     )
-    fetches[0].wait()
+    fetches[2].wait()
     hidden = hidden_ref[...]
     wide = hidden.astype(jnp.float32)
     ones = jnp.ones((8, hidden.shape[1]), jnp.bfloat16)
     high, low = split(wide * wide)
     squares = dot_rows(ones, high) + dot_rows(ones, low)
-    fetches[1].wait()
+    fetches[3].wait()
     partial = dot_rows(out_ref[...], hidden)
     row = lax.broadcasted_iota(jnp.int32, (8, lanes), 0)
     extra = jnp.where(row == 0, squares, modulation)
@@ -336,23 +358,27 @@
 
 def noise_kernel(
     level_ref,
-    first_ref,
+    first_in,
     noise_in,
     order_in,
     second_ref,
     kept_ref,
     pair,
     extra,
+    first_ref,
     noise_ref,
     order_ref,
     arrived,
 ):
-    fetches = fetch_all(arrived, (noise_in, noise_ref), (order_in, order_ref))
+    fetches = fetch_all(
+        arrived, (first_in, first_ref), (noise_in, noise_ref), (order_in, order_ref)
+    )
     f32 = jnp.float32
     level = level_ref[0]
     peers, used, lanes = first_ref.shape
     lat_dim = noise_ref.shape[0]
     mod_width = 40
+    fetches[0].wait()
     total = first_ref[0]
     for peer in range(1, peers):
         total = total + first_ref[peer]
@@ -376,11 +402,11 @@
     extra[4:6, :] = head - head_high
     extra[6:7, :] = jnp.concatenate([tail_high, tail - tail_high], axis=1)
     extra[7:8, :] = jnp.zeros((1, lanes), f32)
-    fetches[1].wait()
+    fetches[2].wait()
     order = order_ref[...]
     extra[0:1, :] = (order // 64).astype(f32)
     extra[1:2, :] = (order % 64).astype(f32)
-    fetches[0].wait()
+    fetches[1].wait()
     noisy = ((1.0 - level) * latent + level * noise_ref[...].astype(f32)).astype(jnp.bfloat16)
     kept_ref[lat_dim : 2 * lat_dim, :] = latent - noisy.astype(f32)
     rows = jnp.concatenate([noisy, extra[...].astype(jnp.bfloat16)], axis=0)
@@ -498,20 +524,19 @@
     level = (timestep / T_STEPS)[None]
     out_turned = out_weight.T
 
-    half_freq = FREQ // 2
-    frequencies = jnp.exp(-math.log(ROPE_BASE) * jnp.arange(half_freq, dtype=f32) / half_freq)
-    phases = timestep * frequencies
-    activated = jax.nn.silu(jnp.concatenate([jnp.cos(phases), jnp.sin(phases)]))
     time_turned = time_weight[0].transpose(1, 2, 0).reshape(-1, FREQ)
+    turns = ROPE_BASE ** (-np.arange(FREQ // 2) / (FREQ // 2)) / (2.0 * np.pi)
 
     (first,) = call(
         start_kernel,
         [((mp_count, lat_dim + 8, local_rows), f32)],
-        activated[None],
+        timestep[None],
         gen_hidden,
         out_turned,
         time_turned,
-        fetched=3,
+        jnp.asarray(np.repeat(in_parts(turns), 8, axis=0)),
+        scalars=1,
+        fetched=4,
     )
     first = exchange(first, "mp")
 
@@ -523,7 +548,7 @@
         noise.T,
         token_order[None],
         scalars=1,
-        fetched=2,
+        fetched=3,
         scratch=[pltpu.VMEM((8, 2 * local_rows), f32), pltpu.VMEM((8, local_rows), f32)],
     )
     second = exchange(second, "seq")

time: 135 us -> 132 us (0.978)
  Pallas kernels: 22.1 us -> 19.7 us
where the time goes in v5:
time: 132 us
  blocking collectives  45.7 us (35%)
  waiting for transfers between devices  39.1 us (30%)
  starting transfers between devices  24.1 us (18%)
  Pallas kernels  19.7 us (15%)
  local copies, waits for them, and re-layouts  1.49 us (1%)
  between operations  1.36 us (1%)
    all_to_all x3, blocking collectives, exchange(): return lax.all_to_all(chunks, axes, 0, 0, tiled=True)  45.7 us
    all_to_all x3, waiting for transfers between devices, exchange(): return lax.all_to_all(chunks, axes, 0, 0, tiled=True)  39.1 us
    all_to_all x3, starting transfers between devices, exchange(): return lax.all_to_all(chunks, axes, 0, 0, tiled=True)  24.1 us
    pallas_call x1, Pallas kernels, run_pass(): pl.pallas_call(pass_kernel, out_shape=jax.ShapeDtypeStruct((blocks, lanes...  11.9 us
    pallas_call x7, Pallas kernels, call(): pl.pallas_call(kernel, out_shape=[jax.ShapeDtypeStruct(*output) for outpu...  7.89 us
  transfers between devices with their start and end apart: 3, of which 3 were waited for; matrix products, arithmetic and copies ran while one was open for 0% of the time, Pallas kernels for 1%

profile of v5, /device:TPU:8, one launch (start us, length us, event | category | flops | bytes accessed | tf_op | source)
XLA Modules:
  0.0 131.6 jit_solution(17815675980598981143)
XLA Ops:
  1.3 2.6 %shard_map.122 = f32[4,72,128]{2,1,0:T(8,128)} custom-call(f32[1]{0:T(128)S(6)} %convert_element_type.4.time_ref, bf16[128,1280]{1,0:T(8,128)(2,1)} %hidden_ref.3, bf16[64,1280]{1,0:T(8,128)(2,1)} %bitcast.15, f32[80,256]{1,0:T(8,128)} %bitcast.20, f32[16,128]{1,0:T(8,128)} %constant.12.clone.table_in), custom_call_target="tpu_custom_call" | custom-call | tf_op jit(solution)/shard_map/pallas_call | solution.py:296
  3.9 0.0 copy-start
  3.9 10.4 %all-to-all-start = ((f32[4,72,128]{2,1,0:T(8,128)}), f32[4,72,128]{2,1,0:T(8,128)S(1)}, u32[]{:S(2)}, u32[]{:S(2)}) async-start(f32[4,72,128]{2,1,0:T(8,128)} %shard_map.122), calls=%async_computation | async-start | bytes 294912 | tf_op jit(solution)/shard_map/all_to_all | solution.py:32
  14.3 10.3 %all-to-all-done.first_in = f32[4,72,128]{2,1,0:T(8,128)S(1)} async-done(((f32[4,72,128]{2,1,0:T(8,128)}), f32[4,72,128]{2,1,0:T(8,128)S(1)}, u32[]{:S(2)}, u32[]{:S(2)}) %all-to-all-start) | async-done | bytes 147488 | tf_op jit(solution)/shard_map/all_to_all | solution.py:32
  24.6 0.7 copy-done.4
  25.3 2.0 %shard_map.123 = (bf16[32,72,128]{2,1,0:T(8,128)(2,1)}, f32[136,128]{1,0:T(8,128)}) custom-call(f32[1]{0:T(128)S(6)} %div.3.level_ref, f32[4,72,128]{2,1,0:T(8,128)} %copy-done.4, bf16[64,128]{1,0:T(8,128)(2,1)} %bitcast.22, s32[1,128]{1,0:T(1,128)} %bitcast.23), custom_call_target="tpu_custom_call" | custom-call | tf_op jit(solution)/shard_map/pallas_call | solution.py:296
  27.3 0.0 copy-start.2
  27.3 9.6 %all-to-all-start.1 = ((bf16[32,72,128]{2,1,0:T(8,128)(2,1)}), bf16[32,72,128]{2,1,0:T(8,128)(2,1)S(1)}, u32[]{:S(2)}, u32[]{:S(2)}) async-start(bf16[32,72,128]{2,1,0:T(8,128)(2,1)} %get-tuple-element.8), calls=%async_computation.1 | async-start | bytes 1179648 | tf_op jit(solution)/shard_map/all_to_all | solution.py:32
  36.9 0.0 copy-start.1
  37.0 19.1 %all-to-all-done.1.gathered_in = bf16[32,72,128]{2,1,0:T(8,128)(2,1)S(1)} async-done(((bf16[32,72,128]{2,1,0:T(8,128)(2,1)}), bf16[32,72,128]{2,1,0:T(8,128)(2,1)S(1)}, u32[]{:S(2)}, u32[]{:S(2)}) %all-to-all-start.1) | async-done | bytes 589856 | tf_op jit(solution)/shard_map/all_to_all | solution.py:32
  56.1 0.8 copy-done.3
  56.9 11.9 %shard_map.124 = bf16[32,16,128]{2,1,0:T(8,128)(2,1)} custom-call(s32[1]{0:T(128)} %bitcast.place_ref, bf16[32,72,128]{2,1,0:T(8,128)(2,1)} %copy-done.3, bf16[64,5120]{1,0:T(8,128)(2,1)} %bitcast.18, bf16[5120,384]{1,0:T(8,128)(2,1)} %bitcast.17, bf16[64,128]{1,0:T(8,128)(2,1)} %bitcast.21, f32[128,128]{1,0:T(8,128)} %constant.13.clone.table_in), custom_call_target="tpu_custom_call" | custom-call | tf_op jit(solution)/shard_map/pallas_call | solution.py:261
  68.8 14.7 %all_to_all.30.scores_ref = bf16[32,16,128]{2,1,0:T(8,128)(2,1)S(1)} all-to-all(bf16[32,16,128]{2,1,0:T(8,128)(2,1)} %shard_map.124), channel_id=1, replica_groups=mesh['role'=4,'seq'=32,'mp'=4] {'seq'}, dimensions={0} | all-to-all | bytes 262144 | tf_op jit(solution)/shard_map/all_to_all | solution.py:32
  83.5 14.8 %all_to_all.31.score_ref = f32[16,16,128]{2,1,0:T(8,128)S(1)} all-to-all(f32[16,16,128]{2,1,0:T(8,128)S(1)} %shard_map.125), channel_id=1, replica_groups=mesh['role'=4,'seq'=32,'mp'=4] {'role','mp'}, dimensions={0} | all-to-all | bytes 262144 | tf_op jit(solution)/shard_map/all_to_all | solution.py:32
  98.4 0.0 copy-done
  98.4 0.0 copy-done.2
  98.4 0.5 shard_map.126
  98.8 16.2 %all_to_all.32.third_ref = bf16[32,8,384]{2,1,0:T(8,128)(2,1)S(1)} all-to-all(bf16[32,8,384]{2,1,0:T(8,128)(2,1)S(1)} %get-tuple-element.10), channel_id=1, replica_groups=mesh['role'=4,'seq'=32,'mp'=4] {'seq'}, dimensions={0} | all-to-all | bytes 393216 | tf_op jit(solution)/shard_map/all_to_all | solution.py:32
  115.0 0.8 shard_map.127
  115.9 4.1 %all-to-all-start.5 = ((bf16[32,8,384]{2,1,0:T(8,128)(2,1)}), bf16[32,8,384]{2,1,0:T(8,128)(2,1)S(1)}, u32[]{:S(2)}, u32[]{:S(2)}) async-start(bf16[32,8,384]{2,1,0:T(8,128)(2,1)} %get-tuple-element.13), calls=%async_computation.5 | async-start | bytes 393216 | tf_op jit(solution)/shard_map/all_to_all | solution.py:32
  120.0 0.0 copy-done.1
  120.0 1.0 shard_map.128
  121.1 9.7 %all-to-all-done.5.fourth_ref = bf16[32,8,384]{2,1,0:T(8,128)(2,1)S(1)} async-done(((bf16[32,8,384]{2,1,0:T(8,128)(2,1)}), bf16[32,8,384]{2,1,0:T(8,128)(2,1)S(1)}, u32[]{:S(2)}, u32[]{:S(2)}) %all-to-all-start.5) | async-done | bytes 196640 | tf_op jit(solution)/shard_map/all_to_all | solution.py:32
  130.8 0.8 shard_map.129
  (3 shorter events, 0.0 us)
Async XLA Ops:
  3.9 94.5 %copy-start = (bf16[128,1280]{1,0:T(8,128)(2,1)S(1)}, bf16[128,1280]{1,0:T(8,128)(2,1)}, u32[]{:S(2)}) copy-start(bf16[128,1280]{1,0:T(8,128)(2,1)} %hidden_ref.3) | copy-start | bytes 983044
  3.9 20.7 %all-to-all-start = ((f32[4,72,128]{2,1,0:T(8,128)}), f32[4,72,128]{2,1,0:T(8,128)S(1)}, u32[]{:S(2)}, u32[]{:S(2)}) async-start(f32[4,72,128]{2,1,0:T(8,128)} %shard_map.122), calls=%async_computation | async-start | bytes 294912 | tf_op jit(solution)/shard_map/all_to_all | solution.py:32
  24.6 0.7 copy-start.4
  27.3 71.0 %copy-start.2 = (f32[136,128]{1,0:T(8,128)S(1)}, f32[136,128]{1,0:T(8,128)}, u32[]{:S(2)}) copy-start(f32[136,128]{1,0:T(8,128)} %get-tuple-element.9.kept_ref) | copy-start | bytes 208900
  27.3 28.7 %all-to-all-start.1 = ((bf16[32,72,128]{2,1,0:T(8,128)(2,1)}), bf16[32,72,128]{2,1,0:T(8,128)(2,1)S(1)}, u32[]{:S(2)}, u32[]{:S(2)}) async-start(bf16[32,72,128]{2,1,0:T(8,128)(2,1)} %get-tuple-element.8), calls=%async_computation.1 | async-start | bytes 1179648 | tf_op jit(solution)/shard_map/all_to_all | solution.py:32
  36.9 83.1 %copy-start.1 = (bf16[1280,64]{0,1:T(8,128)(2,1)S(1)}, bf16[1280,64]{0,1:T(8,128)(2,1)}, u32[]{:S(2)}) copy-start(bf16[1280,64]{0,1:T(8,128)(2,1)} %param.12) | copy-start | bytes 491524
  56.1 0.8 copy-start.3
  115.9 14.9 %all-to-all-start.5 = ((bf16[32,8,384]{2,1,0:T(8,128)(2,1)}), bf16[32,8,384]{2,1,0:T(8,128)(2,1)S(1)}, u32[]{:S(2)}, u32[]{:S(2)}) async-start(bf16[32,8,384]{2,1,0:T(8,128)(2,1)} %get-tuple-element.13), calls=%async_computation.5 | async-start | bytes 393216 | tf_op jit(solution)/shard_map/all_to_all | solution.py:32

commit v6 on v5

--- a/solution.py
+++ b/solution.py
@@ -96,11 +96,10 @@
 
 def pass_kernel(
     place_ref,
-    gathered_in,
-    embed_in,
-    weight_in,
-    readout_in,
-    table_in,
+    gathered_ref,
+    embed_ref,
+    weight_ref,
+    small_ref,
     score_ref,
     modulation,
     scaled,
@@ -112,25 +111,8 @@
     key,
     wide,
     attended,
-    gathered_ref,
-    embed_ref,
-    weight_ref,
-    readout_ref,
-    table_ref,
-    arrived,
 ):
     f32 = jnp.float32
-    fetches = fetch_all(
-        arrived,
-        (gathered_in, gathered_ref),
-        (embed_in, embed_ref),
-        *(
-            (weight_in.at[pl.ds(begin, CHUNK), :], weight_ref.at[pl.ds(begin, CHUNK), :])
-            for begin in range(0, weight_ref.shape[0], CHUNK)
-        ),
-        (table_in, table_ref),
-        (readout_in, readout_ref),
-    )
     blocks, used, lanes = gathered_ref.shape
     lat_dim, width = embed_ref.shape
     head_dim = weight_ref.shape[1] // 3
@@ -141,7 +123,6 @@
     piece = width // blocks
     place = place_ref[0]
 
-    fetches[0].wait()
     for block in range(blocks):
         at = slice(block * lanes, (block + 1) * lanes)
         received = gathered_ref[block]
@@ -170,11 +151,10 @@
         own[lat_dim:, at] = rows
         own_places[0:1, at] = found[lat_dim : lat_dim + 1] * 64.0 + found[lat_dim + 1 : lat_dim + 2]
 
-    fetches[1].wait()
     folded = jnp.zeros((2 * lat_dim + 16, 3 * head_dim), f32)
     for begin in range(0, width, CHUNK):
         at = slice(begin, begin + CHUNK)
-        high, low = split(embed_ref[:, at].astype(f32) * (1.0 + modulation[1:2, at]))
+        high, low = split(embed_ref[:, at] * (1.0 + modulation[1:2, at]))
         scaled[:lat_dim, at] = high
         scaled[lat_dim : 2 * lat_dim, at] = low
         row = lax.broadcasted_iota(jnp.int32, (16, CHUNK), 0)
@@ -182,9 +162,9 @@
         shifted_high = shifted.astype(jnp.bfloat16).astype(f32)
         shifted = jnp.where(row == 0, shifted_high, shifted - shifted_high)
         scaled[2 * lat_dim :, at] = jnp.where(row < 2, shifted, 0.0).astype(jnp.bfloat16)
-        fetches[2 + begin // CHUNK].wait()
         folded = folded + dot32(scaled[:, at], weight_ref[at, :])
-    gram = dot_rows(embed_ref[...], embed_ref[...])
+    embed = embed_ref[...].astype(jnp.bfloat16)
+    gram = dot_rows(embed, embed)
     matrix = folded[:lat_dim] + folded[lat_dim : 2 * lat_dim]
     offset = folded[2 * lat_dim : 2 * lat_dim + 1] + folded[2 * lat_dim + 1 : 2 * lat_dim + 2]
     turned = jnp.concatenate(
@@ -202,8 +182,7 @@
         return product[:count] * lax.rsqrt(mean + EPS_NORM) + offsets
 
     step = 4 * lanes
-    fetches[-2].wait()
-    table = table_ref[...]
+    table = small_ref[lat_dim:, :]
     wide[:, head_dim:] = jnp.ones((key_rows, head_dim), jnp.bfloat16)
     for begin in range(0, query_rows, step):
         at = slice(begin, begin + step)
@@ -240,9 +219,9 @@
 
     lax.fori_loop(0, query_rows // rows, attend, 0, unroll=True)
     half = quarter // 2
-    fetches[-1].wait()
+    readout = small_ref[:lat_dim, :].astype(jnp.bfloat16)
     halves = [
-        dot_rows(attended[:, begin : begin + half, :].reshape(blocks * half, head_dim), readout_ref[...])
+        dot_rows(attended[:, begin : begin + half, :].reshape(blocks * half, head_dim), readout)
         for begin in (0, half)
     ]
     score_ref[...] = (
@@ -250,7 +229,7 @@
     )
 
 
-def run_pass(place, gathered, embed, weights, readout):
+def run_pass(place, gathered, embed, weights, small):
     blocks, unused, lanes = gathered.shape
     lat_dim, width = embed.shape
     head_dim = weights.shape[1] // 3
@@ -261,7 +240,7 @@
     return pl.pallas_call(
         pass_kernel,
         out_shape=jax.ShapeDtypeStruct((blocks, lanes // 8, lanes), bf16),
-        in_specs=[pl.BlockSpec(memory_space=pltpu.SMEM)] + [pl.BlockSpec(memory_space=pl.ANY)] * 5,
+        in_specs=[pl.BlockSpec(memory_space=pltpu.SMEM)] + [vmem] * 4,
         out_specs=vmem,
         scratch_shapes=[
             pltpu.VMEM((8, width), f32),
@@ -274,15 +253,9 @@
             pltpu.VMEM((head_dim, key_rows), bf16),
             pltpu.VMEM((key_rows, 2 * head_dim), bf16),
             pltpu.VMEM((blocks, lanes // 4, head_dim), bf16),
-            pltpu.VMEM(gathered.shape, bf16),
-            pltpu.VMEM(embed.shape, bf16),
-            pltpu.VMEM(weights.shape, bf16),
-            pltpu.VMEM(readout.shape, bf16),
-            pltpu.VMEM((head_dim, 128), f32),
-            pltpu.SemaphoreType.DMA((4 + width // CHUNK,)),
         ],
-        compiler_params=pltpu.CompilerParams(vmem_limit_bytes=VMEM_LIMIT),
-    )(place, gathered, embed, weights, readout, jnp.asarray(rotation_tables(head_dim)))
+        compiler_params=pltpu.CompilerParams(vmem_limit_bytes=40 * 1024 * 1024),
+    )(place, gathered, embed, weights, small)
 
 
 def call(kernel, outputs, *operands, scalars=0, fetched=0, scratch=()):
@@ -358,27 +331,19 @@
 
 def noise_kernel(
     level_ref,
-    first_in,
-    noise_in,
-    order_in,
+    first_ref,
+    noise_ref,
+    order_ref,
     second_ref,
     kept_ref,
     pair,
     extra,
-    first_ref,
-    noise_ref,
-    order_ref,
-    arrived,
 ):
-    fetches = fetch_all(
-        arrived, (first_in, first_ref), (noise_in, noise_ref), (order_in, order_ref)
-    )
     f32 = jnp.float32
     level = level_ref[0]
     peers, used, lanes = first_ref.shape
     lat_dim = noise_ref.shape[0]
     mod_width = 40
-    fetches[0].wait()
     total = first_ref[0]
     for peer in range(1, peers):
         total = total + first_ref[peer]
@@ -402,12 +367,8 @@
     extra[4:6, :] = head - head_high
     extra[6:7, :] = jnp.concatenate([tail_high, tail - tail_high], axis=1)
     extra[7:8, :] = jnp.zeros((1, lanes), f32)
-    fetches[2].wait()
-    order = order_ref[...]
-    extra[0:1, :] = (order // 64).astype(f32)
-    extra[1:2, :] = (order % 64).astype(f32)
-    fetches[1].wait()
-    noisy = ((1.0 - level) * latent + level * noise_ref[...].astype(f32)).astype(jnp.bfloat16)
+    extra[0:2, :] = order_ref[...]
+    noisy = ((1.0 - level) * latent + level * noise_ref[...]).astype(jnp.bfloat16)
     kept_ref[lat_dim : 2 * lat_dim, :] = latent - noisy.astype(f32)
     rows = jnp.concatenate([noisy, extra[...].astype(jnp.bfloat16)], axis=0)
     for peer in range(second_ref.shape[0]):
@@ -545,19 +506,20 @@
         [((seq_count, lat_dim + 8, local_rows), bf16), ((2 * lat_dim + 8, local_rows), f32)],
         level,
         first,
-        noise.T,
-        token_order[None],
+        noise.T.astype(f32),
+        jnp.stack([token_order // 64, token_order % 64]).astype(f32),
         scalars=1,
-        fetched=3,
         scratch=[pltpu.VMEM((8, 2 * local_rows), f32), pltpu.VMEM((8, local_rows), f32)],
     )
     second = exchange(second, "seq")
     scores = run_pass(
         mp_index.astype(jnp.int32)[None],
         second,
-        embed_weight[0],
+        embed_weight[0].astype(f32),
         qkv_weight[0, 0],
-        readout_weight[0, 0].T,
+        jnp.concatenate(
+            [readout_weight[0, 0].T.astype(f32), rotation_tables(qkv_weight.shape[3] // 3)]
+        ),
     )
 
     scores = exchange(scores, "seq")

time: 132 us -> 129 us (0.977)
  Pallas kernels: 19.7 us -> 16.1 us
  waiting for transfers between devices: 39.1 us -> 36 us
  other arithmetic: 0 us -> 3.05 us
    all_to_all x3, waiting for transfers between devices: 39.1 us -> 36 us  [exchange(): return lax.all_to_all(chunks, axes, 0, 0, tiled=True)]
    pallas_call x1, Pallas kernels: 11.9 us -> 9.14 us  [run_pass(): pl.pallas_call(pass_kernel, out_shape=jax.ShapeDtypeStruct((blocks, lanes...]
    convert_element_type x0 -> x4, other arithmetic: none -> 1.54 us  [the longest x1 0.72 us: body(): readout_weight[0, 0].T.astype(f32)]
  transfers between devices with their start and end apart: 3 -> 3, of which waited for: 3 -> 3; matrix products, arithmetic and copies ran while one was open for 0% -> 2% of each run, Pallas kernels for 1% -> 1%
where the time goes in v6:
time: 129 us; the launch traced here: 128 us
  blocking collectives  45.7 us (35%)
  waiting for transfers between devices  36 us (28%)
  starting transfers between devices  23.9 us (19%)
  Pallas kernels  16.1 us (12%)
  other arithmetic  3.05 us (2%)
  local copies, waits for them, and re-layouts  2.13 us (2%)
  between operations  1.36 us (1%)
    all_to_all x3, blocking collectives, exchange(): return lax.all_to_all(chunks, axes, 0, 0, tiled=True)  45.7 us
    all_to_all x3, waiting for transfers between devices, exchange(): return lax.all_to_all(chunks, axes, 0, 0, tiled=True)  36 us
    all_to_all x3, starting transfers between devices, exchange(): return lax.all_to_all(chunks, axes, 0, 0, tiled=True)  23.9 us
    pallas_call x1, Pallas kernels, run_pass(): pl.pallas_call(pass_kernel, out_shape=jax.ShapeDtypeStruct((blocks, lanes...  9.14 us
    pallas_call x7, Pallas kernels, call(): pl.pallas_call(kernel, out_shape=[jax.ShapeDtypeStruct(*output) for outpu...  6.94 us
  transfers between devices with their start and end apart: 3, of which 3 were waited for; matrix products, arithmetic and copies ran while one was open for 2% of the time, Pallas kernels for 1%

profile of v6, /device:TPU:8, one launch (start us, length us, event | category | flops | bytes accessed | tf_op | source)
XLA Modules:
  0.0 128.2 jit_solution(8919203880548288092)
XLA Ops:
  1.3 0.0 copy-start.3
  1.3 2.7 %shard_map.122 = f32[4,72,128]{2,1,0:T(8,128)} custom-call(f32[1]{0:T(128)S(6)} %convert_element_type.26.time_ref, bf16[128,1280]{1,0:T(8,128)(2,1)} %hidden_ref.3, bf16[64,1280]{1,0:T(8,128)(2,1)} %bitcast.24, f32[80,256]{1,0:T(8,128)} %bitcast.27, f32[16,128]{1,0:T(8,128)} %constant.40.clone.table_in), custom_call_target="tpu_custom_call" | custom-call | tf_op jit(solution)/shard_map/pallas_call | solution.py:269
  4.0 10.3 %all-to-all-start = ((f32[4,72,128]{2,1,0:T(8,128)}), f32[4,72,128]{2,1,0:T(8,128)S(1)}, u32[]{:S(2)}, u32[]{:S(2)}) async-start(f32[4,72,128]{2,1,0:T(8,128)} %shard_map.122), calls=%async_computation | async-start | bytes 294912 | tf_op jit(solution)/shard_map/all_to_all | solution.py:32
  14.3 0.7 fusion.1
  14.9 0.7 convert_bitcast_fusion
  15.6 0.9 pad_maximum_fusion.small_ref
  16.5 0.7 convert_bitcast_fusion.1.noise_ref
  17.2 7.3 %all-to-all-done.first_ref = f32[4,72,128]{2,1,0:T(8,128)S(1)} async-done(((f32[4,72,128]{2,1,0:T(8,128)}), f32[4,72,128]{2,1,0:T(8,128)S(1)}, u32[]{:S(2)}, u32[]{:S(2)}) %all-to-all-start) | async-done | bytes 147488 | tf_op jit(solution)/shard_map/all_to_all | solution.py:32
  24.6 1.0 shard_map.123
  25.6 9.4 %all-to-all-start.1 = ((bf16[32,72,128]{2,1,0:T(8,128)(2,1)}), bf16[32,72,128]{2,1,0:T(8,128)(2,1)S(1)}, u32[]{:S(2)}, u32[]{:S(2)}) async-start(bf16[32,72,128]{2,1,0:T(8,128)(2,1)} %get-tuple-element.8), calls=%async_computation.1 | async-start | bytes 1179648 | tf_op jit(solution)/shard_map/all_to_all | solution.py:32
  35.0 0.1 bitcast_convert_fusion.embed_ref
  35.1 19.0 %all-to-all-done.1.gathered_ref = bf16[32,72,128]{2,1,0:T(8,128)(2,1)S(1)} async-done(((bf16[32,72,128]{2,1,0:T(8,128)(2,1)}), bf16[32,72,128]{2,1,0:T(8,128)(2,1)S(1)}, u32[]{:S(2)}, u32[]{:S(2)}) %all-to-all-start.1) | async-done | bytes 589856 | tf_op jit(solution)/shard_map/all_to_all | solution.py:32
  54.2 2.1 %copy-done = bf16[1,1,5120,384]{3,2,1,0:T(8,128)(2,1)S(1)} copy-done((bf16[1,1,5120,384]{3,2,1,0:T(8,128)(2,1)S(1)}, bf16[1,1,5120,384]{3,2,1,0:T(8,128)(2,1)}, u32[]{:S(2)}) %copy-start) | copy-done | bytes 3932184
  56.3 9.1 %shard_map.124 = bf16[32,16,128]{2,1,0:T(8,128)(2,1)S(1)} custom-call(s32[1]{0:T(128)} %bitcast.place_ref, bf16[32,72,128]{2,1,0:T(8,128)(2,1)S(1)} %all-to-all-done.1.gathered_ref, f32[64,5120]{1,0:T(8,128)S(1)} %bitcast_convert_fusion.embed_ref, bf16[5120,384]{1,0:T(8,128)(2,1)S(1)} %bitcast.23, f32[192,128]{1,0:T(8,128)S(1)} %pad_maximum_fusion.small_ref), custom_call_target="tpu_custom_call" | custom-call | tf_op jit(solution)/shard_map/pallas_call | solution.py:240
  65.4 0.0 copy-start.2
  65.4 14.7 %all_to_all.30.scores_ref = bf16[32,16,128]{2,1,0:T(8,128)(2,1)S(1)} all-to-all(bf16[32,16,128]{2,1,0:T(8,128)(2,1)S(1)} %shard_map.124), channel_id=1, replica_groups=mesh['role'=4,'seq'=32,'mp'=4] {'seq'}, dimensions={0} | all-to-all | bytes 262144 | tf_op jit(solution)/shard_map/all_to_all | solution.py:32
  80.2 14.8 %all_to_all.31.score_ref = f32[16,16,128]{2,1,0:T(8,128)S(1)} all-to-all(f32[16,16,128]{2,1,0:T(8,128)S(1)} %shard_map.125), channel_id=1, replica_groups=mesh['role'=4,'seq'=32,'mp'=4] {'role','mp'}, dimensions={0} | all-to-all | bytes 262144 | tf_op jit(solution)/shard_map/all_to_all | solution.py:32
  95.0 0.5 shard_map.126
  95.5 16.2 %all_to_all.32.third_ref = bf16[32,8,384]{2,1,0:T(8,128)(2,1)S(1)} all-to-all(bf16[32,8,384]{2,1,0:T(8,128)(2,1)S(1)} %get-tuple-element.10), channel_id=1, replica_groups=mesh['role'=4,'seq'=32,'mp'=4] {'seq'}, dimensions={0} | all-to-all | bytes 393216 | tf_op jit(solution)/shard_map/all_to_all | solution.py:32
  111.7 0.8 shard_map.127
  112.5 4.1 %all-to-all-start.5 = ((bf16[32,8,384]{2,1,0:T(8,128)(2,1)}), bf16[32,8,384]{2,1,0:T(8,128)(2,1)S(1)}, u32[]{:S(2)}, u32[]{:S(2)}) async-start(bf16[32,8,384]{2,1,0:T(8,128)(2,1)} %get-tuple-element.13), calls=%async_computation.5 | async-start | bytes 393216 | tf_op jit(solution)/shard_map/all_to_all | solution.py:32
  116.7 1.0 shard_map.128
  117.7 9.7 %all-to-all-done.5.fourth_ref = bf16[32,8,384]{2,1,0:T(8,128)(2,1)S(1)} async-done(((bf16[32,8,384]{2,1,0:T(8,128)(2,1)}), bf16[32,8,384]{2,1,0:T(8,128)(2,1)S(1)}, u32[]{:S(2)}, u32[]{:S(2)}) %all-to-all-start.5) | async-done | bytes 196640 | tf_op jit(solution)/shard_map/all_to_all | solution.py:32
  127.4 0.8 shard_map.129
  (7 shorter events, 0.1 us)
Async XLA Ops:
  1.3 33.8 %copy-start.3 = (bf16[1,64,5120]{2,1,0:T(8,128)(2,1)S(1)}, bf16[1,64,5120]{2,1,0:T(8,128)(2,1)}, u32[]{:S(2)}) copy-start(bf16[1,64,5120]{2,1,0:T(8,128)(2,1)} %param.17) | copy-start | bytes 1966084
  4.0 20.6 %all-to-all-start = ((f32[4,72,128]{2,1,0:T(8,128)}), f32[4,72,128]{2,1,0:T(8,128)S(1)}, u32[]{:S(2)}, u32[]{:S(2)}) async-start(f32[4,72,128]{2,1,0:T(8,128)} %shard_map.122), calls=%async_computation | async-start | bytes 294912 | tf_op jit(solution)/shard_map/all_to_all | solution.py:32
  25.6 28.6 %all-to-all-start.1 = ((bf16[32,72,128]{2,1,0:T(8,128)(2,1)}), bf16[32,72,128]{2,1,0:T(8,128)(2,1)S(1)}, u32[]{:S(2)}, u32[]{:S(2)}) async-start(bf16[32,72,128]{2,1,0:T(8,128)(2,1)} %get-tuple-element.8), calls=%async_computation.1 | async-start | bytes 1179648 | tf_op jit(solution)/shard_map/all_to_all | solution.py:32
  54.2 2.1 %copy-start = (bf16[1,1,5120,384]{3,2,1,0:T(8,128)(2,1)S(1)}, bf16[1,1,5120,384]{3,2,1,0:T(8,128)(2,1)}, u32[]{:S(2)}) copy-start(bf16[1,1,5120,384]{3,2,1,0:T(8,128)(2,1)} %param.18) | copy-start | bytes 11796484
  56.3 38.7 %copy-start.1 = (bf16[128,1280]{1,0:T(8,128)(2,1)S(1)}, bf16[128,1280]{1,0:T(8,128)(2,1)}, u32[]{:S(2)}) copy-start(bf16[128,1280]{1,0:T(8,128)(2,1)} %hidden_ref.3) | copy-start | bytes 983044
  65.4 51.2 %copy-start.2 = (bf16[1280,64]{0,1:T(8,128)(2,1)S(1)}, bf16[1280,64]{0,1:T(8,128)(2,1)}, u32[]{:S(2)}) copy-start(bf16[1280,64]{0,1:T(8,128)(2,1)} %param.12) | copy-start | bytes 491524
  112.5 14.9 %all-to-all-start.5 = ((bf16[32,8,384]{2,1,0:T(8,128)(2,1)}), bf16[32,8,384]{2,1,0:T(8,128)(2,1)S(1)}, u32[]{:S(2)}, u32[]{:S(2)}) async-start(bf16[32,8,384]{2,1,0:T(8,128)(2,1)} %get-tuple-element.13), calls=%async_computation.5 | async-start | bytes 393216 | tf_op jit(solution)/shard_map/all_to_all | solution.py:32

commit v7 on v6

--- a/solution.py
+++ b/solution.py
@@ -200,7 +200,7 @@
 
     lax.fori_loop(0, key_rows // step, keys_and_values, 0, unroll=True)
 
-    rows = 512
+    rows, step = 1024, 256
     factor = SHARPNESS / math.sqrt(head_dim) * math.log2(math.e)
 
     def attend(index, carry):
@@ -300,10 +300,10 @@
     )
     lanes = hidden_ref.shape[0]
     lat_dim = out_ref.shape[0]
-    fetches[0].wait()
+    for fetch in fetches:
+        fetch.wait()
     waves = rotations(jnp.broadcast_to(time_ref[0], (1, lanes)), table_ref[...])
     active = jnp.concatenate([wave / (1.0 + jnp.exp(-wave)) for wave in waves], axis=1)
-    fetches[1].wait()
     modulation = lax.dot_general(
         active,
         weight_ref[...],
@@ -314,19 +314,19 @@
     modulation = jnp.concatenate(
         [modulation, jnp.zeros((8, lanes - modulation.shape[1]), jnp.float32)], axis=1
     )
-    fetches[2].wait()
     hidden = hidden_ref[...]
     wide = hidden.astype(jnp.float32)
     ones = jnp.ones((8, hidden.shape[1]), jnp.bfloat16)
     high, low = split(wide * wide)
     squares = dot_rows(ones, high) + dot_rows(ones, low)
-    fetches[3].wait()
     partial = dot_rows(out_ref[...], hidden)
     row = lax.broadcasted_iota(jnp.int32, (8, lanes), 0)
-    extra = jnp.where(row == 0, squares, modulation)
+    values = jnp.where(row < 2, squares, jnp.where(row < 4, modulation, 0.0))
+    high = values.astype(jnp.bfloat16).astype(jnp.float32)
+    extra = jnp.where(row % 2 == 0, high, values - high)
+    rows = jnp.concatenate([partial, extra], axis=0).astype(jnp.bfloat16)
     for peer in range(first_ref.shape[0]):
-        first_ref[peer, :lat_dim, :] = partial
-        first_ref[peer, lat_dim:, :] = extra
+        first_ref[peer] = rows
 
 
 def noise_kernel(
@@ -344,20 +344,21 @@
     peers, used, lanes = first_ref.shape
     lat_dim = noise_ref.shape[0]
     mod_width = 40
-    total = first_ref[0]
-    for peer in range(1, peers):
-        total = total + first_ref[peer]
+    parts = [first_ref[peer].astype(f32) for peer in range(peers)]
+    total = sum(parts[1:], parts[0])
     projected = total[:lat_dim]
-    root_mean = jnp.sqrt(total[lat_dim : lat_dim + 1] / D + EPS_NORM)
+    root_mean = jnp.sqrt(
+        (total[lat_dim : lat_dim + 1] + total[lat_dim + 1 : lat_dim + 2]) / D + EPS_NORM
+    )
     latent = projected / root_mean
     kept_ref[:lat_dim, :] = projected
     kept_ref[2 * lat_dim :, :] = jnp.broadcast_to(root_mean, (8, lanes))
     pair[...] = jnp.zeros_like(pair)
     for peer in range(peers):
         at = slice(peer * mod_width, (peer + 1) * mod_width)
-        row = first_ref[peer, lat_dim : lat_dim + 8, :]
-        pair[0:1, at] = row[1:2, :mod_width]
-        pair[1:2, at] = row[1:2, mod_width : 2 * mod_width]
+        row = parts[peer][lat_dim + 2 : lat_dim + 3] + parts[peer][lat_dim + 3 : lat_dim + 4]
+        pair[0:1, at] = row[:, :mod_width]
+        pair[1:2, at] = row[:, mod_width : 2 * mod_width]
     rest = peers * mod_width - lanes
     head = pair[0:2, :lanes]
     head_high = head.astype(jnp.bfloat16).astype(f32)
@@ -490,7 +491,7 @@
 
     (first,) = call(
         start_kernel,
-        [((mp_count, lat_dim + 8, local_rows), f32)],
+        [((mp_count, lat_dim + 8, local_rows), bf16)],
         timestep[None],
         gen_hidden,
         out_turned,

time: 129 us -> 127 us (0.984)
  waiting for transfers between devices: 36 us -> 34.1 us
    all_to_all x3, waiting for transfers between devices: 36 us -> 34.1 us  [exchange(): return lax.all_to_all(chunks, axes, 0, 0, tiled=True)]
where the time goes in v7:
time: 127 us
  blocking collectives  46.5 us (37%)
  waiting for transfers between devices  34.1 us (27%)
  starting transfers between devices  24.2 us (19%)
  Pallas kernels  15.3 us (12%)
  other arithmetic  3.05 us (2%)
  local copies, waits for them, and re-layouts  2.13 us (2%)
  between operations  1.43 us (1%)
    all_to_all x3, blocking collectives, exchange(): return lax.all_to_all(chunks, axes, 0, 0, tiled=True)  46.5 us
    all_to_all x3, waiting for transfers between devices, exchange(): return lax.all_to_all(chunks, axes, 0, 0, tiled=True)  34.1 us
    all_to_all x3, starting transfers between devices, exchange(): return lax.all_to_all(chunks, axes, 0, 0, tiled=True)  24.2 us
    pallas_call x1, Pallas kernels, run_pass(): pl.pallas_call(pass_kernel, out_shape=jax.ShapeDtypeStruct((blocks, lanes...  8.84 us
    pallas_call x7, Pallas kernels, call(): pl.pallas_call(kernel, out_shape=[jax.ShapeDtypeStruct(*output) for outpu...  6.51 us
  transfers between devices with their start and end apart: 3, of which 3 were waited for; matrix products, arithmetic and copies ran while one was open for 2% of the time, Pallas kernels for 1%

profile of v7, /device:TPU:8, one launch (start us, length us, event | category | flops | bytes accessed | tf_op | source)
XLA Modules:
  0.0 126.7 jit_solution(11345577536158311824)
XLA Ops:
  1.4 2.2 %shard_map.122 = bf16[4,72,128]{2,1,0:T(8,128)(2,1)} custom-call(f32[1]{0:T(128)S(6)} %convert_element_type.26.time_ref, bf16[128,1280]{1,0:T(8,128)(2,1)} %hidden_ref.3, bf16[64,1280]{1,0:T(8,128)(2,1)} %bitcast.24, f32[80,256]{1,0:T(8,128)} %bitcast.27, f32[16,128]{1,0:T(8,128)} %constant.40.clone.table_in), custom_call_target="tpu_custom_call" | custom-call | tf_op jit(solution)/shard_map/pallas_call | solution.py:269
  3.6 10.3 %all-to-all-start = ((bf16[4,72,128]{2,1,0:T(8,128)(2,1)}), bf16[4,72,128]{2,1,0:T(8,128)(2,1)S(1)}, u32[]{:S(2)}, u32[]{:S(2)}) async-start(bf16[4,72,128]{2,1,0:T(8,128)(2,1)} %shard_map.122), calls=%async_computation | async-start | bytes 147456 | tf_op jit(solution)/shard_map/all_to_all | solution.py:32
  13.9 0.7 fusion.1
  14.5 0.7 convert_bitcast_fusion.1.noise_ref
  15.3 0.7 convert_bitcast_fusion
  16.0 0.8 pad_maximum_fusion.small_ref
  16.8 5.8 %all-to-all-done.first_ref = bf16[4,72,128]{2,1,0:T(8,128)(2,1)S(1)} async-done(((bf16[4,72,128]{2,1,0:T(8,128)(2,1)}), bf16[4,72,128]{2,1,0:T(8,128)(2,1)S(1)}, u32[]{:S(2)}, u32[]{:S(2)}) %all-to-all-start) | async-done | bytes 73760 | tf_op jit(solution)/shard_map/all_to_all | solution.py:32
  22.7 1.0 shard_map.123
  23.7 9.7 %all-to-all-start.1 = ((bf16[32,72,128]{2,1,0:T(8,128)(2,1)}), bf16[32,72,128]{2,1,0:T(8,128)(2,1)S(1)}, u32[]{:S(2)}, u32[]{:S(2)}) async-start(bf16[32,72,128]{2,1,0:T(8,128)(2,1)} %get-tuple-element.8), calls=%async_computation.1 | async-start | bytes 1179648 | tf_op jit(solution)/shard_map/all_to_all | solution.py:32
  33.4 0.0 copy-done.3
  33.4 0.1 bitcast_convert_fusion.embed_ref
  33.5 18.6 %all-to-all-done.1.gathered_ref = bf16[32,72,128]{2,1,0:T(8,128)(2,1)S(1)} async-done(((bf16[32,72,128]{2,1,0:T(8,128)(2,1)}), bf16[32,72,128]{2,1,0:T(8,128)(2,1)S(1)}, u32[]{:S(2)}, u32[]{:S(2)}) %all-to-all-start.1) | async-done | bytes 589856 | tf_op jit(solution)/shard_map/all_to_all | solution.py:32
  52.2 2.1 %copy-done = bf16[1,1,5120,384]{3,2,1,0:T(8,128)(2,1)S(1)} copy-done((bf16[1,1,5120,384]{3,2,1,0:T(8,128)(2,1)S(1)}, bf16[1,1,5120,384]{3,2,1,0:T(8,128)(2,1)}, u32[]{:S(2)}) %copy-start) | copy-done | bytes 3932184
  54.3 8.8 %shard_map.124 = bf16[32,16,128]{2,1,0:T(8,128)(2,1)S(1)} custom-call(s32[1]{0:T(128)} %bitcast.place_ref, bf16[32,72,128]{2,1,0:T(8,128)(2,1)S(1)} %all-to-all-done.1.gathered_ref, f32[64,5120]{1,0:T(8,128)S(1)} %bitcast_convert_fusion.embed_ref, bf16[5120,384]{1,0:T(8,128)(2,1)S(1)} %bitcast.23, f32[192,128]{1,0:T(8,128)S(1)} %pad_maximum_fusion.small_ref), custom_call_target="tpu_custom_call" | custom-call | tf_op jit(solution)/shard_map/pallas_call | solution.py:240
  63.1 0.0 copy-start.2
  63.1 14.5 %all_to_all.30.scores_ref = bf16[32,16,128]{2,1,0:T(8,128)(2,1)S(1)} all-to-all(bf16[32,16,128]{2,1,0:T(8,128)(2,1)S(1)} %shard_map.124), channel_id=1, replica_groups=mesh['role'=4,'seq'=32,'mp'=4] {'seq'}, dimensions={0} | all-to-all | bytes 262144 | tf_op jit(solution)/shard_map/all_to_all | solution.py:32
  77.6 15.8 %all_to_all.31.score_ref = f32[16,16,128]{2,1,0:T(8,128)S(1)} all-to-all(f32[16,16,128]{2,1,0:T(8,128)S(1)} %shard_map.125), channel_id=1, replica_groups=mesh['role'=4,'seq'=32,'mp'=4] {'role','mp'}, dimensions={0} | all-to-all | bytes 262144 | tf_op jit(solution)/shard_map/all_to_all | solution.py:32
  93.4 0.5 shard_map.126
  93.9 16.2 %all_to_all.32.third_ref = bf16[32,8,384]{2,1,0:T(8,128)(2,1)S(1)} all-to-all(bf16[32,8,384]{2,1,0:T(8,128)(2,1)S(1)} %get-tuple-element.10), channel_id=1, replica_groups=mesh['role'=4,'seq'=32,'mp'=4] {'seq'}, dimensions={0} | all-to-all | bytes 393216 | tf_op jit(solution)/shard_map/all_to_all | solution.py:32
  110.1 0.8 shard_map.127
  111.0 4.2 %all-to-all-start.5 = ((bf16[32,8,384]{2,1,0:T(8,128)(2,1)}), bf16[32,8,384]{2,1,0:T(8,128)(2,1)S(1)}, u32[]{:S(2)}, u32[]{:S(2)}) async-start(bf16[32,8,384]{2,1,0:T(8,128)(2,1)} %get-tuple-element.13), calls=%async_computation.5 | async-start | bytes 393216 | tf_op jit(solution)/shard_map/all_to_all | solution.py:32
  115.1 1.0 shard_map.128
  116.2 9.7 %all-to-all-done.5.fourth_ref = bf16[32,8,384]{2,1,0:T(8,128)(2,1)S(1)} async-done(((bf16[32,8,384]{2,1,0:T(8,128)(2,1)}), bf16[32,8,384]{2,1,0:T(8,128)(2,1)S(1)}, u32[]{:S(2)}, u32[]{:S(2)}) %all-to-all-start.5) | async-done | bytes 196640 | tf_op jit(solution)/shard_map/all_to_all | solution.py:32
  125.8 0.8 shard_map.129
  (7 shorter events, 0.1 us)
Async XLA Ops:
  0.6 32.8 %copy-start.3 = (bf16[1,64,5120]{2,1,0:T(8,128)(2,1)S(1)}, bf16[1,64,5120]{2,1,0:T(8,128)(2,1)}, u32[]{:S(2)}) copy-start(bf16[1,64,5120]{2,1,0:T(8,128)(2,1)} %param.17) | copy-start | bytes 1966084
  3.6 19.1 %all-to-all-start = ((bf16[4,72,128]{2,1,0:T(8,128)(2,1)}), bf16[4,72,128]{2,1,0:T(8,128)(2,1)S(1)}, u32[]{:S(2)}, u32[]{:S(2)}) async-start(bf16[4,72,128]{2,1,0:T(8,128)(2,1)} %shard_map.122), calls=%async_computation | async-start | bytes 147456 | tf_op jit(solution)/shard_map/all_to_all | solution.py:32
  23.7 28.4 %all-to-all-start.1 = ((bf16[32,72,128]{2,1,0:T(8,128)(2,1)}), bf16[32,72,128]{2,1,0:T(8,128)(2,1)S(1)}, u32[]{:S(2)}, u32[]{:S(2)}) async-start(bf16[32,72,128]{2,1,0:T(8,128)(2,1)} %get-tuple-element.8), calls=%async_computation.1 | async-start | bytes 1179648 | tf_op jit(solution)/shard_map/all_to_all | solution.py:32
  52.2 2.1 %copy-start = (bf16[1,1,5120,384]{3,2,1,0:T(8,128)(2,1)S(1)}, bf16[1,1,5120,384]{3,2,1,0:T(8,128)(2,1)}, u32[]{:S(2)}) copy-start(bf16[1,1,5120,384]{3,2,1,0:T(8,128)(2,1)} %param.18) | copy-start | bytes 11796484
  54.3 39.2 %copy-start.1 = (bf16[128,1280]{1,0:T(8,128)(2,1)S(1)}, bf16[128,1280]{1,0:T(8,128)(2,1)}, u32[]{:S(2)}) copy-start(bf16[128,1280]{1,0:T(8,128)(2,1)} %hidden_ref.3) | copy-start | bytes 983044
  63.1 52.0 %copy-start.2 = (bf16[1280,64]{0,1:T(8,128)(2,1)S(1)}, bf16[1280,64]{0,1:T(8,128)(2,1)}, u32[]{:S(2)}) copy-start(bf16[1280,64]{0,1:T(8,128)(2,1)} %param.12) | copy-start | bytes 491524
  111.0 14.9 %all-to-all-start.5 = ((bf16[32,8,384]{2,1,0:T(8,128)(2,1)}), bf16[32,8,384]{2,1,0:T(8,128)(2,1)S(1)}, u32[]{:S(2)}, u32[]{:S(2)}) async-start(bf16[32,8,384]{2,1,0:T(8,128)(2,1)} %get-tuple-element.13), calls=%async_computation.5 | async-start | bytes 393216 | tf_op jit(solution)/shard_map/all_to_all | solution.py:32

commit v8 on v7

--- a/solution.py
+++ b/solution.py
@@ -333,7 +333,6 @@
     level_ref,
     first_ref,
     noise_ref,
-    order_ref,
     second_ref,
     kept_ref,
     pair,
@@ -342,7 +341,7 @@
     f32 = jnp.float32
     level = level_ref[0]
     peers, used, lanes = first_ref.shape
-    lat_dim = noise_ref.shape[0]
+    lat_dim = used - 8
     mod_width = 40
     parts = [first_ref[peer].astype(f32) for peer in range(peers)]
     total = sum(parts[1:], parts[0])
@@ -368,8 +367,11 @@
     extra[4:6, :] = head - head_high
     extra[6:7, :] = jnp.concatenate([tail_high, tail - tail_high], axis=1)
     extra[7:8, :] = jnp.zeros((1, lanes), f32)
-    extra[0:2, :] = order_ref[...]
-    noisy = ((1.0 - level) * latent + level * noise_ref[...]).astype(jnp.bfloat16)
+    order = noise_ref[lat_dim : lat_dim + 1, :]
+    coarse = jnp.floor(order * (1.0 / 64.0))
+    extra[0:1, :] = coarse
+    extra[1:2, :] = order - 64.0 * coarse
+    noisy = ((1.0 - level) * latent + level * noise_ref[:lat_dim, :]).astype(jnp.bfloat16)
     kept_ref[lat_dim : 2 * lat_dim, :] = latent - noisy.astype(f32)
     rows = jnp.concatenate([noisy, extra[...].astype(jnp.bfloat16)], axis=0)
     for peer in range(second_ref.shape[0]):
@@ -507,11 +509,17 @@
         [((seq_count, lat_dim + 8, local_rows), bf16), ((2 * lat_dim + 8, local_rows), f32)],
         level,
         first,
-        noise.T.astype(f32),
-        jnp.stack([token_order // 64, token_order % 64]).astype(f32),
+        jnp.concatenate(
+            [
+                noise.T.astype(f32),
+                token_order.astype(f32)[None],
+                jnp.zeros((7, local_rows), f32),
+            ]
+        ),
         scalars=1,
         scratch=[pltpu.VMEM((8, 2 * local_rows), f32), pltpu.VMEM((8, local_rows), f32)],
     )
+    readout, kept = lax.optimization_barrier((readout_weight[0, 0], kept))
     second = exchange(second, "seq")
     scores = run_pass(
         mp_index.astype(jnp.int32)[None],
@@ -519,7 +527,7 @@
         embed_weight[0].astype(f32),
         qkv_weight[0, 0],
         jnp.concatenate(
-            [readout_weight[0, 0].T.astype(f32), rotation_tables(qkv_weight.shape[3] // 3)]
+            [readout.T.astype(f32), rotation_tables(qkv_weight.shape[3] // 3)]
         ),
     )
 

time: 127 us -> 127 us (level)
  other arithmetic: 3.05 us -> 1.56 us
  waiting for transfers between devices: 34.1 us -> 35.5 us
    all_to_all x3, waiting for transfers between devices: 34.1 us -> 35.5 us  [exchange(): return lax.all_to_all(chunks, axes, 0, 0, tiled=True)]
  transfers between devices with their start and end apart: 3 -> 3, of which waited for: 3 -> 3; matrix products, arithmetic and copies ran while one was open for 2% -> 1% of each run, Pallas kernels for 1% -> 1%
where the time goes in v8:
time: 127 us; the launch traced here: 126 us
  blocking collectives  45.6 us (36%)
  waiting for transfers between devices  35.5 us (28%)
  starting transfers between devices  24.3 us (19%)
  Pallas kernels  15.4 us (12%)
  local copies, waits for them, and re-layouts  2.21 us (2%)
  other arithmetic  1.56 us (1%)
  between operations  1.46 us (1%)
    all_to_all x3, blocking collectives, exchange(): return lax.all_to_all(chunks, axes, 0, 0, tiled=True)  45.6 us
    all_to_all x3, waiting for transfers between devices, exchange(): return lax.all_to_all(chunks, axes, 0, 0, tiled=True)  35.5 us
    all_to_all x3, starting transfers between devices, exchange(): return lax.all_to_all(chunks, axes, 0, 0, tiled=True)  24.3 us
    pallas_call x1, Pallas kernels, run_pass(): pl.pallas_call(pass_kernel, out_shape=jax.ShapeDtypeStruct((blocks, lanes...  8.85 us
    pallas_call x7, Pallas kernels, call(): pl.pallas_call(kernel, out_shape=[jax.ShapeDtypeStruct(*output) for outpu...  6.52 us
  transfers between devices with their start and end apart: 3, of which 3 were waited for; matrix products, arithmetic and copies ran while one was open for 1% of the time, Pallas kernels for 1%

profile of v8, /device:TPU:8, one launch (start us, length us, event | category | flops | bytes accessed | tf_op | source)
XLA Modules:
  0.0 126.0 jit_solution(11879173555021476683)
XLA Ops:
  1.4 2.2 %shard_map.122 = bf16[4,72,128]{2,1,0:T(8,128)(2,1)} custom-call(f32[1]{0:T(128)S(6)} %convert_element_type.24.time_ref, bf16[128,1280]{1,0:T(8,128)(2,1)} %hidden_ref.3, bf16[64,1280]{1,0:T(8,128)(2,1)} %bitcast.20, f32[80,256]{1,0:T(8,128)} %bitcast.23, f32[16,128]{1,0:T(8,128)} %constant.14.clone.table_in), custom_call_target="tpu_custom_call" | custom-call | tf_op jit(solution)/shard_map/pallas_call | solution.py:269
  3.6 10.3 %all-to-all-start = ((bf16[4,72,128]{2,1,0:T(8,128)(2,1)}), bf16[4,72,128]{2,1,0:T(8,128)(2,1)S(1)}, u32[]{:S(2)}, u32[]{:S(2)}) async-start(bf16[4,72,128]{2,1,0:T(8,128)(2,1)} %shard_map.122), calls=%async_computation | async-start | bytes 147456 | tf_op jit(solution)/shard_map/all_to_all | solution.py:32
  13.9 0.7 convert_bitcast_fusion.2
  14.5 0.7 convert_bitcast_fusion.1
  15.3 0.1 pad.4.clone
  15.3 0.1 maximum_maximum_fusion.noise_ref
  15.4 7.3 %all-to-all-done.first_ref = bf16[4,72,128]{2,1,0:T(8,128)(2,1)S(1)} async-done(((bf16[4,72,128]{2,1,0:T(8,128)(2,1)}), bf16[4,72,128]{2,1,0:T(8,128)(2,1)S(1)}, u32[]{:S(2)}, u32[]{:S(2)}) %all-to-all-start) | async-done | bytes 73760 | tf_op jit(solution)/shard_map/all_to_all | solution.py:32
  22.7 1.1 shard_map.123
  23.7 9.8 %all-to-all-start.1 = ((bf16[32,72,128]{2,1,0:T(8,128)(2,1)}), bf16[32,72,128]{2,1,0:T(8,128)(2,1)S(1)}, u32[]{:S(2)}, u32[]{:S(2)}) async-start(bf16[32,72,128]{2,1,0:T(8,128)(2,1)} %get-tuple-element.10), calls=%async_computation.1 | async-start | bytes 1179648 | tf_op jit(solution)/shard_map/all_to_all | solution.py:32
  33.6 0.1 bitcast_convert_fusion.embed_ref
  33.7 0.0 copy-done.5
  33.7 18.6 %all-to-all-done.1.gathered_ref = bf16[32,72,128]{2,1,0:T(8,128)(2,1)S(1)} async-done(((bf16[32,72,128]{2,1,0:T(8,128)(2,1)}), bf16[32,72,128]{2,1,0:T(8,128)(2,1)S(1)}, u32[]{:S(2)}, u32[]{:S(2)}) %all-to-all-start.1) | async-done | bytes 589856 | tf_op jit(solution)/shard_map/all_to_all | solution.py:32
  52.3 2.1 %copy-done = bf16[1,1,5120,384]{3,2,1,0:T(8,128)(2,1)S(1)} copy-done((bf16[1,1,5120,384]{3,2,1,0:T(8,128)(2,1)S(1)}, bf16[1,1,5120,384]{3,2,1,0:T(8,128)(2,1)}, u32[]{:S(2)}) %copy-start) | copy-done | bytes 3932184
  54.4 8.8 %shard_map.124 = bf16[32,16,128]{2,1,0:T(8,128)(2,1)S(1)} custom-call(s32[1]{0:T(128)} %bitcast.place_ref, bf16[32,72,128]{2,1,0:T(8,128)(2,1)S(1)} %all-to-all-done.1.gathered_ref, f32[64,5120]{1,0:T(8,128)S(1)} %bitcast_convert_fusion.embed_ref, bf16[5120,384]{1,0:T(8,128)(2,1)S(1)} %bitcast.19, f32[192,128]{1,0:T(8,128)S(1)} %pad_maximum_fusion.small_ref), custom_call_target="tpu_custom_call" | custom-call | tf_op jit(solution)/shard_map/pallas_call | solution.py:240
  63.3 0.0 copy-start.2
  63.3 14.5 %all_to_all.30.scores_ref = bf16[32,16,128]{2,1,0:T(8,128)(2,1)S(1)} all-to-all(bf16[32,16,128]{2,1,0:T(8,128)(2,1)S(1)} %shard_map.124), channel_id=1, replica_groups=mesh['role'=4,'seq'=32,'mp'=4] {'seq'}, dimensions={0} | all-to-all | bytes 262144 | tf_op jit(solution)/shard_map/all_to_all | solution.py:32
  77.8 15.0 %all_to_all.31.score_ref = f32[16,16,128]{2,1,0:T(8,128)S(1)} all-to-all(f32[16,16,128]{2,1,0:T(8,128)S(1)} %shard_map.125), channel_id=1, replica_groups=mesh['role'=4,'seq'=32,'mp'=4] {'role','mp'}, dimensions={0} | all-to-all | bytes 262144 | tf_op jit(solution)/shard_map/all_to_all | solution.py:32
  92.8 0.5 shard_map.126
  93.3 16.2 %all_to_all.32.third_ref = bf16[32,8,384]{2,1,0:T(8,128)(2,1)S(1)} all-to-all(bf16[32,8,384]{2,1,0:T(8,128)(2,1)S(1)} %get-tuple-element.14), channel_id=1, replica_groups=mesh['role'=4,'seq'=32,'mp'=4] {'seq'}, dimensions={0} | all-to-all | bytes 393216 | tf_op jit(solution)/shard_map/all_to_all | solution.py:32
  109.4 0.8 shard_map.127
  110.3 4.2 %all-to-all-start.5 = ((bf16[32,8,384]{2,1,0:T(8,128)(2,1)}), bf16[32,8,384]{2,1,0:T(8,128)(2,1)S(1)}, u32[]{:S(2)}, u32[]{:S(2)}) async-start(bf16[32,8,384]{2,1,0:T(8,128)(2,1)} %get-tuple-element.17), calls=%async_computation.5 | async-start | bytes 393216 | tf_op jit(solution)/shard_map/all_to_all | solution.py:32
  114.5 1.0 shard_map.128
  115.5 9.7 %all-to-all-done.5.fourth_ref = bf16[32,8,384]{2,1,0:T(8,128)(2,1)S(1)} async-done(((bf16[32,8,384]{2,1,0:T(8,128)(2,1)}), bf16[32,8,384]{2,1,0:T(8,128)(2,1)S(1)}, u32[]{:S(2)}, u32[]{:S(2)}) %all-to-all-start.5) | async-done | bytes 196640 | tf_op jit(solution)/shard_map/all_to_all | solution.py:32
  125.2 0.8 shard_map.129
  (13 shorter events, 0.1 us)
Async XLA Ops:
  0.6 33.0 %copy-start.3 = (bf16[1,64,5120]{2,1,0:T(8,128)(2,1)S(1)}, bf16[1,64,5120]{2,1,0:T(8,128)(2,1)}, u32[]{:S(2)}) copy-start(bf16[1,64,5120]{2,1,0:T(8,128)(2,1)} %param.17) | copy-start | bytes 1966084
  3.6 19.1 %all-to-all-start = ((bf16[4,72,128]{2,1,0:T(8,128)(2,1)}), bf16[4,72,128]{2,1,0:T(8,128)(2,1)S(1)}, u32[]{:S(2)}, u32[]{:S(2)}) async-start(bf16[4,72,128]{2,1,0:T(8,128)(2,1)} %shard_map.122), calls=%async_computation | async-start | bytes 147456 | tf_op jit(solution)/shard_map/all_to_all | solution.py:32
  23.7 10.0 %copy-start.5 = (bf16[1,1,128,64]{2,3,1,0:T(8,128)(2,1)S(1)}, bf16[1,1,128,64]{2,3,1,0:T(8,128)(2,1)}, u32[]{:S(2)}) copy-start(bf16[1,1,128,64]{2,3,1,0:T(8,128)(2,1)} %param.19) | copy-start | bytes 49156
  23.7 10.0 %copy-start.4 = (f32[128,128]{1,0:T(8,128)S(1)}, f32[128,128]{1,0:T(8,128)}, u32[]{:S(2)}) copy-start(f32[128,128]{1,0:T(8,128)} %constant.15.clone) | copy-start | bytes 196612
  23.7 28.6 %all-to-all-start.1 = ((bf16[32,72,128]{2,1,0:T(8,128)(2,1)}), bf16[32,72,128]{2,1,0:T(8,128)(2,1)S(1)}, u32[]{:S(2)}, u32[]{:S(2)}) async-start(bf16[32,72,128]{2,1,0:T(8,128)(2,1)} %get-tuple-element.10), calls=%async_computation.1 | async-start | bytes 1179648 | tf_op jit(solution)/shard_map/all_to_all | solution.py:32
  52.3 2.1 %copy-start = (bf16[1,1,5120,384]{3,2,1,0:T(8,128)(2,1)S(1)}, bf16[1,1,5120,384]{3,2,1,0:T(8,128)(2,1)}, u32[]{:S(2)}) copy-start(bf16[1,1,5120,384]{3,2,1,0:T(8,128)(2,1)} %param.18) | copy-start | bytes 11796484
  54.4 38.4 %copy-start.1 = (bf16[128,1280]{1,0:T(8,128)(2,1)S(1)}, bf16[128,1280]{1,0:T(8,128)(2,1)}, u32[]{:S(2)}) copy-start(bf16[128,1280]{1,0:T(8,128)(2,1)} %hidden_ref.3) | copy-start | bytes 983044
  63.3 51.2 %copy-start.2 = (bf16[1280,64]{0,1:T(8,128)(2,1)S(1)}, bf16[1280,64]{0,1:T(8,128)(2,1)}, u32[]{:S(2)}) copy-start(bf16[1280,64]{0,1:T(8,128)(2,1)} %param.12) | copy-start | bytes 491524
  110.3 14.9 %all-to-all-start.5 = ((bf16[32,8,384]{2,1,0:T(8,128)(2,1)}), bf16[32,8,384]{2,1,0:T(8,128)(2,1)S(1)}, u32[]{:S(2)}, u32[]{:S(2)}) async-start(bf16[32,8,384]{2,1,0:T(8,128)(2,1)} %get-tuple-element.17), calls=%async_computation.5 | async-start | bytes 393216 | tf_op jit(solution)/shard_map/all_to_all | solution.py:32

commit v9 on v7

--- a/solution.py
+++ b/solution.py
@@ -284,11 +284,13 @@
     out_in,
     weight_in,
     table_in,
+    order_in,
     first_ref,
     hidden_ref,
     out_ref,
     weight_ref,
     table_ref,
+    order_ref,
     arrived,
 ):
     fetches = fetch_all(
@@ -297,6 +299,7 @@
         (weight_in, weight_ref),
         (hidden_in, hidden_ref),
         (out_in, out_ref),
+        (order_in, order_ref),
     )
     lanes = hidden_ref.shape[0]
     lat_dim = out_ref.shape[0]
@@ -324,6 +327,9 @@
     values = jnp.where(row < 2, squares, jnp.where(row < 4, modulation, 0.0))
     high = values.astype(jnp.bfloat16).astype(jnp.float32)
     extra = jnp.where(row % 2 == 0, high, values - high)
+    order = order_ref[...].astype(jnp.float32)
+    coarse = jnp.floor(order * (1.0 / 64.0))
+    extra = jnp.where(row == 4, coarse, jnp.where(row == 5, order - 64.0 * coarse, extra))
     rows = jnp.concatenate([partial, extra], axis=0).astype(jnp.bfloat16)
     for peer in range(first_ref.shape[0]):
         first_ref[peer] = rows
@@ -333,7 +339,6 @@
     level_ref,
     first_ref,
     noise_ref,
-    order_ref,
     second_ref,
     kept_ref,
     pair,
@@ -342,7 +347,7 @@
     f32 = jnp.float32
     level = level_ref[0]
     peers, used, lanes = first_ref.shape
-    lat_dim = noise_ref.shape[0]
+    lat_dim = used - 8
     mod_width = 40
     parts = [first_ref[peer].astype(f32) for peer in range(peers)]
     total = sum(parts[1:], parts[0])
@@ -368,7 +373,7 @@
     extra[4:6, :] = head - head_high
     extra[6:7, :] = jnp.concatenate([tail_high, tail - tail_high], axis=1)
     extra[7:8, :] = jnp.zeros((1, lanes), f32)
-    extra[0:2, :] = order_ref[...]
+    extra[0:2, :] = parts[0][lat_dim + 4 : lat_dim + 6]
     noisy = ((1.0 - level) * latent + level * noise_ref[...]).astype(jnp.bfloat16)
     kept_ref[lat_dim : 2 * lat_dim, :] = latent - noisy.astype(f32)
     rows = jnp.concatenate([noisy, extra[...].astype(jnp.bfloat16)], axis=0)
@@ -497,8 +502,9 @@
         out_turned,
         time_turned,
         jnp.asarray(np.repeat(in_parts(turns), 8, axis=0)),
+        token_order[None],
         scalars=1,
-        fetched=4,
+        fetched=5,
     )
     first = exchange(first, "mp")
 
@@ -508,10 +514,10 @@
         level,
         first,
         noise.T.astype(f32),
-        jnp.stack([token_order // 64, token_order % 64]).astype(f32),
         scalars=1,
         scratch=[pltpu.VMEM((8, 2 * local_rows), f32), pltpu.VMEM((8, local_rows), f32)],
     )
+    readout, kept = lax.optimization_barrier((readout_weight[0, 0], kept))
     second = exchange(second, "seq")
     scores = run_pass(
         mp_index.astype(jnp.int32)[None],
@@ -519,7 +525,7 @@
         embed_weight[0].astype(f32),
         qkv_weight[0, 0],
         jnp.concatenate(
-            [readout_weight[0, 0].T.astype(f32), rotation_tables(qkv_weight.shape[3] // 3)]
+            [readout.T.astype(f32), rotation_tables(qkv_weight.shape[3] // 3)]
         ),
     )
 

time: 127 us -> 127 us (level)
  other arithmetic: 3.05 us -> 0.82 us
  waiting for transfers between devices: 34.1 us -> 36.3 us
    all_to_all x3, waiting for transfers between devices: 34.1 us -> 36.3 us  [exchange(): return lax.all_to_all(chunks, axes, 0, 0, tiled=True)]
  transfers between devices with their start and end apart: 3 -> 3, of which waited for: 3 -> 3; matrix products, arithmetic and copies ran while one was open for 2% -> 1% of each run, Pallas kernels for 1% -> 1%
where the time goes in v9:
time: 127 us; the launch traced here: 126 us
  blocking collectives  45.6 us (36%)
  waiting for transfers between devices  36.3 us (29%)
  starting transfers between devices  24.3 us (19%)
  Pallas kernels  15.4 us (12%)
  local copies, waits for them, and re-layouts  2.13 us (2%)
  between operations  1.46 us (1%)
    all_to_all x3, blocking collectives, exchange(): return lax.all_to_all(chunks, axes, 0, 0, tiled=True)  45.6 us
    all_to_all x3, waiting for transfers between devices, exchange(): return lax.all_to_all(chunks, axes, 0, 0, tiled=True)  36.3 us
    all_to_all x3, starting transfers between devices, exchange(): return lax.all_to_all(chunks, axes, 0, 0, tiled=True)  24.3 us
    pallas_call x1, Pallas kernels, run_pass(): pl.pallas_call(pass_kernel, out_shape=jax.ShapeDtypeStruct((blocks, lanes...  8.84 us
    pallas_call x7, Pallas kernels, call(): pl.pallas_call(kernel, out_shape=[jax.ShapeDtypeStruct(*output) for outpu...  6.52 us
  transfers between devices with their start and end apart: 3, of which 3 were waited for; matrix products, arithmetic and copies ran while one was open for 1% of the time, Pallas kernels for 1%

profile of v9, /device:TPU:8, one launch (start us, length us, event | category | flops | bytes accessed | tf_op | source)
XLA Modules:
  0.0 126.0 jit_solution(10338395866788370334)
XLA Ops:
  0.6 0.0 copy-start.3
  1.4 2.2 %shard_map.122 = bf16[4,72,128]{2,1,0:T(8,128)(2,1)} custom-call(f32[1]{0:T(128)S(6)} %convert_element_type.20.time_ref, bf16[128,1280]{1,0:T(8,128)(2,1)} %hidden_ref.3, bf16[64,1280]{1,0:T(8,128)(2,1)} %bitcast.19, f32[80,256]{1,0:T(8,128)} %bitcast.22, f32[16,128]{1,0:T(8,128)} %constant.12.clone.table_in, s32[1,128]{1,0:T(1,128)} %bitcast.24), custom_call_target="tpu_custom_call" | custom-call | tf_op jit(solution)/shard_map/pallas_call | solution.py:269
  3.6 10.3 %all-to-all-start = ((bf16[4,72,128]{2,1,0:T(8,128)(2,1)}), bf16[4,72,128]{2,1,0:T(8,128)(2,1)S(1)}, u32[]{:S(2)}, u32[]{:S(2)}) async-start(bf16[4,72,128]{2,1,0:T(8,128)(2,1)} %shard_map.122), calls=%async_computation | async-start | bytes 147456 | tf_op jit(solution)/shard_map/all_to_all | solution.py:32
  13.9 0.7 convert_bitcast_fusion.1.noise_ref
  14.6 8.1 %all-to-all-done.first_ref = bf16[4,72,128]{2,1,0:T(8,128)(2,1)S(1)} async-done(((bf16[4,72,128]{2,1,0:T(8,128)(2,1)}), bf16[4,72,128]{2,1,0:T(8,128)(2,1)S(1)}, u32[]{:S(2)}, u32[]{:S(2)}) %all-to-all-start) | async-done | bytes 73760 | tf_op jit(solution)/shard_map/all_to_all | solution.py:32
  22.7 1.1 shard_map.123
  23.7 9.8 %all-to-all-start.1 = ((bf16[32,72,128]{2,1,0:T(8,128)(2,1)}), bf16[32,72,128]{2,1,0:T(8,128)(2,1)S(1)}, u32[]{:S(2)}, u32[]{:S(2)}) async-start(bf16[32,72,128]{2,1,0:T(8,128)(2,1)} %get-tuple-element.10), calls=%async_computation.1 | async-start | bytes 1179648 | tf_op jit(solution)/shard_map/all_to_all | solution.py:32
  33.6 0.0 copy-done.3
  33.6 0.1 bitcast_convert_fusion.embed_ref
  33.7 0.0 copy-done.5
  33.7 18.6 %all-to-all-done.1.gathered_ref = bf16[32,72,128]{2,1,0:T(8,128)(2,1)S(1)} async-done(((bf16[32,72,128]{2,1,0:T(8,128)(2,1)}), bf16[32,72,128]{2,1,0:T(8,128)(2,1)S(1)}, u32[]{:S(2)}, u32[]{:S(2)}) %all-to-all-start.1) | async-done | bytes 589856 | tf_op jit(solution)/shard_map/all_to_all | solution.py:32
  52.3 2.1 %copy-done = bf16[1,1,5120,384]{3,2,1,0:T(8,128)(2,1)S(1)} copy-done((bf16[1,1,5120,384]{3,2,1,0:T(8,128)(2,1)S(1)}, bf16[1,1,5120,384]{3,2,1,0:T(8,128)(2,1)}, u32[]{:S(2)}) %copy-start) | copy-done | bytes 3932184
  54.4 8.8 %shard_map.124 = bf16[32,16,128]{2,1,0:T(8,128)(2,1)S(1)} custom-call(s32[1]{0:T(128)} %bitcast.place_ref, bf16[32,72,128]{2,1,0:T(8,128)(2,1)S(1)} %all-to-all-done.1.gathered_ref, f32[64,5120]{1,0:T(8,128)S(1)} %bitcast_convert_fusion.embed_ref, bf16[5120,384]{1,0:T(8,128)(2,1)S(1)} %bitcast.18, f32[192,128]{1,0:T(8,128)S(1)} %pad_maximum_fusion.small_ref), custom_call_target="tpu_custom_call" | custom-call | tf_op jit(solution)/shard_map/pallas_call | solution.py:240
  63.3 0.0 copy-start.2
  63.3 14.5 %all_to_all.30.scores_ref = bf16[32,16,128]{2,1,0:T(8,128)(2,1)S(1)} all-to-all(bf16[32,16,128]{2,1,0:T(8,128)(2,1)S(1)} %shard_map.124), channel_id=1, replica_groups=mesh['role'=4,'seq'=32,'mp'=4] {'seq'}, dimensions={0} | all-to-all | bytes 262144 | tf_op jit(solution)/shard_map/all_to_all | solution.py:32
  77.8 15.0 %all_to_all.31.score_ref = f32[16,16,128]{2,1,0:T(8,128)S(1)} all-to-all(f32[16,16,128]{2,1,0:T(8,128)S(1)} %shard_map.125), channel_id=1, replica_groups=mesh['role'=4,'seq'=32,'mp'=4] {'role','mp'}, dimensions={0} | all-to-all | bytes 262144 | tf_op jit(solution)/shard_map/all_to_all | solution.py:32
  92.8 0.5 shard_map.126
  93.3 16.2 %all_to_all.32.third_ref = bf16[32,8,384]{2,1,0:T(8,128)(2,1)S(1)} all-to-all(bf16[32,8,384]{2,1,0:T(8,128)(2,1)S(1)} %get-tuple-element.14), channel_id=1, replica_groups=mesh['role'=4,'seq'=32,'mp'=4] {'seq'}, dimensions={0} | all-to-all | bytes 393216 | tf_op jit(solution)/shard_map/all_to_all | solution.py:32
  109.5 0.8 shard_map.127
  110.3 4.1 %all-to-all-start.5 = ((bf16[32,8,384]{2,1,0:T(8,128)(2,1)}), bf16[32,8,384]{2,1,0:T(8,128)(2,1)S(1)}, u32[]{:S(2)}, u32[]{:S(2)}) async-start(bf16[32,8,384]{2,1,0:T(8,128)(2,1)} %get-tuple-element.17), calls=%async_computation.5 | async-start | bytes 393216 | tf_op jit(solution)/shard_map/all_to_all | solution.py:32
  114.5 0.0 copy-done.2
  114.5 1.0 shard_map.128
  115.5 9.7 %all-to-all-done.5.fourth_ref = bf16[32,8,384]{2,1,0:T(8,128)(2,1)S(1)} async-done(((bf16[32,8,384]{2,1,0:T(8,128)(2,1)}), bf16[32,8,384]{2,1,0:T(8,128)(2,1)S(1)}, u32[]{:S(2)}, u32[]{:S(2)}) %all-to-all-start.5) | async-done | bytes 196640 | tf_op jit(solution)/shard_map/all_to_all | solution.py:32
  125.2 0.8 shard_map.129
  (9 shorter events, 0.1 us)
Async XLA Ops:
  0.6 33.0 %copy-start.3 = (bf16[1,64,5120]{2,1,0:T(8,128)(2,1)S(1)}, bf16[1,64,5120]{2,1,0:T(8,128)(2,1)}, u32[]{:S(2)}) copy-start(bf16[1,64,5120]{2,1,0:T(8,128)(2,1)} %param.17) | copy-start | bytes 1966084
  3.6 19.1 %all-to-all-start = ((bf16[4,72,128]{2,1,0:T(8,128)(2,1)}), bf16[4,72,128]{2,1,0:T(8,128)(2,1)S(1)}, u32[]{:S(2)}, u32[]{:S(2)}) async-start(bf16[4,72,128]{2,1,0:T(8,128)(2,1)} %shard_map.122), calls=%async_computation | async-start | bytes 147456 | tf_op jit(solution)/shard_map/all_to_all | solution.py:32
  23.7 10.0 %copy-start.5 = (bf16[1,1,128,64]{2,3,1,0:T(8,128)(2,1)S(1)}, bf16[1,1,128,64]{2,3,1,0:T(8,128)(2,1)}, u32[]{:S(2)}) copy-start(bf16[1,1,128,64]{2,3,1,0:T(8,128)(2,1)} %param.19) | copy-start | bytes 49156
  23.7 10.0 %copy-start.4 = (f32[128,128]{1,0:T(8,128)S(1)}, f32[128,128]{1,0:T(8,128)}, u32[]{:S(2)}) copy-start(f32[128,128]{1,0:T(8,128)} %constant.13.clone) | copy-start | bytes 196612
  23.7 28.6 %all-to-all-start.1 = ((bf16[32,72,128]{2,1,0:T(8,128)(2,1)}), bf16[32,72,128]{2,1,0:T(8,128)(2,1)S(1)}, u32[]{:S(2)}, u32[]{:S(2)}) async-start(bf16[32,72,128]{2,1,0:T(8,128)(2,1)} %get-tuple-element.10), calls=%async_computation.1 | async-start | bytes 1179648 | tf_op jit(solution)/shard_map/all_to_all | solution.py:32
  52.3 2.1 %copy-start = (bf16[1,1,5120,384]{3,2,1,0:T(8,128)(2,1)S(1)}, bf16[1,1,5120,384]{3,2,1,0:T(8,128)(2,1)}, u32[]{:S(2)}) copy-start(bf16[1,1,5120,384]{3,2,1,0:T(8,128)(2,1)} %param.18) | copy-start | bytes 11796484
  54.4 38.4 %copy-start.1 = (bf16[128,1280]{1,0:T(8,128)(2,1)S(1)}, bf16[128,1280]{1,0:T(8,128)(2,1)}, u32[]{:S(2)}) copy-start(bf16[128,1280]{1,0:T(8,128)(2,1)} %hidden_ref.3) | copy-start | bytes 983044
  63.3 51.2 %copy-start.2 = (bf16[1280,64]{0,1:T(8,128)(2,1)S(1)}, bf16[1280,64]{0,1:T(8,128)(2,1)}, u32[]{:S(2)}) copy-start(bf16[1280,64]{0,1:T(8,128)(2,1)} %param.12) | copy-start | bytes 491524
  110.3 14.9 %all-to-all-start.5 = ((bf16[32,8,384]{2,1,0:T(8,128)(2,1)}), bf16[32,8,384]{2,1,0:T(8,128)(2,1)S(1)}, u32[]{:S(2)}, u32[]{:S(2)}) async-start(bf16[32,8,384]{2,1,0:T(8,128)(2,1)} %get-tuple-element.17), calls=%async_computation.5 | async-start | bytes 393216 | tf_op jit(solution)/shard_map/all_to_all | solution.py:32
